TPU v7x, 32 devices: a whole 2x2x4 slice. The times are simulated.
32 devices in a mesh: view: 2 (over core), tm: 16 (over z, y, x).
Axes of the slice: x: 2, y: 2, z: 4, core: 2. Of those that a mesh axis runs over, the one named last changes fastest.
Arguments:
- frames_x: bfloat16 [2, 16, 384, 1152], P('view', 'tm'), may hold values from -6 to 6
- box_embed: bfloat16 [2, 16, 16, 1152], P('view', 'tm'), may hold values from -6 to 6
- box_count: int32 [2, 16], P('view', 'tm'), may hold values from 1 to 16
- frame_valid: int32 [2, 16], P('view', 'tm'), may hold values 0 or 1
- cycle_link: int32 [2, 2], P('view'), may hold values 0 or 1
- w_qkv: bfloat16 [1152, 3456], P('tm'), may hold values from -0.47140452 to 0.47140452
- w_out: bfloat16 [1152, 1152], P('tm'), may hold values from -0.1875 to 0.1875
- box_gate: float32 [288], replicated, may hold values from -2 to 2
Outputs:
- mixed: bfloat16 [2, 16, 384, 1152], P('view', 'tm')
All inputs are finite; a program needn't handle non-finite values. No bound on the sum of `frame_valid` or of `cycle_link` on one device may be relied on, other than what follows from the above.
Results may differ from a plain program's by a relative error of at most 0.0045.
The roundings to bfloat16 on the way count: a program that leaves them out, or rounds other values in their place, can miss the bound.
Values may be sent and summed in bfloat16 or wider, within the bound.
No kernel may reach another device: no remote copies, remote signals or barrier semaphores. Data moves between devices by JAX's collectives and lax.ppermute only.
A program may use at most 128 MiB of HBM per device.

v0:
```python
import functools

import jax
import jax.numpy as jnp
from jax import lax
from jax.experimental import pallas as pl
from jax.experimental.pallas import tpu as pltpu
from jax.sharding import PartitionSpec as P

HD = 72
CROSS_HEADS = 8
TIME_HEADS = 4
BOX_HEADS = 4
DEAD = -1e30
VMEM_BYTES = 50 * 2**20
F32 = jnp.float32
BF16 = jnp.bfloat16


def swap(value, axis, by):
    size = lax.axis_size(axis)
    return lax.ppermute(value, axis, [(i, i ^ by) for i in range(size)])


def gather_blocks(shard, first, second):
    size = lax.axis_size("tm")
    near = jnp.concatenate([shard] + [swap(shard, "tm", d) for d in range(4, size, 4)], axis=0)
    one = swap(near, "tm", first)
    two = swap(jnp.concatenate([near, one], axis=0), "tm", second)
    rows = near.shape[0]
    if first == 1:
        return jnp.concatenate([near, one, two], axis=0)
    return jnp.concatenate([near, two[:rows], one, two[rows:]], axis=0)


def block_order(size):
    far = list(range(0, size, 4))
    return [f ^ low for low in range(4) for f in far]


def dot(a, b):
    return jnp.dot(a, b, preferred_element_type=F32)


def dot_t(a, b):
    return lax.dot_general(a, b, (((1,), (1,)), ((), ())), preferred_element_type=F32)


def chooser(rows, source, offset=0):
    row_ids = lax.broadcasted_iota(jnp.int32, (rows, source.shape[1]), 0)
    return (row_ids + offset == source).astype(F32).astype(BF16)


def attend_heads(query, keys, values, score_edits, weight_edits, acc_ref):
    width = query.shape[1]
    scale = HD ** (-0.5)
    for head in range(width // HD):
        low, high = head * HD, (head + 1) * HD
        left = low // 128 * 128
        right = min(width, -(-high // 128) * 128)
        lane = lax.broadcasted_iota(jnp.int32, (1, right - left), 1) + left
        mine = (lane >= low) & (lane < high)
        q = jnp.where(mine, query[:, left:right].astype(F32), 0.0).astype(BF16)
        scores = [edit(dot_t(q, k[:, left:right]) * scale) for k, edit in zip(keys, score_edits)]
        top = functools.reduce(
            jnp.maximum, [jnp.max(s, axis=-1, keepdims=True) for s in scores]
        )
        expos = [edit(jnp.exp(s - top)) for s, edit in zip(scores, weight_edits)]
        total = sum(jnp.sum(e, axis=-1, keepdims=True) for e in expos)
        out = sum(dot(e.astype(BF16), v[:, left:right]) for e, v in zip(expos, values))
        out = out / total
        acc_ref[:, left:right] = jnp.where(mine, out, acc_ref[:, left:right])


def same(x):
    return x


def order_kernel(tokens_ref, *refs, others):
    other_refs = refs[:others]
    source_ref, wide_source_ref, out_ref, wide_ref = refs[others : others + 4]
    out_refs = refs[others + 4 :]
    depth = tokens_ref.shape[1]
    pick = chooser(depth, source_ref[...])
    out_ref[...] = dot(tokens_ref[...], pick).astype(BF16)
    for a, b in zip(other_refs, out_refs):
        b[...] = dot(a[...], pick).astype(BF16)
    wide_ref[...] = dot(tokens_ref[...], chooser(depth, wide_source_ref[...])).astype(BF16)


def time_kernel(tokens_ref, source_ref, mine_ref, theirs_ref, out_ref, acc_ref, *, positions):
    rows, depth = tokens_ref.shape
    part = out_ref.shape[1] // 2
    tokens = dot(tokens_ref[...], chooser(depth, source_ref[...])).astype(BF16)
    place = lax.rem(lax.broadcasted_iota(jnp.int32, (rows, 1), 0), positions)
    place_t = lax.rem(lax.broadcasted_iota(jnp.int32, (1, rows), 1), positions)
    live = place == place_t
    for half, ref in enumerate((mine_ref, theirs_ref)):
        qkv = dot(tokens, ref[...]).astype(BF16)
        attend_heads(
            qkv[:, :part],
            [qkv[:, part : 2 * part]],
            [qkv[:, 2 * part : 3 * part]],
            [lambda s: jnp.where(live, s, DEAD)],
            [same],
            acc_ref,
        )
        out_ref[:, half * part : (half + 1) * part] = acc_ref[...].astype(BF16)


def box_kernel(
    tokens_ref, wide_ref, source_ref, gate_ref, first_mine, first_theirs, mine_ref, theirs_ref,
    out_ref, acc_ref, box_ref, *, slots, blocks,
):
    rows, depth = tokens_ref.shape
    part = out_ref.shape[1] // 2
    fold = mine_ref.shape[1]
    folds = depth // fold
    block = mine_ref.shape[0] // blocks
    lane = lax.broadcasted_iota(jnp.int32, (1, blocks * slots), 1)
    live = jnp.zeros((1, blocks * slots), F32)
    repeats = -(-blocks * slots // fold)
    for b in range(blocks):
        for j in range(folds):
            box_ref[b * slots : (b + 1) * slots, j * fold : (j + 1) * fold] = mine_ref[
                b * block + j * slots : b * block + (j + 1) * slots, :
            ]
        at = b * block + folds * slots
        flags = mine_ref[at : at + 16, :].astype(F32)[:1]
        flags = jnp.concatenate([flags] * repeats, axis=1)[:, : blocks * slots]
        live = jnp.where(lane // slots == b, flags, live)
    box = dot(box_ref[...], chooser(depth, source_ref[...])).astype(BF16)
    box_wide_source = None
    del box_wide_source
    tokens = tokens_ref[...]
    wide = wide_ref[...]
    cut = 3 * part - fold
    for half, (early, late) in enumerate(((first_mine, mine_ref), (first_theirs, theirs_ref))):
        weights = late[...]
        kvq = dot(wide, weights).astype(BF16)
        q_low = dot(tokens, early[...][:, -cut:]).astype(BF16)
        query = jnp.concatenate([q_low, kvq[:, 2 * part :]], axis=1)
        box_kv = dot(box, weights[:, : 2 * part]).astype(BF16)
        attend_heads(
            query,
            [kvq[:, :part], box_kv[:, :part]],
            [kvq[:, part : 2 * part], box_kv[:, part : 2 * part]],
            [same, lambda s: jnp.where(live > 0, s, DEAD)],
            [same, same],
            acc_ref,
        )
        out_ref[:, half * part : (half + 1) * part] = (
            acc_ref[...] * jnp.tanh(gate_ref[half : half + 1, :])
        ).astype(BF16)


def cross_kernel(count_ref, tokens_ref, *refs, others):
    other_refs = refs[:others]
    mine_ref, theirs_ref, out_ref, acc_ref = refs[others:]
    part = out_ref.shape[1] // 2
    counts = [count_ref[0, j] for j in range(others)]
    score_edits = [same] + [
        lambda s, c=c: jnp.where(jnp.full((1, 1), c, F32) > 0, s, DEAD) for c in counts
    ]
    weight_edits = [same] + [lambda e, c=c: e * c for c in counts]
    for half, ref in enumerate((mine_ref, theirs_ref)):
        weights = ref[...]
        own = dot(tokens_ref[...], weights).astype(BF16)
        kv = [own[:, part:]] + [dot(o[...], weights[:, part:]).astype(BF16) for o in other_refs]
        attend_heads(
            own[:, :part],
            [x[:, :part] for x in kv],
            [x[:, part:] for x in kv],
            score_edits,
            weight_edits,
            acc_ref,
        )
        out_ref[:, half * part : (half + 1) * part] = acc_ref[...].astype(BF16)


def collect_kernel(half_ref, source_ref, cross_ref, time_ref, box_ref, out_ref):
    which = half_ref[0]
    total = None
    base = 0
    for ref in (cross_ref, time_ref, box_ref):
        part = ref.shape[1] // 2
        for half in range(2):
            side = which if half == 0 else 1 - which
            pick = chooser(part, source_ref[...], base + side * part)
            term = dot(ref[:, half * part : (half + 1) * part], pick)
            total = term if total is None else total + term
        base += 2 * part
    out_ref[...] = total.astype(BF16)


def final_kernel(half_ref, tokens_ref, attn_ref, mine_ref, theirs_ref, out_ref):
    width = mine_ref.shape[1]
    step = out_ref.shape[1] - width
    for half, ref in enumerate((mine_ref, theirs_ref)):
        side = half_ref[0] if half == 0 else 1 - half_ref[0]
        at = pl.ds(pl.multiple_of(side * step, 128), width)
        out_ref[:, at] = (tokens_ref[:, at].astype(F32) + dot(attn_ref[...], ref[...])).astype(
            BF16
        )


def call(kernel, outs, *args, scalars=0, scratch=(), name=None):
    vmem = pl.BlockSpec(memory_space=pltpu.VMEM)
    smem = pl.BlockSpec(memory_space=pltpu.SMEM)
    single = not isinstance(outs, list)
    result = pl.pallas_call(
        kernel,
        out_shape=outs if single else tuple(outs),
        in_specs=[smem] * scalars + [vmem] * (len(args) - scalars),
        out_specs=vmem if single else tuple(vmem for _ in outs),
        scratch_shapes=list(scratch),
        compiler_params=pltpu.CompilerParams(vmem_limit_bytes=VMEM_BYTES),
        name=name,
    )(*args)
    return result


def shaped(*dims):
    return jax.ShapeDtypeStruct(dims, BF16)


def per_device(frames_x, box_embed, box_count, frame_valid, cycle_link, w_qkv, w_out, box_gate):
    size = lax.axis_size("tm")
    cameras = lax.axis_size("view")
    depth = frames_x.shape[3]
    tokens = frames_x.reshape(-1, depth)
    count = tokens.shape[0]
    slots = box_embed.shape[2]
    boxes = box_embed.reshape(slots, depth)
    rows = w_qkv.shape[0]
    index = lax.axis_index("tm")
    half = lax.axis_index("view") % 2
    cw, tw, bw = (heads * HD // 2 for heads in (CROSS_HEADS, TIME_HEADS, BOX_HEADS))
    fold = depth // 3
    cut = 3 * bw - fold

    def pieces(side):
        def part(kind, base, width):
            at = kind * depth + base + side * width
            return w_qkv[:, at : at + width]

        cross = [part(kind, 0, cw) for kind in range(3)]
        timed = [part(kind, 2 * cw, tw) for kind in range(3)]
        q, k, v = [part(kind, 2 * cw + 2 * tw, bw) for kind in range(3)]
        out_width = -(-(depth // 2) // 128) * 128
        out_at = side * (depth - out_width)
        return (
            jnp.concatenate(timed + [q[:, :cut]], axis=1),
            jnp.concatenate([k, v, q[:, cut:]], axis=1),
            jnp.concatenate(cross, axis=1),
            w_out[:, out_at : out_at + out_width],
        )

    first, second, third, fourth = (
        jnp.where(half == 0, a, b) for a, b in zip(pieces(0), pieces(1))
    )
    live = (jnp.arange(slots, dtype=jnp.int32) < box_count[0, 0]) & (frame_valid[0, 0] == 1)
    flag_rows = jnp.broadcast_to(jnp.tile(live.astype(BF16), fold // slots)[None], (8, fold))
    box_rows = [boxes[:, j * fold : (j + 1) * fold] for j in range(3)]
    used = 3 * slots + 8 + rows
    block = -(-used // 16) * 16
    second = jnp.concatenate(
        box_rows + [flag_rows, second, jnp.zeros((block - used, fold), BF16)], axis=0
    )

    if cameras == 2:
        others = [swap(tokens, "view", 1)]
        link_counts = (cycle_link[:, :1] + cycle_link[:, 1:]).astype(F32)
    else:
        ring = range(cameras)
        others = [
            lax.ppermute(tokens, "view", [(i, (i + by) % cameras) for i in ring]) for by in (1, -1)
        ]
        link_counts = cycle_link.astype(F32)
    positions = count // size
    token_slices = lax.all_to_all(
        tokens.reshape(size, positions, depth), "tm", split_axis=0, concat_axis=0, tiled=True
    ).reshape(count, depth)

    gathered = []
    for number, piece in enumerate((first, second, third, fourth)):
        mine = gather_blocks(piece, *((1, 2) if number % 2 == 0 else (2, 1)))
        gathered.append((mine, swap(mine, "view", 1)))

    owners = index ^ jnp.array(block_order(size), jnp.int32)
    source = (owners[:, None] * rows + jnp.arange(rows)[None]).reshape(1, -1)
    wide_source = jnp.full((size, block), -1, jnp.int32)
    wide_source = wide_source.at[:, 3 * slots + 8 : used].set(source.reshape(size, rows))
    wide_source = wide_source.reshape(1, -1)

    ordered, wide, *ordered_others = call(
        functools.partial(order_kernel, others=len(others)),
        [shaped(count, depth), shaped(count, size * block)] + [shaped(count, depth) for _ in others],
        tokens, *others, source, wide_source,
        name="order",
    )
    timed = call(
        functools.partial(time_kernel, positions=positions),
        shaped(count, 2 * tw),
        token_slices, source, gathered[0][0][:, : 3 * tw], gathered[0][1][:, : 3 * tw],
        scratch=[pltpu.VMEM((count, tw), F32)],
        name="timed",
    )
    timed = lax.all_to_all(
        timed.reshape(size, positions, 2 * tw), "tm", split_axis=0, concat_axis=0, tiled=True
    ).reshape(count, 2 * tw)
    gates = box_gate.reshape(2, bw)
    gates = jnp.where(half == 0, gates, gates[::-1])
    boxed = call(
        functools.partial(box_kernel, slots=slots, blocks=size),
        shaped(count, 2 * bw),
        ordered, wide, wide_source, gates, *gathered[0], *gathered[1],
        scratch=[pltpu.VMEM((count, bw), F32), pltpu.VMEM((size * slots, depth), BF16)],
        name="boxed",
    )
    cross = call(
        functools.partial(cross_kernel, others=len(others)),
        shaped(count, 2 * cw),
        link_counts, ordered, *ordered_others, *gathered[2],
        scalars=1,
        scratch=[pltpu.VMEM((count, cw), F32)],
        name="cross",
    )
    which = half.reshape(1).astype(jnp.int32)
    attn = call(
        collect_kernel, shaped(count, depth), which, source, cross, timed, boxed,
        scalars=1, name="collect",
    )
    result = call(
        final_kernel, shaped(count, depth), which, tokens, attn, *gathered[3],
        scalars=1, name="final",
    )
    return result.reshape(frames_x.shape)


def solution(mesh):
    in_specs = (
        P("view", "tm", None, None),
        P("view", "tm", None, None),
        P("view", "tm"),
        P("view", "tm"),
        P("view", None),
        P("tm", None),
        P("tm", None),
        P(),
    )
    out_specs = P("view", "tm", None, None)
    return jax.shard_map(
        per_device, mesh=mesh, in_specs=in_specs, out_specs=out_specs, check_vma=False
    )
```

profile of v0, /device:TPU:0, one launch (start us, length us, event | category | flops | bytes accessed | tf_op | source)
XLA Modules:
  0.0 173.1 jit_solution(4499293259933180829)
XLA Ops:
  2.0 3.0 %collective-permute-start.1 = (bf16[72,864]{1,0:T(8,128)(2,1)S(1)}, bf16[72,864]{1,0:T(8,128)(2,1)S(1)}, u32[]{:S(2)}, u32[]{:S(2)}) collective-permute-start(bf16[72,864]{1,0:T(8,128)(2,1)S(1)} %get-tuple-element.30), channel_id=1, source_target_pairs={{0,4},{1,5},{2,6},{3,7},{4,0},{5,1},{6,2},{7,3},{8,12},{9,13},{10,... | collective-permute-start | bytes 373256 | tf_op jit(solution)/shard_map/ppermute | solution.py:22
  5.0 2.6 %collective-permute-start.2 = (bf16[72,864]{1,0:T(8,128)(2,1)S(1)}, bf16[72,864]{1,0:T(8,128)(2,1)S(1)}, u32[]{:S(2)}, u32[]{:S(2)}) collective-permute-start(bf16[72,864]{1,0:T(8,128)(2,1)S(1)} %get-tuple-element.30), channel_id=1, source_target_pairs={{0,8},{1,9},{2,10},{3,11},{4,12},{5,13},{6,14},{7,15},{8,0},{9,1},... | collective-permute-start | bytes 373256 | tf_op jit(solution)/shard_map/ppermute | solution.py:22
  10.4 3.5 %collective-permute-start.8 = (bf16[72,480]{1,0:T(8,128)(2,1)S(1)}, bf16[72,480]{1,0:T(8,128)(2,1)S(1)}, u32[]{:S(2)}, u32[]{:S(2)}) collective-permute-start(bf16[72,480]{1,0:T(8,128)(2,1)S(1)} %get-tuple-element.28), channel_id=1, source_target_pairs={{0,8},{1,9},{2,10},{3,11},{4,12},{5,13},{6,14},{7,15},{8,0},{9,1},... | collective-permute-start | bytes 207368 | tf_op jit(solution)/shard_map/ppermute | solution.py:22
  23.3 5.1 %collective-permute-done.9 = bf16[72,480]{1,0:T(8,128)(2,1)S(1)} collective-permute-done((bf16[72,480]{1,0:T(8,128)(2,1)S(1)}, bf16[72,480]{1,0:T(8,128)(2,1)S(1)}, u32[]{:S(2)}, u32[]{:S(2)}) %collective-permute-start.9) | collective-permute-done | bytes 69152 | tf_op jit(solution)/shard_map/ppermute | solution.py:22
  31.8 2.4 %collective-permute-done.20 = bf16[72,640]{1,0:T(8,128)(2,1)S(1)} collective-permute-done((bf16[72,640]{1,0:T(8,128)(2,1)S(1)}, bf16[72,640]{1,0:T(8,128)(2,1)S(1)}, u32[]{:S(2)}, u32[]{:S(2)}) %collective-permute-start.20) | collective-permute-done | bytes 92192 | tf_op jit(solution)/shard_map/ppermute | solution.py:22
  34.2 2.1 %collective-permute-done.21 = bf16[72,640]{1,0:T(8,128)(2,1)S(1)} collective-permute-done((bf16[72,640]{1,0:T(8,128)(2,1)S(1)}, bf16[72,640]{1,0:T(8,128)(2,1)S(1)}, u32[]{:S(2)}, u32[]{:S(2)}) %collective-permute-start.21) | collective-permute-done | bytes 92192 | tf_op jit(solution)/shard_map/ppermute | solution.py:22
  36.2 2.2 %collective-permute-start.14 = (bf16[128,384]{1,0:T(8,128)(2,1)S(1)}, bf16[128,384]{1,0:T(8,128)(2,1)S(1)}, u32[]{:S(2)}, u32[]{:S(2)}) collective-permute-start(bf16[128,384]{1,0:T(8,128)(2,1)S(1)} %get-tuple-element.84), channel_id=1, source_target_pairs={{0,8},{1,9},{2,10},{3,11},{4,12},{5,13},{6,14},{7,15},{8,0},{9,1},... | collective-permute-start | bytes 294920 | tf_op jit(solution)/shard_map/ppermute | solution.py:22
  41.6 2.0 %collective-permute-done.14 = bf16[128,384]{1,0:T(8,128)(2,1)S(1)} collective-permute-done((bf16[128,384]{1,0:T(8,128)(2,1)S(1)}, bf16[128,384]{1,0:T(8,128)(2,1)S(1)}, u32[]{:S(2)}, u32[]{:S(2)}) %collective-permute-start.14) | collective-permute-done | bytes 98336 | tf_op jit(solution)/shard_map/ppermute | solution.py:22
  43.5 1.8 %collective-permute-start.10 = (bf16[288,480]{1,0:T(8,128)(2,1)S(1)}, bf16[288,480]{1,0:T(8,128)(2,1)S(1)}, u32[]{:S(2)}, u32[]{:S(2)}) collective-permute-start(bf16[288,480]{1,0:T(8,128)(2,1)S(1)} %pad_maximum_fusion.2), channel_id=1, source_target_pairs={{0,1},{1,0},{2,3},{3,2},{4,5},{5,4},{6,7},{7,6},{8,9},{9,8},{10,11... | collective-permute-start | bytes 829448 | tf_op jit(solution)/shard_map/ppermute | solution.py:22
  46.3 1.9 %collective-permute-start.22 = (bf16[288,640]{1,0:T(8,128)(2,1)S(1)}, bf16[288,640]{1,0:T(8,128)(2,1)S(1)}, u32[]{:S(2)}, u32[]{:S(2)}) collective-permute-start(bf16[288,640]{1,0:T(8,128)(2,1)S(1)} %pad_maximum_fusion.1), channel_id=1, source_target_pairs={{0,2},{1,3},{2,0},{3,1},{4,6},{5,7},{6,4},{7,5},{8,10},{9,11},{10,... | collective-permute-start | bytes 1105928 | tf_op jit(solution)/shard_map/ppermute | solution.py:22
  49.0 1.9 %collective-permute-start.4 = (bf16[288,864]{1,0:T(8,128)(2,1)S(1)}, bf16[288,864]{1,0:T(8,128)(2,1)S(1)}, u32[]{:S(2)}, u32[]{:S(2)}) collective-permute-start(bf16[288,864]{1,0:T(8,128)(2,1)S(1)} %pad_maximum_fusion), channel_id=1, source_target_pairs={{0,1},{1,0},{2,3},{3,2},{4,5},{5,4},{6,7},{7,6},{8,9},{9,8},{10,11... | collective-permute-start | bytes 1493000 | tf_op jit(solution)/shard_map/ppermute | solution.py:22
  53.2 1.9 %collective-permute-start.11 = (bf16[576,480]{1,0:T(8,128)(2,1)}, bf16[576,480]{1,0:T(8,128)(2,1)}, u32[]{:S(2)}, u32[]{:S(2)}) collective-permute-start(bf16[576,480]{1,0:T(8,128)(2,1)} %get-tuple-element.53), channel_id=1, source_target_pairs={{0,2},{1,3},{2,0},{3,1},{4,6},{5,7},{6,4},{7,5},{8,10},{9,11},{10,... | collective-permute-start | bytes 1658888 | tf_op jit(solution)/shard_map/ppermute | solution.py:22
  55.1 2.7 %collective-permute-done.22 = bf16[288,640]{1,0:T(8,128)(2,1)S(1)} collective-permute-done((bf16[288,640]{1,0:T(8,128)(2,1)S(1)}, bf16[288,640]{1,0:T(8,128)(2,1)S(1)}, u32[]{:S(2)}, u32[]{:S(2)}) %collective-permute-start.22) | collective-permute-done | bytes 368672 | tf_op jit(solution)/shard_map/ppermute | solution.py:22
  58.6 1.9 %collective-permute-start.23 = (bf16[576,640]{1,0:T(8,128)(2,1)}, bf16[576,640]{1,0:T(8,128)(2,1)}, u32[]{:S(2)}, u32[]{:S(2)}) collective-permute-start(bf16[576,640]{1,0:T(8,128)(2,1)} %constant_dynamic-update-slice_fusion.53), channel_id=1, source_target_pairs={{0,1},{1,0},{2,3},{3,2},{4,5},{5,4},{6,7},{7,6},{8,9},{9,8},{10,11... | collective-permute-start | bytes 2211848 | tf_op jit(solution)/shard_map/ppermute | solution.py:22
  61.2 5.0 %collective-permute-done.16 = bf16[512,384]{1,0:T(8,128)(2,1)S(1)} collective-permute-done((bf16[512,384]{1,0:T(8,128)(2,1)S(1)}, bf16[512,384]{1,0:T(8,128)(2,1)S(1)}, u32[]{:S(2)}, u32[]{:S(2)}) %collective-permute-start.16) | collective-permute-done | bytes 393248 | tf_op jit(solution)/shard_map/ppermute | solution.py:22
  67.0 1.9 %collective-permute-start.17 = (bf16[1024,384]{1,0:T(8,128)(2,1)}, bf16[1024,384]{1,0:T(8,128)(2,1)}, u32[]{:S(2)}, u32[]{:S(2)}) collective-permute-start(bf16[1024,384]{1,0:T(8,128)(2,1)} %constant_dynamic-update-slice_fusion.35), channel_id=1, source_target_pairs={{0,1},{1,0},{2,3},{3,2},{4,5},{5,4},{6,7},{7,6},{8,9},{9,8},{10,11... | collective-permute-start | bytes 2359304 | tf_op jit(solution)/shard_map/ppermute | solution.py:22
  71.4 3.6 %all-to-all-start = ((bf16[16,24,1152]{2,1,0:T(8,128)(2,1)}), bf16[16,24,1152]{2,1,0:T(8,128)(2,1)S(1)}, u32[]{:S(2)}, u32[]{:S(2)}) async-start(bf16[16,24,1152]{2,1,0:T(8,128)(2,1)} %bitcast.3), calls=%async_computation | async-start | bytes 1769472 | tf_op jit(solution)/shard_map/all_to_all | solution.py:281
  75.1 8.6 %collective-permute-done.11 = bf16[576,480]{1,0:T(8,128)(2,1)} collective-permute-done((bf16[576,480]{1,0:T(8,128)(2,1)}, bf16[576,480]{1,0:T(8,128)(2,1)}, u32[]{:S(2)}, u32[]{:S(2)}) %collective-permute-start.11) | collective-permute-done | bytes 552992 | tf_op jit(solution)/shard_map/ppermute | solution.py:22
  88.7 13.6 %collective-permute-done.17 = bf16[1024,384]{1,0:T(8,128)(2,1)} collective-permute-done((bf16[1024,384]{1,0:T(8,128)(2,1)}, bf16[1024,384]{1,0:T(8,128)(2,1)}, u32[]{:S(2)}, u32[]{:S(2)}) %collective-permute-start.17) | collective-permute-done | bytes 786464 | tf_op jit(solution)/shard_map/ppermute | solution.py:22
  102.4 1.8 %slice_dynamic-update-slice_fusion.1 = bf16[2048,384]{1,0:T(8,128)(2,1)} fusion(bf16[2048,384]{1,0:T(8,128)(2,1)} %get-tuple-element.62, bf16[1024,384]{1,0:T(8,128)(2,1)} %collective-permute-done.17), kind=kLoop, calls=%fused_computation.2 | loop fusion | bytes 786432
  105.9 2.3 %constant_dynamic-update-slice_fusion.5.refs_1_ = bf16[1152,864]{1,0:T(8,128)(2,1)} fusion(bf16[1152,864]{1,0:T(8,128)(2,1)} %get-tuple-element.32, bf16[576,864]{1,0:T(8,128)(2,1)} %collective-permute-done.5), kind=kLoop, calls=%fused_computation.12 | loop fusion | bytes 2064384 | tf_op jit(solution)/shard_map/concatenate | solution.py:32
  108.2 4.1 %copy.10 = bf16[1152,864]{0,1:T(8,128)(2,1)} copy(bf16[1152,864]{1,0:T(8,128)(2,1)} %constant_dynamic-update-slice_fusion.5.refs_1_) | data formatting | bytes 3981312 | tf_op jit(solution)/shard_map/concatenate | solution.py:32
  113.1 1.8 %slice_dynamic-update-slice_fusion.mine_ref = bf16[2048,384]{1,0:T(8,128)(2,1)} fusion(bf16[2048,384]{1,0:T(8,128)(2,1)} %constant_dynamic-update-slice_fusion.44, bf16[1024,384]{1,0:T(8,128)(2,1)} %collective-permute-done.17), kind=kLoop, calls=%fused_computation.1 | loop fusion | bytes 786432 | tf_op jit(solution)/shard_map/concatenate | solution.py:33
  115.4 1.8 %slice_dynamic-update-slice_fusion.2.mine_ref = bf16[1152,640]{1,0:T(8,128)(2,1)} fusion(bf16[1152,640]{1,0:T(8,128)(2,1)} %constant_dynamic-update-slice_fusion.58, bf16[576,640]{1,0:T(8,128)(2,1)} %collective-permute-done.23), kind=kLoop, calls=%fused_computation.3 | loop fusion | bytes 737280 | tf_op jit(solution)/shard_map/concatenate | solution.py:33
  119.5 5.5 %timed.1 = bf16[384,288]{1,0:T(8,128)(2,1)} custom-call(bf16[384,1152]{1,0:T(8,128)(2,1)S(1)} %bitcast.16, s32[1,1152]{1,0:T(1,128)S(1)} %add.38.refs_1_.source_ref, bf16[1152,432]{1,0:T(8,128)(2,1)S(1)} %bitcast.14, bf16[1152,432]{1,0:T(8,128)(2,1)S(1)} %bitcast.15), custom_call_target="tpu_custom_call" | custom-call | tf_op jit(solution)/shard_map/timed/pallas_call | solution.py:211
  125.0 5.6 %all-to-all-start.1 = ((bf16[16,24,288]{2,1,0:T(8,128)(2,1)}), bf16[16,24,288]{2,1,0:T(8,128)(2,1)}, u32[]{:S(2)}, u32[]{:S(2)}) async-start(bf16[16,24,288]{2,1,0:T(8,128)(2,1)} %bitcast.5), calls=%async_computation.1 | async-start | bytes 589824 | tf_op jit(solution)/shard_map/all_to_all | solution.py:309
  132.7 7.6 %order.1 = (bf16[384,1152]{1,0:T(8,128)(2,1)S(1)}, bf16[384,2048]{1,0:T(8,128)(2,1)}, bf16[384,1152]{1,0:T(8,128)(2,1)S(1)}) custom-call(bf16[384,1152]{1,0:T(8,128)(2,1)} %bitcast.1.tokens_ref, bf16[384,1152]{1,0:T(8,128)(2,1)} %collective-permute-done.refs_0_, s32[1,1152]{1,0:T(1,128)S(1)} %add.38.refs_1_.source_ref, s32[1,2048]{1,0:T(1,128)S(1)} %bitcast.17), custom_call_target="tpu_custom_call" | custom-call | tf_op jit(solution)/shard_map/order/pallas_call | solution.py:211
  140.3 10.1 %boxed.1.box_ref = bf16[384,288]{1,0:T(8,128)(2,1)S(1)} custom-call(bf16[384,1152]{1,0:T(8,128)(2,1)S(1)} %get-tuple-element.20.tokens_ref, bf16[384,2048]{1,0:T(8,128)(2,1)} %get-tuple-element.22.wide_ref, s32[1,2048]{1,0:T(1,128)S(1)} %bitcast.18, f32[2,144]{1,0:T(2,128)S(1)} %broadcast_select_fusion.gate_ref, ...), custom_call_target="tpu_custom_call" | custom-call | tf_op jit(solution)/shard_map/boxed/pallas_call | solution.py:211
  150.4 4.2 %copy.11.refs_2_ = bf16[1152,864]{1,0:T(8,128)(2,1)} copy(bf16[1152,864]{0,1:T(8,128)(2,1)} %collective-permute-done.6) | data formatting | bytes 3981312 | tf_op jit(solution)/shard_map/ppermute | solution.py:22
  154.6 10.6 %cross.1.cross_ref = bf16[384,576]{1,0:T(8,128)(2,1)S(1)} custom-call(f32[1,1]{1,0:T(1,128)S(6)} %convert_element_type.10.count_ref, bf16[384,1152]{1,0:T(8,128)(2,1)S(1)} %get-tuple-element.20.tokens_ref, bf16[384,1152]{1,0:T(8,128)(2,1)S(1)} %copy-done.1, bf16[1152,864]{1,0:T(8,128)(2,1)} %constant_dynamic-update-slice_fusion.5.refs_1_, ...), custom_call_target="tpu_custom_call" | custom-call | tf_op jit(solution)/shard_map/cross/pallas_call | solution.py:211
  165.3 3.2 %collect.1.attn_ref = bf16[384,1152]{1,0:T(8,128)(2,1)S(1)} custom-call(s32[1]{0:T(128)} %bitcast.half_ref, s32[1,1152]{1,0:T(1,128)S(1)} %add.38.refs_1_.source_ref, bf16[384,576]{1,0:T(8,128)(2,1)S(1)} %cross.1.cross_ref, bf16[384,288]{1,0:T(8,128)(2,1)} %bitcast.6.time_ref, bf16[384,288]{1,0:T(8,128)(2,1)S(1)} %boxed.1.box_ref), custom_call_target="tpu_custom_call" | custom-call | tf_op jit(solution)/shard_map/collect/pallas_call | solution.py:211
  168.4 4.7 %final.1 = bf16[384,1152]{1,0:T(8,128)(2,1)} custom-call(s32[1]{0:T(128)} %bitcast.half_ref, bf16[384,1152]{1,0:T(8,128)(2,1)} %bitcast.1.tokens_ref, bf16[384,1152]{1,0:T(8,128)(2,1)S(1)} %collect.1.attn_ref, bf16[1152,640]{1,0:T(8,128)(2,1)} %slice_dynamic-update-slice_fusion.2.mine_ref, bf16[1152,640]{1,0:T(8,128)(2,1)} %collective-permute-done.24.theirs_ref), custom_call_target="tpu_custom_call" | custom-call | tf_op jit(solution)/shard_map/final/pallas_call | solution.py:211
  (105 shorter events, 39.5 us)
Async XLA Ops:
  0.0 14.6 %copy-start.3 = (bf16[1,1,16,1152]{3,2,1,0:T(8,128)(2,1)S(1)}, bf16[1,1,16,1152]{3,2,1,0:T(8,128)(2,1)}, u32[]{:S(2)}) copy-start(bf16[1,1,16,1152]{3,2,1,0:T(8,128)(2,1)} %param.12) | copy-start | bytes 110596
  0.0 19.1 %copy-start.4 = (bf16[72,1152]{1,0:T(8,128)(2,1)S(1)}, bf16[72,1152]{1,0:T(8,128)(2,1)}, u32[]{:S(2)}) copy-start(bf16[72,1152]{1,0:T(8,128)(2,1)} %param.17) | copy-start | bytes 497668
  2.0 46.9 %collective-permute-start.1 = (bf16[72,864]{1,0:T(8,128)(2,1)S(1)}, bf16[72,864]{1,0:T(8,128)(2,1)S(1)}, u32[]{:S(2)}, u32[]{:S(2)}) collective-permute-start(bf16[72,864]{1,0:T(8,128)(2,1)S(1)} %get-tuple-element.30), channel_id=1, source_target_pairs={{0,4},{1,5},{2,6},{3,7},{4,0},{5,1},{6,2},{7,3},{8,12},{9,13},{10,... | collective-permute-start | bytes 373256 | tf_op jit(solution)/shard_map/ppermute | solution.py:22
  5.0 44.0 %collective-permute-start.2 = (bf16[72,864]{1,0:T(8,128)(2,1)S(1)}, bf16[72,864]{1,0:T(8,128)(2,1)S(1)}, u32[]{:S(2)}, u32[]{:S(2)}) collective-permute-start(bf16[72,864]{1,0:T(8,128)(2,1)S(1)} %get-tuple-element.30), channel_id=1, source_target_pairs={{0,8},{1,9},{2,10},{3,11},{4,12},{5,13},{6,14},{7,15},{8,0},{9,1},... | collective-permute-start | bytes 373256 | tf_op jit(solution)/shard_map/ppermute | solution.py:22
  7.6 41.4 %collective-permute-start.3 = (bf16[72,864]{1,0:T(8,128)(2,1)S(1)}, bf16[72,864]{1,0:T(8,128)(2,1)S(1)}, u32[]{:S(2)}, u32[]{:S(2)}) collective-permute-start(bf16[72,864]{1,0:T(8,128)(2,1)S(1)} %get-tuple-element.30), channel_id=1, source_target_pairs={{0,12},{1,13},{2,14},{3,15},{4,8},{5,9},{6,10},{7,11},{8,4},{9,5},... | collective-permute-start | bytes 373256 | tf_op jit(solution)/shard_map/ppermute | solution.py:22
  9.5 12.3 %collective-permute-start.7 = (bf16[72,480]{1,0:T(8,128)(2,1)S(1)}, bf16[72,480]{1,0:T(8,128)(2,1)S(1)}, u32[]{:S(2)}, u32[]{:S(2)}) collective-permute-start(bf16[72,480]{1,0:T(8,128)(2,1)S(1)} %get-tuple-element.28), channel_id=1, source_target_pairs={{0,4},{1,5},{2,6},{3,7},{4,0},{5,1},{6,2},{7,3},{8,12},{9,13},{10,... | collective-permute-start | bytes 207368 | tf_op jit(solution)/shard_map/ppermute | solution.py:22
  10.4 12.1 %collective-permute-start.8 = (bf16[72,480]{1,0:T(8,128)(2,1)S(1)}, bf16[72,480]{1,0:T(8,128)(2,1)S(1)}, u32[]{:S(2)}, u32[]{:S(2)}) collective-permute-start(bf16[72,480]{1,0:T(8,128)(2,1)S(1)} %get-tuple-element.28), channel_id=1, source_target_pairs={{0,8},{1,9},{2,10},{3,11},{4,12},{5,13},{6,14},{7,15},{8,0},{9,1},... | collective-permute-start | bytes 207368 | tf_op jit(solution)/shard_map/ppermute | solution.py:22
  21.8 6.7 %collective-permute-start.9 = (bf16[72,480]{1,0:T(8,128)(2,1)S(1)}, bf16[72,480]{1,0:T(8,128)(2,1)S(1)}, u32[]{:S(2)}, u32[]{:S(2)}) collective-permute-start(bf16[72,480]{1,0:T(8,128)(2,1)S(1)} %get-tuple-element.28), channel_id=1, source_target_pairs={{0,12},{1,13},{2,14},{3,15},{4,8},{5,9},{6,10},{7,11},{8,4},{9,5},... | collective-permute-start | bytes 207368 | tf_op jit(solution)/shard_map/ppermute | solution.py:22
  22.5 7.3 %collective-permute-start.19 = (bf16[72,640]{1,0:T(8,128)(2,1)S(1)}, bf16[72,640]{1,0:T(8,128)(2,1)S(1)}, u32[]{:S(2)}, u32[]{:S(2)}) collective-permute-start(bf16[72,640]{1,0:T(8,128)(2,1)S(1)} %get-tuple-element.24), channel_id=1, source_target_pairs={{0,4},{1,5},{2,6},{3,7},{4,0},{5,1},{6,2},{7,3},{8,12},{9,13},{10,... | collective-permute-start | bytes 276488 | tf_op jit(solution)/shard_map/ppermute | solution.py:22
  28.5 5.7 %collective-permute-start.20 = (bf16[72,640]{1,0:T(8,128)(2,1)S(1)}, bf16[72,640]{1,0:T(8,128)(2,1)S(1)}, u32[]{:S(2)}, u32[]{:S(2)}) collective-permute-start(bf16[72,640]{1,0:T(8,128)(2,1)S(1)} %get-tuple-element.24), channel_id=1, source_target_pairs={{0,8},{1,9},{2,10},{3,11},{4,12},{5,13},{6,14},{7,15},{8,0},{9,1},... | collective-permute-start | bytes 276488 | tf_op jit(solution)/shard_map/ppermute | solution.py:22
  29.8 6.4 %collective-permute-start.21 = (bf16[72,640]{1,0:T(8,128)(2,1)S(1)}, bf16[72,640]{1,0:T(8,128)(2,1)S(1)}, u32[]{:S(2)}, u32[]{:S(2)}) collective-permute-start(bf16[72,640]{1,0:T(8,128)(2,1)S(1)} %get-tuple-element.24), channel_id=1, source_target_pairs={{0,12},{1,13},{2,14},{3,15},{4,8},{5,9},{6,10},{7,11},{8,4},{9,5},... | collective-permute-start | bytes 276488 | tf_op jit(solution)/shard_map/ppermute | solution.py:22
  34.2 5.7 %collective-permute-start.13 = (bf16[128,384]{1,0:T(8,128)(2,1)S(1)}, bf16[128,384]{1,0:T(8,128)(2,1)S(1)}, u32[]{:S(2)}, u32[]{:S(2)}) collective-permute-start(bf16[128,384]{1,0:T(8,128)(2,1)S(1)} %get-tuple-element.84), channel_id=1, source_target_pairs={{0,4},{1,5},{2,6},{3,7},{4,0},{5,1},{6,2},{7,3},{8,12},{9,13},{10,... | collective-permute-start | bytes 294920 | tf_op jit(solution)/shard_map/ppermute | solution.py:22
  36.2 7.3 %collective-permute-start.14 = (bf16[128,384]{1,0:T(8,128)(2,1)S(1)}, bf16[128,384]{1,0:T(8,128)(2,1)S(1)}, u32[]{:S(2)}, u32[]{:S(2)}) collective-permute-start(bf16[128,384]{1,0:T(8,128)(2,1)S(1)} %get-tuple-element.84), channel_id=1, source_target_pairs={{0,8},{1,9},{2,10},{3,11},{4,12},{5,13},{6,14},{7,15},{8,0},{9,1},... | collective-permute-start | bytes 294920 | tf_op jit(solution)/shard_map/ppermute | solution.py:22
  39.8 6.4 %collective-permute-start.15 = (bf16[128,384]{1,0:T(8,128)(2,1)S(1)}, bf16[128,384]{1,0:T(8,128)(2,1)S(1)}, u32[]{:S(2)}, u32[]{:S(2)}) collective-permute-start(bf16[128,384]{1,0:T(8,128)(2,1)S(1)} %get-tuple-element.84), channel_id=1, source_target_pairs={{0,12},{1,13},{2,14},{3,15},{4,8},{5,9},{6,10},{7,11},{8,4},{9,5},... | collective-permute-start | bytes 294920 | tf_op jit(solution)/shard_map/ppermute | solution.py:22
  43.5 8.9 %collective-permute-start.10 = (bf16[288,480]{1,0:T(8,128)(2,1)S(1)}, bf16[288,480]{1,0:T(8,128)(2,1)S(1)}, u32[]{:S(2)}, u32[]{:S(2)}) collective-permute-start(bf16[288,480]{1,0:T(8,128)(2,1)S(1)} %pad_maximum_fusion.2), channel_id=1, source_target_pairs={{0,1},{1,0},{2,3},{3,2},{4,5},{5,4},{6,7},{7,6},{8,9},{9,8},{10,11... | collective-permute-start | bytes 829448 | tf_op jit(solution)/shard_map/ppermute | solution.py:22
  46.3 11.5 %collective-permute-start.22 = (bf16[288,640]{1,0:T(8,128)(2,1)S(1)}, bf16[288,640]{1,0:T(8,128)(2,1)S(1)}, u32[]{:S(2)}, u32[]{:S(2)}) collective-permute-start(bf16[288,640]{1,0:T(8,128)(2,1)S(1)} %pad_maximum_fusion.1), channel_id=1, source_target_pairs={{0,2},{1,3},{2,0},{3,1},{4,6},{5,7},{6,4},{7,5},{8,10},{9,11},{10,... | collective-permute-start | bytes 1105928 | tf_op jit(solution)/shard_map/ppermute | solution.py:22
  48.8 17.4 %collective-permute-start.16 = (bf16[512,384]{1,0:T(8,128)(2,1)S(1)}, bf16[512,384]{1,0:T(8,128)(2,1)S(1)}, u32[]{:S(2)}, u32[]{:S(2)}) collective-permute-start(bf16[512,384]{1,0:T(8,128)(2,1)S(1)} %get-tuple-element.61), channel_id=1, source_target_pairs={{0,2},{1,3},{2,0},{3,1},{4,6},{5,7},{6,4},{7,5},{8,10},{9,11},{10,... | collective-permute-start | bytes 1179656 | tf_op jit(solution)/shard_map/ppermute | solution.py:22
  49.0 19.8 %collective-permute-start.4 = (bf16[288,864]{1,0:T(8,128)(2,1)S(1)}, bf16[288,864]{1,0:T(8,128)(2,1)S(1)}, u32[]{:S(2)}, u32[]{:S(2)}) collective-permute-start(bf16[288,864]{1,0:T(8,128)(2,1)S(1)} %pad_maximum_fusion), channel_id=1, source_target_pairs={{0,1},{1,0},{2,3},{3,2},{4,5},{5,4},{6,7},{7,6},{8,9},{9,8},{10,11... | collective-permute-start | bytes 1493000 | tf_op jit(solution)/shard_map/ppermute | solution.py:22
  53.2 30.5 %collective-permute-start.11 = (bf16[576,480]{1,0:T(8,128)(2,1)}, bf16[576,480]{1,0:T(8,128)(2,1)}, u32[]{:S(2)}, u32[]{:S(2)}) collective-permute-start(bf16[576,480]{1,0:T(8,128)(2,1)} %get-tuple-element.53), channel_id=1, source_target_pairs={{0,2},{1,3},{2,0},{3,1},{4,6},{5,7},{6,4},{7,5},{8,10},{9,11},{10,... | collective-permute-start | bytes 1658888 | tf_op jit(solution)/shard_map/ppermute | solution.py:22
  58.6 27.6 %collective-permute-start.23 = (bf16[576,640]{1,0:T(8,128)(2,1)}, bf16[576,640]{1,0:T(8,128)(2,1)}, u32[]{:S(2)}, u32[]{:S(2)}) collective-permute-start(bf16[576,640]{1,0:T(8,128)(2,1)} %constant_dynamic-update-slice_fusion.53), channel_id=1, source_target_pairs={{0,1},{1,0},{2,3},{3,2},{4,5},{5,4},{6,7},{7,6},{8,9},{9,8},{10,11... | collective-permute-start | bytes 2211848 | tf_op jit(solution)/shard_map/ppermute | solution.py:22
  67.0 35.4 %collective-permute-start.17 = (bf16[1024,384]{1,0:T(8,128)(2,1)}, bf16[1024,384]{1,0:T(8,128)(2,1)}, u32[]{:S(2)}, u32[]{:S(2)}) collective-permute-start(bf16[1024,384]{1,0:T(8,128)(2,1)} %constant_dynamic-update-slice_fusion.35), channel_id=1, source_target_pairs={{0,1},{1,0},{2,3},{3,2},{4,5},{5,4},{6,7},{7,6},{8,9},{9,8},{10,11... | collective-permute-start | bytes 2359304 | tf_op jit(solution)/shard_map/ppermute | solution.py:22
  69.9 36.0 %collective-permute-start.5 = (bf16[576,864]{1,0:T(8,128)(2,1)}, bf16[576,864]{1,0:T(8,128)(2,1)}, u32[]{:S(2)}, u32[]{:S(2)}) collective-permute-start(bf16[576,864]{1,0:T(8,128)(2,1)} %get-tuple-element.31), channel_id=1, source_target_pairs={{0,2},{1,3},{2,0},{3,1},{4,6},{5,7},{6,4},{7,5},{8,10},{9,11},{10,... | collective-permute-start | bytes 2985992 | tf_op jit(solution)/shard_map/ppermute | solution.py:22
  71.4 48.0 %all-to-all-start = ((bf16[16,24,1152]{2,1,0:T(8,128)(2,1)}), bf16[16,24,1152]{2,1,0:T(8,128)(2,1)S(1)}, u32[]{:S(2)}, u32[]{:S(2)}) async-start(bf16[16,24,1152]{2,1,0:T(8,128)(2,1)} %bitcast.3), calls=%async_computation | async-start | bytes 1769472 | tf_op jit(solution)/shard_map/all_to_all | solution.py:281
  86.2 31.6 %collective-permute-start.12 = (bf16[1152,480]{0,1:T(8,128)(2,1)}, bf16[1152,480]{0,1:T(8,128)(2,1)}, u32[]{:S(2)}, u32[]{:S(2)}) collective-permute-start(bf16[1152,480]{0,1:T(8,128)(2,1)} %copy.12), channel_id=1, source_target_pairs={{0,16},{16,0},{1,17},{17,1},{2,18},{18,2},{3,19},{19,3},{4,20},{20... | collective-permute-start | bytes 3317768 | tf_op jit(solution)/shard_map/ppermute | solution.py:22
  112.3 38.1 %collective-permute-start.6 = (bf16[1152,864]{0,1:T(8,128)(2,1)}, bf16[1152,864]{0,1:T(8,128)(2,1)}, u32[]{:S(2)}, u32[]{:S(2)}) collective-permute-start(bf16[1152,864]{0,1:T(8,128)(2,1)} %copy.10), channel_id=1, source_target_pairs={{0,16},{16,0},{1,17},{17,1},{2,18},{18,2},{3,19},{19,3},{4,20},{20... | collective-permute-start | bytes 5971976 | tf_op jit(solution)/shard_map/ppermute | solution.py:22
  114.9 25.3 %collective-permute-start.18 = (bf16[2048,384]{1,0:T(8,128)(2,1)}, bf16[2048,384]{1,0:T(8,128)(2,1)}, u32[]{:S(2)}, u32[]{:S(2)}) collective-permute-start(bf16[2048,384]{1,0:T(8,128)(2,1)} %slice_dynamic-update-slice_fusion.mine_ref), channel_id=1, source_target_pairs={{0,16},{16,0},{1,17},{17,1},{2,18},{18,2},{3,19},{19,3},{4,20},{20... | collective-permute-start | bytes 4718600 | tf_op jit(solution)/shard_map/ppermute | solution.py:22
  117.2 51.2 %collective-permute-start.24 = (bf16[1152,640]{1,0:T(8,128)(2,1)}, bf16[1152,640]{1,0:T(8,128)(2,1)}, u32[]{:S(2)}, u32[]{:S(2)}) collective-permute-start(bf16[1152,640]{1,0:T(8,128)(2,1)} %slice_dynamic-update-slice_fusion.2.mine_ref), channel_id=1, source_target_pairs={{0,16},{16,0},{1,17},{17,1},{2,18},{18,2},{3,19},{19,3},{4,20},{20... | collective-permute-start | bytes 4423688 | tf_op jit(solution)/shard_map/ppermute | solution.py:22
  117.2 15.5 %collective-permute-start = (bf16[384,1152]{1,0:T(8,128)(2,1)}, bf16[384,1152]{1,0:T(8,128)(2,1)}, u32[]{:S(2)}, u32[]{:S(2)}) collective-permute-start(bf16[384,1152]{1,0:T(8,128)(2,1)} %bitcast.1.tokens_ref), channel_id=1, source_target_pairs={{0,16},{16,0},{1,17},{17,1},{2,18},{18,2},{3,19},{19,3},{4,20},{20... | collective-permute-start | bytes 2654216 | tf_op jit(solution)/shard_map/ppermute | solution.py:22
  119.5 11.1 %copy-start.6 = (s32[1,2]{1,0:T(1,128)S(1)}, s32[1,2]{1,0:T(1,128)}, u32[]{:S(2)}) copy-start(s32[1,2]{1,0:T(1,128)} %param.15) | copy-start | bytes 28
  119.5 13.0 %copy-start.5 = (f32[288]{0:T(512)S(1)}, f32[288]{0:T(512)}, u32[]{:S(2)}) copy-start(f32[288]{0:T(512)} %param.18) | copy-start | bytes 3460
  125.0 40.2 %all-to-all-start.1 = ((bf16[16,24,288]{2,1,0:T(8,128)(2,1)}), bf16[16,24,288]{2,1,0:T(8,128)(2,1)}, u32[]{:S(2)}, u32[]{:S(2)}) async-start(bf16[16,24,288]{2,1,0:T(8,128)(2,1)} %bitcast.5), calls=%async_computation.1 | async-start | bytes 589824 | tf_op jit(solution)/shard_map/all_to_all | solution.py:309
  140.2 10.2 %copy-start = (bf16[384,1152]{1,0:T(8,128)(2,1)}, bf16[384,1152]{1,0:T(8,128)(2,1)S(1)}, u32[]{:S(2)}) copy-start(bf16[384,1152]{1,0:T(8,128)(2,1)S(1)} %get-tuple-element.21.refs_0_) | copy-start | bytes 2654212
  (3 other events, 18.1 us)
where the time goes:
time: 174 us; the launch traced here: 173 us
  local copies, waits for them, and re-layouts  44 us (25%)
  waiting for transfers between devices  43.5 us (25%)
  Pallas kernels  41.7 us (24%)
  starting transfers between devices  38.5 us (22%)
  between operations  2.83 us (2%)
  other arithmetic  2.55 us (1%)
    ppermute x25, waiting for transfers between devices, swap(): return lax.ppermute(value, axis, [(i, i ^ by) for i in range(size)])  43.5 us
    pallas_call x6, Pallas kernels, call(): pl.pallas_call(kernel, out_shape=outs if single else tuple(outs), in_spec...  41.7 us
    ppermute x25, starting transfers between devices, swap(): return lax.ppermute(value, axis, [(i, i ^ by) for i in range(size)])  29.3 us
    unnamed x42, local copies, waits for them, and re-layouts  18.4 us
    concatenate x4, local copies, waits for them, and re-layouts, gather_blocks(): return jnp.concatenate([near, one, two], axis=0)  8.92 us
    ppermute x2, local copies, waits for them, and re-layouts, swap(): return lax.ppermute(value, axis, [(i, i ^ by) for i in range(size)])  5.76 us
    all_to_all x1, starting transfers between devices, per_device(): lax.all_to_all(timed.reshape(size, positions, 2 * tw), 'tm', split_axis=0...  5.57 us
    all_to_all x1, starting transfers between devices, per_device(): lax.all_to_all(tokens.reshape(size, positions, depth), 'tm', split_axis=0...  3.63 us
  transfers between devices with their start and end apart: 27, of which 10 were waited for; matrix products, arithmetic and copies ran while one was open for 26% of the time, Pallas kernels for 21%

commit v1 on v0

v1 whole, which is shorter than its diff:
```python
import functools
import math

import jax
import jax.numpy as jnp
from jax import lax
from jax.experimental import pallas as pl
from jax.experimental.pallas import tpu as pltpu
from jax.sharding import PartitionSpec as P

HD = 72
CROSS_HEADS = 8
TIME_HEADS = 4
BOX_HEADS = 4
DEAD = -1e30
DEFINITE = 1e29
F32 = jnp.float32
BF16 = jnp.bfloat16
FLOPS_A_US = 1.1e9
BYTES_A_US = 3.6e6


def swap(value, axis, by):
    size = lax.axis_size(axis)
    return lax.ppermute(value, axis, [(i, i ^ by) for i in range(size)])


def tie(value, *before):
    return lax.optimization_barrier((value, *before))[0]


def tie_all(values, *before):
    return lax.optimization_barrier((*values, *before))[: len(values)]


def far_blocks(shard):
    size = lax.axis_size("tm")
    return jnp.concatenate([shard] + [swap(shard, "tm", d) for d in range(4, size, 4)], axis=0)


def near_step(value, step):
    size, cameras = lax.axis_size("tm"), lax.axis_size("view")
    pairs = [
        (v * size + i, v * size + (i ^ (1 << (v + step) % 2)))
        for v in range(cameras)
        for i in range(size)
    ]
    return lax.ppermute(value, ("view", "tm"), pairs)


def load_blocks(pieces, first, scratch, sems, columns):
    rows = pieces[0].shape[0]
    to = [0, (1 + first) * rows, (2 - first) * rows, 3 * rows]
    copies = [
        pltpu.make_async_copy(
            piece.at[:, columns], scratch.at[pl.ds(pl.multiple_of(at, 16), rows)], sems.at[j]
        )
        for j, (piece, at) in enumerate(zip(pieces, to))
    ]
    for copy in copies:
        copy.start()

    def wait():
        for copy in copies:
            copy.wait()

    return wait


def block_order(size):
    far = list(range(0, size, 4))
    return [f ^ low for low in range(4) for f in far]


def dot(a, b):
    return jnp.dot(a, b, preferred_element_type=F32)


def dot_t(a, b):
    return lax.dot_general(a, b, (((1,), (1,)), ((), ())), preferred_element_type=F32)


def chooser(rows, source, offset=0):
    row_ids = lax.broadcasted_iota(jnp.int32, (rows, source.shape[1]), 0)
    return (row_ids + offset == source).astype(F32).astype(BF16)


def attend_heads(query, keys, values, masks, offsets, store):
    width = query.shape[1]
    scale = HD ** (-0.5) * math.log2(math.e)
    for head in range(width // HD):
        low, high = head * HD, (head + 1) * HD
        left = low // 128 * 128
        right = min(width, -(-high // 128) * 128)
        lane = lax.broadcasted_iota(jnp.int32, (1, right - left), 1) + left
        mine = (lane >= low) & (lane < high)
        q = jnp.where(mine, query[:, left:right].astype(F32), 0.0).astype(BF16)
        scores = [dot_t(q, k[:, left:right]) for k in keys]
        scores = [s if m is None else jnp.where(m, s, DEAD) for s, m in zip(scores, masks)]
        tops = [jnp.max(s, axis=-1, keepdims=True) for s in scores]
        tops = [t if o is None else jnp.where(o < DEFINITE, t, DEAD) for t, o in zip(tops, offsets)]
        top = functools.reduce(jnp.maximum, tops)
        expos = [
            jnp.exp2((s - (top if o is None else top + o)) * scale) for s, o in zip(scores, offsets)
        ]
        total = sum(jnp.sum(e, axis=-1, keepdims=True) for e in expos)
        out = sum(dot(e.astype(BF16), v[:, left:right]) for e, v in zip(expos, values))
        store(left, right, mine, out / total)


def keep_rows(half, ref, at, end, left, right, mine, result):
    ref[half, at:end, left:right] = jnp.where(mine, result, ref[half, at:end, left:right])


def keep_in(ref):
    def store(left, right, mine, result):
        ref[:, left:right] = jnp.where(mine, result, ref[:, left:right])

    return store


def send_kernel(
    half_ref, count_ref, valid_ref, qkv_ref, w_out_ref, box_ref, early_ref, cross_ref, closing_ref,
    *, parts,
):
    cw, tw, bw = parts
    block, width = early_ref.shape
    rows, depth = w_out_ref.shape
    lane = lax.broadcasted_iota(jnp.int32, (8, 128), 1)
    live = (lane < count_ref[0, 0]) & (lane < box_ref.shape[0])
    flags = jnp.where(live & (jnp.full((8, 128), valid_ref[0, 0]) == 1), 1.0, 0.0)
    boxes = box_ref[...].astype(F32)
    carried = [boxes[:8], boxes[8:], flags]
    filled = 2 * depth + 128
    carried = jnp.concatenate(carried + [jnp.zeros((8, 3 * width - filled), F32)], axis=1)
    carried = [carried[:, j * width : (j + 1) * width] for j in range(3)]

    def side_columns(side):
        def part(base, size):
            at = [kind * depth + base + side * size for kind in range(3)]
            return [qkv_ref[:, a : a + size].astype(F32) for a in at]

        def fill(x, to, axis):
            size = list(x.shape)
            size[axis] = to - size[axis]
            return jnp.concatenate([x, jnp.zeros(size, F32)], axis) if size[axis] else x

        weights = jnp.concatenate(part(2 * cw, tw) + part(2 * cw + 2 * tw, bw), axis=1)
        early = jnp.concatenate(carried + [fill(weights, width, 1)], axis=0)
        early_ref[...] = fill(early, block, 0).astype(BF16)
        cross = jnp.concatenate(part(0, cw), axis=1)
        cross_ref[...] = fill(cross, cross_ref.shape[1], 1).astype(BF16)
        at = side * (depth - closing_ref.shape[1])
        closing_ref[...] = w_out_ref[:, at : at + closing_ref.shape[1]]

    for side in range(2):
        pl.when(half_ref[0] == side)(functools.partial(side_columns, side))


def order_kernel(tokens_ref, *refs, others):
    other_refs = refs[:others]
    source_ref, wide_source_ref, out_ref, wide_ref, pick_ref = refs[others : others + 5]
    out_refs = refs[others + 5 :]
    depth = tokens_ref.shape[1]
    pick = chooser(depth, source_ref[...])
    out_ref[...] = dot(tokens_ref[...], pick).astype(BF16)
    for a, b in zip(other_refs, out_refs):
        b[...] = dot(a[...], pick).astype(BF16)
    pick_ref[...] = chooser(depth, wide_source_ref[...])
    wide_ref[...] = dot(tokens_ref[...], pick_ref[...]).astype(BF16)


def regroup(rows, positions):
    frames = rows // positions
    to = lax.broadcasted_iota(jnp.int32, (rows, 1), 0)
    source = (to % frames) * positions + to // frames
    return (lax.broadcasted_iota(jnp.int32, (1, rows), 1) == source).astype(F32).astype(BF16)


def widen_kernel(tokens_ref, pick_ref, wide_ref, *, positions):
    tokens = tokens_ref[...]
    tokens = dot(regroup(tokens.shape[0], positions), tokens).astype(BF16)
    wide_ref[...] = dot(tokens, pick_ref[...]).astype(BF16)


def load_halves(half_ref, piece_refs, scratch, sems, columns):
    return [
        load_blocks(
            piece_refs[4 * j : 4 * j + 4],
            half_ref[0] if j == 0 else 1 - half_ref[0],
            scratch.at[j],
            sems.at[j],
            columns,
        )
        for j in range(2)
    ]


def time_kernel(half_ref, wide_ref, *refs, positions):
    piece_refs, (out_ref, acc_ref, weight_ref, sems) = refs[:8], refs[8:]
    waits = load_halves(half_ref, piece_refs, weight_ref, sems, pl.ds(0, weight_ref.shape[2]))
    rows = wide_ref.shape[0]
    frames = rows // positions
    part = out_ref.shape[1] // 2
    step = max(frames, 128) if rows % max(frames, 128) == 0 else rows
    group = lax.broadcasted_iota(jnp.int32, (step, 1), 0) // frames
    group_t = lax.broadcasted_iota(jnp.int32, (1, step), 1) // frames
    live = group == group_t
    wide = wide_ref[...]
    for half in range(2):
        waits[half]()
        qkv = dot(wide, weight_ref[half]).astype(BF16)
        q, k, v = (qkv[:, j * part : (j + 1) * part] for j in range(3))
        for at in range(0, rows, step):
            end = at + step
            attend_heads(
                q[at:end], [k[at:end]], [v[at:end]], [live], [None],
                functools.partial(keep_rows, half, acc_ref, at, end),
            )
    timed = jnp.concatenate([acc_ref[0].astype(BF16), acc_ref[1].astype(BF16)], axis=1)
    back = lax.dot_general(
        regroup(rows, positions), timed, (((0,), (0,)), ((), ())), preferred_element_type=F32
    )
    out_ref[...] = back.astype(BF16)


def box_kernel(
    half_ref, wide_ref, pick_ref, gate_ref, *refs, slots, blocks, skip
):
    piece_refs = refs[:8]
    out_ref, acc_ref, box_ref, flag_ref, weight_ref, carried_ref, sems, carried_sems = refs[8:]
    part = out_ref.shape[1] // 2
    depth = box_ref.shape[1]
    block, width = carried_ref.shape[0] // blocks, carried_ref.shape[1]
    left = skip // 128 * 128
    carried = load_blocks(
        piece_refs[:4], half_ref[0], carried_ref, carried_sems, pl.ds(0, width)
    )
    waits = load_halves(
        half_ref, piece_refs, weight_ref, sems, pl.ds(left, weight_ref.shape[2])
    )
    wide = wide_ref[...]
    shift = skip - left
    carried()
    for b in range(blocks):
        at = b * block
        top = carried_ref[at : at + 16, :].astype(F32)
        low = carried_ref[at + 16 : at + 32, :].astype(F32)[:8]
        spread = 2 * width - depth
        rest = depth - spread
        to = b * 8
        box_ref[to : to + 8, :width] = top[:8]
        box_ref[to : to + 8, width:] = top[8:, : depth - width]
        to += blocks * 8
        box_ref[to : to + 8, :spread] = top[8:, depth - width :]
        box_ref[to : to + 8, spread:] = low[:, :rest]
        flag_ref[b : b + 1, :] = low[:1, rest : rest + 128]
    slot_lane = lax.broadcasted_iota(jnp.int32, (1, blocks * slots), 1)
    group = slot_lane // (8 * blocks)
    slot = group * 8 + slot_lane % 8
    of_block = (slot_lane // 8) % blocks
    spread_slots = (
        lax.broadcasted_iota(jnp.int32, (128, blocks * slots), 0) == slot
    ).astype(F32)
    flags = dot(flag_ref[...].astype(BF16), spread_slots.astype(BF16))
    mine = lax.broadcasted_iota(jnp.int32, (blocks, blocks * slots), 0) == of_block
    live = jnp.sum(jnp.where(mine, flags, 0.0), axis=0, keepdims=True)
    box = dot(box_ref[...].astype(BF16), pick_ref[...]).astype(BF16)
    for half in range(2):
        waits[half]()
        weights = weight_ref[half]
        qkv = dot(wide, weights).astype(BF16)[:, shift : shift + 3 * part]
        box_kv = dot(box, weights).astype(BF16)[:, shift + part : shift + 3 * part]
        attend_heads(
            qkv[:, :part],
            [qkv[:, part : 2 * part], box_kv[:, :part]],
            [qkv[:, 2 * part :], box_kv[:, part:]],
            [None, live > 0],
            [None, None],
            keep_in(acc_ref),
        )
        out_ref[:, half * part : (half + 1) * part] = (
            acc_ref[...] * jnp.tanh(gate_ref[half : half + 1, :])
        ).astype(BF16)


def cross_kernel(half_ref, count_ref, tokens_ref, *refs, others):
    other_refs, piece_refs = refs[:others], refs[others : others + 8]
    out_ref, acc_ref, weight_ref, sems = refs[others + 8 :]
    waits = load_halves(half_ref, piece_refs, weight_ref, sems, pl.ds(0, weight_ref.shape[2]))
    part = out_ref.shape[1] // 2
    unit = math.log(2) / HD ** (-0.5)
    offsets = [None]
    for j in range(others):
        count = jnp.full((1, 1), count_ref[0, j], F32)
        offsets.append(jnp.where(count > 1.5, -unit, jnp.where(count > 0.5, 0.0, -DEAD)))
    for half in range(2):
        waits[half]()
        weights = weight_ref[half]
        own = dot(tokens_ref[...], weights).astype(BF16)
        at = part // 128 * 128
        kv = [own[:, part : 3 * part]] + [
            dot(o[...], weights[:, at:]).astype(BF16)[:, part - at : 3 * part - at]
            for o in other_refs
        ]
        attend_heads(
            own[:, :part],
            [x[:, :part] for x in kv],
            [x[:, part:] for x in kv],
            [None] * (1 + others),
            offsets,
            keep_in(acc_ref),
        )
        out_ref[:, half * part : (half + 1) * part] = acc_ref[...].astype(BF16)


def collect_kernel(half_ref, source_ref, cross_ref, time_ref, box_ref, out_ref):
    which = half_ref[0]
    total = None
    base = 0
    for ref in (cross_ref, time_ref, box_ref):
        part = ref.shape[1] // 2
        for half in range(2):
            side = which if half == 0 else 1 - which
            pick = chooser(part, source_ref[...], base + side * part)
            term = dot(ref[:, half * part : (half + 1) * part], pick)
            total = term if total is None else total + term
        base += 2 * part
    out_ref[...] = total.astype(BF16)


def final_kernel(half_ref, tokens_ref, attn_ref, *refs):
    piece_refs, (out_ref, weight_ref, sems) = refs[:8], refs[8:]
    width = weight_ref.shape[2]
    waits = load_halves(half_ref, piece_refs, weight_ref, sems, pl.ds(0, width))
    step = out_ref.shape[1] - width
    for half in range(2):
        waits[half]()
        side = half_ref[0] if half == 0 else 1 - half_ref[0]
        at = pl.ds(pl.multiple_of(side * step, 128), width)
        out_ref[:, at] = (tokens_ref[:, at].astype(F32) + dot(attn_ref[...], weight_ref[half])).astype(
            BF16
        )


def call(kernel, outs, *args, scalars=0, scratch=(), pieces=(), name=None, vmem_mib=24, us=4):
    vmem = pl.BlockSpec(memory_space=pltpu.VMEM)
    smem = pl.BlockSpec(memory_space=pltpu.SMEM)
    anywhere = pl.BlockSpec(memory_space=pl.ANY)
    single = not isinstance(outs, list)
    return pl.pallas_call(
        kernel,
        out_shape=outs if single else tuple(outs),
        in_specs=[smem] * scalars + [vmem] * (len(args) - scalars) + [anywhere] * len(pieces),
        out_specs=vmem if single else tuple(vmem for _ in outs),
        scratch_shapes=list(scratch),
        compiler_params=pltpu.CompilerParams(vmem_limit_bytes=vmem_mib * 2**20),
        cost_estimate=pl.CostEstimate(
            flops=int(us * FLOPS_A_US), bytes_accessed=int(us * BYTES_A_US), transcendentals=0
        ),
        name=name,
    )(*args, *pieces)


def whole_tiles(width):
    return -(-width // 128) * 128


def shaped(*dims):
    return jax.ShapeDtypeStruct(dims, BF16)


def per_device(frames_x, box_embed, box_count, frame_valid, cycle_link, w_qkv, w_out, box_gate):
    size = lax.axis_size("tm")
    cameras = lax.axis_size("view")
    depth = frames_x.shape[3]
    tokens = frames_x.reshape(-1, depth)
    count = tokens.shape[0]
    slots = box_embed.shape[2]
    boxes = box_embed.reshape(slots, depth)
    rows = w_qkv.shape[0]
    index = lax.axis_index("tm")
    half = lax.axis_index("view") % 2
    cw, tw, bw = (heads * HD // 2 for heads in (CROSS_HEADS, TIME_HEADS, BOX_HEADS))

    width, out_width = whole_tiles(3 * (tw + bw)), whole_tiles(depth // 2)
    cross_width = whole_tiles(3 * cw)
    used = 24 + rows
    block = -(-used // 16) * 16
    which = half.reshape(1).astype(jnp.int32)
    early, crossing, closing = call(
        functools.partial(send_kernel, parts=(cw, tw, bw)),
        [shaped(block, width), shaped(rows, cross_width), shaped(rows, out_width)],
        which, box_count, frame_valid, w_qkv, w_out, boxes,
        scalars=3, name="send", us=2,
    )

    if cameras == 2:
        others = [swap(tokens, "view", 1)]
        link_counts = (cycle_link[:, :1] + cycle_link[:, 1:]).astype(F32)
    else:
        ring = range(cameras)
        others = [
            lax.ppermute(tokens, "view", [(i, (i + by) % cameras) for i in ring]) for by in (1, -1)
        ]
        link_counts = cycle_link.astype(F32)
    owners = index ^ jnp.array(block_order(size), jnp.int32)
    source = (owners[:, None] * rows + jnp.arange(rows)[None]).reshape(1, -1)
    wide_source = jnp.full((size, block), -1, jnp.int32)
    wide_source = wide_source.at[:, 24:used].set(source.reshape(size, rows)).reshape(1, -1)

    ordered, wide, pick, *ordered_others = call(
        functools.partial(order_kernel, others=len(others)),
        [shaped(count, depth), shaped(count, size * block), shaped(depth, size * block)]
        + [shaped(count, depth) for _ in others],
        tokens, *others, source, wide_source,
        name="order", us=6,
    )

    def near_blocks(far, *before):
        one = near_step(far, 0)
        two = near_step(far, 1)
        return far, one, two, near_step(tie(one, *before) if before else one, 1)

    def with_other_core(blocks):
        return (*blocks, *(swap(b, "view", 1) for b in blocks))

    def weight_scratch(far_rows, columns):
        return [pltpu.VMEM((2, 4 * far_rows, columns), BF16), pltpu.SemaphoreType.DMA((2, 4))]

    early = far_blocks(early)
    crossing = far_blocks(tie(crossing, early))
    positions = count // size
    token_slices = lax.all_to_all(
        tie(tokens, early).reshape(size, positions, depth),
        "tm", split_axis=0, concat_axis=0, tiled=True,
    ).reshape(count, depth)
    early = near_blocks(early, ordered)
    wide_slices = call(
        functools.partial(widen_kernel, positions=positions),
        shaped(count, size * block), token_slices, pick, name="widen", us=2,
    )
    closing = far_blocks(tie(closing, token_slices))
    early_rows = early[0].shape[0]
    early_near = early
    early = with_other_core(early)
    timed = call(
        functools.partial(time_kernel, positions=positions),
        shaped(count, 2 * tw),
        which, wide_slices,
        scalars=1,
        pieces=early,
        scratch=[pltpu.VMEM((2, count, tw), F32)]
        + weight_scratch(early_rows, whole_tiles(3 * tw)),
        name="timed", us=5,
    )
    timed_here = timed
    crossing = near_blocks(tie(crossing, early_near[1], early_near[2]), timed_here)
    timed = lax.all_to_all(
        timed.reshape(size, positions, 2 * tw), "tm", split_axis=0, concat_axis=0, tiled=True
    ).reshape(count, 2 * tw)
    closing = near_blocks(closing, timed_here)
    link_counts = tie(link_counts, timed_here)
    gates = box_gate.reshape(2, bw)
    gates = jnp.where(half == 0, gates, gates[::-1])
    boxed = call(
        functools.partial(box_kernel, slots=slots, blocks=size, skip=3 * tw),
        shaped(count, 2 * bw),
        which, wide, pick, gates,
        scalars=1,
        pieces=early,
        scratch=[
            pltpu.VMEM((count, bw), F32),
            pltpu.VMEM((size * slots, depth), F32),
            pltpu.VMEM((size, 128), F32),
            *weight_scratch(early_rows, width - 3 * tw // 128 * 128)[:1],
            pltpu.VMEM((size * block, width), BF16),
            *weight_scratch(early_rows, width)[1:],
            pltpu.SemaphoreType.DMA((4,)),
        ],
        name="boxed", us=7,
    )
    cross_rows = crossing[0].shape[0]
    cross = call(
        functools.partial(cross_kernel, others=len(others)),
        shaped(count, 2 * cw),
        which, link_counts, ordered, *ordered_others,
        scalars=2,
        pieces=with_other_core(crossing),
        scratch=[pltpu.VMEM((count, cw), F32)] + weight_scratch(cross_rows, cross_width),
        name="cross", us=9,
    )
    attn = call(
        collect_kernel, shaped(count, depth), which, source, cross, timed, boxed,
        scalars=1, name="collect", us=2,
    )
    result = call(
        final_kernel, shaped(count, depth), which, tokens, attn,
        scalars=1,
        pieces=with_other_core(closing),
        scratch=weight_scratch(closing[0].shape[0], out_width),
        name="final", us=4,
    )
    return result.reshape(frames_x.shape)


def solution(mesh):
    in_specs = (
        P("view", "tm", None, None),
        P("view", "tm", None, None),
        P("view", "tm"),
        P("view", "tm"),
        P("view", None),
        P("tm", None),
        P("tm", None),
        P(),
    )
    out_specs = P("view", "tm", None, None)
    return jax.shard_map(
        per_device, mesh=mesh, in_specs=in_specs, out_specs=out_specs, check_vma=False
    )
```

time: 174 us -> 128 us (0.74)
  local copies, waits for them, and re-layouts: 44 us -> 16.3 us
  waiting for transfers between devices: 43.5 us -> 27.8 us
  other arithmetic: 2.55 us -> 0.12 us
    ppermute x25 -> x22, waiting for transfers between devices: 43.5 us -> 25.1 us  [swap(): return lax.ppermute(value, axis, [(i, i ^ by) for i in range(size)])]
    concatenate x11 -> x2, local copies, waits for them, and re-layouts: 16.6 us -> 0.04 us  [far_blocks(): jnp.concatenate([shard] + [swap(shard, 'tm', d) for d in range(4, size, 4...]
    ppermute x25 -> x22, starting transfers between devices: 29.3 us -> 17.7 us  [swap(): return lax.ppermute(value, axis, [(i, i ^ by) for i in range(size)])]
    ppermute x0 -> x9, starting transfers between devices: none -> 11.2 us  [near_step(): return lax.ppermute(value, ('view', 'tm'), pairs)]
    ppermute x2 -> x0, local copies, waits for them, and re-layouts: 5.76 us -> none  [swap(): return lax.ppermute(value, axis, [(i, i ^ by) for i in range(size)])]
    unnamed x42 -> x44, local copies, waits for them, and re-layouts: 18.4 us -> 15.3 us
    ppermute x0 -> x9, waiting for transfers between devices: none -> 2.78 us  [near_step(): return lax.ppermute(value, ('view', 'tm'), pairs)]
    all_to_all x1, starting transfers between devices: 3.63 us -> 6.13 us  [per_device(): lax.all_to_all(tie(tokens, early).reshape(size, positions, depth), 'tm',...]
  transfers between devices with their start and end apart: 27 -> 33, of which waited for: 10 -> 6; matrix products, arithmetic and copies ran while one was open for 26% -> 1% of each run, Pallas kernels for 21% -> 28%
where the time goes in v1:
time: 128 us
  Pallas kernels  41.1 us (32%)
  starting transfers between devices  39.3 us (31%)
  waiting for transfers between devices  27.8 us (22%)
  local copies, waits for them, and re-layouts  16.3 us (13%)
  between operations  2.99 us (2%)
    pallas_call x8, Pallas kernels, call(): pl.pallas_call(kernel, out_shape=outs if single else tuple(outs), in_spec...  41.1 us
    ppermute x22, waiting for transfers between devices, swap(): return lax.ppermute(value, axis, [(i, i ^ by) for i in range(size)])  25.1 us
    ppermute x22, starting transfers between devices, swap(): return lax.ppermute(value, axis, [(i, i ^ by) for i in range(size)])  17.7 us
    unnamed x44, local copies, waits for them, and re-layouts  15.3 us
    ppermute x9, starting transfers between devices, near_step(): return lax.ppermute(value, ('view', 'tm'), pairs)  11.2 us
    all_to_all x1, starting transfers between devices, per_device(): lax.all_to_all(tie(tokens, early).reshape(size, positions, depth), 'tm',...  6.13 us
    all_to_all x1, starting transfers between devices, per_device(): lax.all_to_all(timed.reshape(size, positions, 2 * tw), 'tm', split_axis=0...  4.3 us
    ppermute x9, waiting for transfers between devices, near_step(): return lax.ppermute(value, ('view', 'tm'), pairs)  2.78 us
  transfers between devices with their start and end apart: 33, of which 6 were waited for; matrix products, arithmetic and copies ran while one was open for 1% of the time, Pallas kernels for 28%

profile of v1, /device:TPU:0, one launch (start us, length us, event | category | flops | bytes accessed | tf_op | source)
XLA Modules:
  0.0 127.7 jit_solution(14115108287944804905)
XLA Ops:
  1.3 1.0 copy-done
  4.2 3.1 %collective-permute-start = (bf16[96,896]{1,0:T(8,128)(2,1)S(1)}, bf16[96,896]{1,0:T(8,128)(2,1)S(1)}, u32[]{:S(2)}, u32[]{:S(2)}) collective-permute-start(bf16[96,896]{1,0:T(8,128)(2,1)S(1)} %get-tuple-element.32), channel_id=1, source_target_pairs={{0,4},{1,5},{2,6},{3,7},{4,0},{5,1},{6,2},{7,3},{8,12},{9,13},{10,... | collective-permute-start | bytes 516104 | tf_op jit(solution)/shard_map/ppermute | solution.py:25
  7.3 2.6 %collective-permute-start.1 = (bf16[96,896]{1,0:T(8,128)(2,1)S(1)}, bf16[96,896]{1,0:T(8,128)(2,1)S(1)}, u32[]{:S(2)}, u32[]{:S(2)}) collective-permute-start(bf16[96,896]{1,0:T(8,128)(2,1)S(1)} %get-tuple-element.32), channel_id=1, source_target_pairs={{0,8},{1,9},{2,10},{3,11},{4,12},{5,13},{6,14},{7,15},{8,0},{9,1},... | collective-permute-start | bytes 516104 | tf_op jit(solution)/shard_map/ppermute | solution.py:25
  9.9 4.4 %collective-permute-done = bf16[96,896]{1,0:T(8,128)(2,1)S(1)} collective-permute-done((bf16[96,896]{1,0:T(8,128)(2,1)S(1)}, bf16[96,896]{1,0:T(8,128)(2,1)S(1)}, u32[]{:S(2)}, u32[]{:S(2)}) %collective-permute-start) | collective-permute-done | bytes 172064 | tf_op jit(solution)/shard_map/ppermute | solution.py:25
  14.4 8.5 %collective-permute-done.1 = bf16[96,896]{1,0:T(8,128)(2,1)S(1)} collective-permute-done((bf16[96,896]{1,0:T(8,128)(2,1)S(1)}, bf16[96,896]{1,0:T(8,128)(2,1)S(1)}, u32[]{:S(2)}, u32[]{:S(2)}) %collective-permute-start.1) | collective-permute-done | bytes 172064 | tf_op jit(solution)/shard_map/ppermute | solution.py:25
  22.9 1.6 %collective-permute-start.4 = (bf16[384,896]{1,0:T(8,128)(2,1)S(1)}, bf16[384,896]{1,0:T(8,128)(2,1)}, u32[]{:S(2)}, u32[]{:S(2)}) collective-permute-start(bf16[384,896]{1,0:T(8,128)(2,1)S(1)} %constant_dynamic-update-slice_fusion.refs_0_), channel_id=1, source_target_pairs={{0,1},{1,0},{2,3},{3,2},{4,5},{5,4},{6,7},{7,6},{8,9},{9,8},{10,11... | collective-permute-start | bytes 2064392 | tf_op jit(solution)/shard_map/ppermute | solution.py:48
  24.5 6.1 %all-to-all-start = ((bf16[16,24,1152]{2,1,0:T(8,128)(2,1)}), bf16[16,24,1152]{2,1,0:T(8,128)(2,1)S(1)}, u32[]{:S(2)}, u32[]{:S(2)}) async-start(bf16[16,24,1152]{2,1,0:T(8,128)(2,1)} %bitcast.3), calls=%async_computation | async-start | bytes 1769472 | tf_op jit(solution)/shard_map/all_to_all | solution.py:434
  30.9 2.0 %collective-permute-start.5 = (bf16[384,896]{1,0:T(8,128)(2,1)S(1)}, bf16[384,896]{1,0:T(8,128)(2,1)}, u32[]{:S(2)}, u32[]{:S(2)}) collective-permute-start(bf16[384,896]{1,0:T(8,128)(2,1)S(1)} %constant_dynamic-update-slice_fusion.refs_0_), channel_id=1, source_target_pairs={{0,2},{1,3},{2,0},{3,1},{4,6},{5,7},{6,4},{7,5},{8,10},{9,11},{10,... | collective-permute-start | bytes 2064392 | tf_op jit(solution)/shard_map/ppermute | solution.py:48
  32.9 5.7 %order.1 = (bf16[384,1152]{1,0:T(8,128)(2,1)S(1)}, bf16[384,1536]{1,0:T(8,128)(2,1)S(1)}, bf16[1152,1536]{1,0:T(8,128)(2,1)S(1)}, bf16[384,1152]{1,0:T(8,128)(2,1)S(1)}) custom-call(bf16[384,1152]{1,0:T(8,128)(2,1)} %bitcast.1.tokens_ref, bf16[384,1152]{1,0:T(8,128)(2,1)S(1)} %collective-permute-done.3.refs_0_, s32[1,1152]{1,0:T(1,128)S(1)} %add.38.refs_1_.source_ref, ...), custom_call_target="tpu_custom_call" | custom-call | flops 6600000000 | bytes 21600000 | tf_op jit(solution)/shard_map/order/pallas_call | solution.py:351
  38.6 1.8 %copy-done.3 = bf16[1152,1536]{1,0:T(8,128)(2,1)} copy-done((bf16[1152,1536]{1,0:T(8,128)(2,1)}, bf16[1152,1536]{1,0:T(8,128)(2,1)S(1)}, u32[]{:S(2)}) %copy-start.3) | copy-done | bytes 3538968
  40.4 1.0 copy-done.10
  43.4 2.0 %collective-permute-start.11 = (bf16[72,896]{1,0:T(8,128)(2,1)S(1)}, bf16[72,896]{1,0:T(8,128)(2,1)S(1)}, u32[]{:S(2)}, u32[]{:S(2)}) collective-permute-start(bf16[72,896]{1,0:T(8,128)(2,1)S(1)} %get-tuple-element.40), channel_id=1, source_target_pairs={{0,4},{1,5},{2,6},{3,7},{4,0},{5,1},{6,2},{7,3},{8,12},{9,13},{10,... | collective-permute-start | bytes 387080 | tf_op jit(solution)/shard_map/ppermute | solution.py:25
  45.4 2.2 %collective-permute-start.12 = (bf16[72,896]{1,0:T(8,128)(2,1)S(1)}, bf16[72,896]{1,0:T(8,128)(2,1)S(1)}, u32[]{:S(2)}, u32[]{:S(2)}) collective-permute-start(bf16[72,896]{1,0:T(8,128)(2,1)S(1)} %get-tuple-element.40), channel_id=1, source_target_pairs={{0,8},{1,9},{2,10},{3,11},{4,12},{5,13},{6,14},{7,15},{8,0},{9,1},... | collective-permute-start | bytes 387080 | tf_op jit(solution)/shard_map/ppermute | solution.py:25
  49.4 11.4 %collective-permute-done.12 = bf16[72,896]{1,0:T(8,128)(2,1)S(1)} collective-permute-done((bf16[72,896]{1,0:T(8,128)(2,1)S(1)}, bf16[72,896]{1,0:T(8,128)(2,1)S(1)}, u32[]{:S(2)}, u32[]{:S(2)}) %collective-permute-start.12) | collective-permute-done | bytes 129056 | tf_op jit(solution)/shard_map/ppermute | solution.py:25
  61.4 1.7 %collective-permute-start.21 = (bf16[72,640]{1,0:T(8,128)(2,1)S(1)}, bf16[72,640]{1,0:T(8,128)(2,1)S(1)}, u32[]{:S(2)}, u32[]{:S(2)}) collective-permute-start(bf16[72,640]{1,0:T(8,128)(2,1)S(1)} %get-tuple-element.45), channel_id=1, source_target_pairs={{0,4},{1,5},{2,6},{3,7},{4,0},{5,1},{6,2},{7,3},{8,12},{9,13},{10,... | collective-permute-start | bytes 276488 | tf_op jit(solution)/shard_map/ppermute | solution.py:25
  63.2 2.0 %copy-done.4 = bf16[1152,1536]{1,0:T(8,128)(2,1)S(1)} copy-done((bf16[1152,1536]{1,0:T(8,128)(2,1)S(1)}, bf16[1152,1536]{1,0:T(8,128)(2,1)}, u32[]{:S(2)}) %copy-start.4) | copy-done | bytes 3538968
  65.2 2.2 %widen.1.wide_ref = bf16[384,1536]{1,0:T(8,128)(2,1)S(1)} custom-call(bf16[384,1152]{1,0:T(8,128)(2,1)S(1)} %bitcast.8, bf16[1152,1536]{1,0:T(8,128)(2,1)S(1)} %copy-done.4), custom_call_target="tpu_custom_call" | custom-call | flops 2200000000 | bytes 7200000 | tf_op jit(solution)/shard_map/widen/pallas_call | solution.py:351
  67.4 1.5 %collective-permute-start.14 = (bf16[288,896]{1,0:T(8,128)(2,1)S(1)}, bf16[288,896]{1,0:T(8,128)(2,1)S(1)}, u32[]{:S(2)}, u32[]{:S(2)}) collective-permute-start(bf16[288,896]{1,0:T(8,128)(2,1)S(1)} %pad_maximum_fusion.refs_1_), channel_id=1, source_target_pairs={{0,1},{1,0},{2,3},{3,2},{4,5},{5,4},{6,7},{7,6},{8,9},{9,8},{10,11... | collective-permute-start | bytes 1548296 | tf_op jit(solution)/shard_map/ppermute | solution.py:48
  69.0 1.5 %collective-permute-start.15 = (bf16[288,896]{1,0:T(8,128)(2,1)S(1)}, bf16[288,896]{1,0:T(8,128)(2,1)}, u32[]{:S(2)}, u32[]{:S(2)}) collective-permute-start(bf16[288,896]{1,0:T(8,128)(2,1)S(1)} %pad_maximum_fusion.refs_1_), channel_id=1, source_target_pairs={{0,2},{1,3},{2,0},{3,1},{4,6},{5,7},{6,4},{7,5},{8,10},{9,11},{10,... | collective-permute-start | bytes 1548296 | tf_op jit(solution)/shard_map/ppermute | solution.py:48
  70.9 2.4 %collective-permute-start.23 = (bf16[72,640]{1,0:T(8,128)(2,1)S(1)}, bf16[72,640]{1,0:T(8,128)(2,1)S(1)}, u32[]{:S(2)}, u32[]{:S(2)}) collective-permute-start(bf16[72,640]{1,0:T(8,128)(2,1)S(1)} %get-tuple-element.45), channel_id=1, source_target_pairs={{0,12},{1,13},{2,14},{3,15},{4,8},{5,9},{6,10},{7,11},{8,4},{9,5},... | collective-permute-start | bytes 276488 | tf_op jit(solution)/shard_map/ppermute | solution.py:25
  73.3 5.8 %timed.1 = bf16[384,288]{1,0:T(8,128)(2,1)} custom-call(s32[1]{0:T(128)} %bitcast.half_ref, bf16[384,1536]{1,0:T(8,128)(2,1)S(1)} %widen.1.wide_ref, bf16[384,896]{1,0:T(8,128)(2,1)S(1)} %constant_dynamic-update-slice_fusion.refs_0_, bf16[384,896]{1,0:T(8,128)(2,1)} %collective-permute-done.4.refs_1_, bf16[384,896]{1,0:T(8,128)(2,1)} %collective-permute-done.5.refs_2_, ...), custom_call_target="tpu_custom_call" | custom-call | flops 5500000256 | bytes 18000000 | tf_op jit(solution)/shard_map/timed/pallas_call | solution.py:351
  79.1 2.1 %collective-permute-done.14.refs_2_ = bf16[288,896]{1,0:T(8,128)(2,1)S(1)} collective-permute-done((bf16[288,896]{1,0:T(8,128)(2,1)S(1)}, bf16[288,896]{1,0:T(8,128)(2,1)S(1)}, u32[]{:S(2)}, u32[]{:S(2)}) %collective-permute-start.14) | collective-permute-done | bytes 516128 | tf_op jit(solution)/shard_map/ppermute | solution.py:48
  81.8 1.9 %collective-permute-start.24 = (bf16[288,640]{1,0:T(8,128)(2,1)S(1)}, bf16[288,640]{1,0:T(8,128)(2,1)}, u32[]{:S(2)}, u32[]{:S(2)}) collective-permute-start(bf16[288,640]{1,0:T(8,128)(2,1)S(1)} %constant_dynamic-update-slice_fusion.4.refs_0_), channel_id=1, source_target_pairs={{0,1},{1,0},{2,3},{3,2},{4,5},{5,4},{6,7},{7,6},{8,9},{9,8},{10,11... | collective-permute-start | bytes 1105928 | tf_op jit(solution)/shard_map/ppermute | solution.py:48
  86.2 4.3 %all-to-all-start.1 = ((bf16[16,24,288]{2,1,0:T(8,128)(2,1)}), bf16[16,24,288]{2,1,0:T(8,128)(2,1)S(1)}, u32[]{:S(2)}, u32[]{:S(2)}) async-start(bf16[16,24,288]{2,1,0:T(8,128)(2,1)} %bitcast.5), calls=%async_computation.1 | async-start | bytes 589824 | tf_op jit(solution)/shard_map/all_to_all | solution.py:459
  91.2 1.3 %collective-permute-start.25 = (bf16[288,640]{1,0:T(8,128)(2,1)S(1)}, bf16[288,640]{1,0:T(8,128)(2,1)}, u32[]{:S(2)}, u32[]{:S(2)}) collective-permute-start(bf16[288,640]{1,0:T(8,128)(2,1)S(1)} %constant_dynamic-update-slice_fusion.4.refs_0_), channel_id=1, source_target_pairs={{0,2},{1,3},{2,0},{3,1},{4,6},{5,7},{6,4},{7,5},{8,10},{9,11},{10,... | collective-permute-start | bytes 1105928 | tf_op jit(solution)/shard_map/ppermute | solution.py:48
  93.3 2.0 %copy-done.5 = bf16[1152,1536]{1,0:T(8,128)(2,1)S(1)} copy-done((bf16[1152,1536]{1,0:T(8,128)(2,1)S(1)}, bf16[1152,1536]{1,0:T(8,128)(2,1)}, u32[]{:S(2)}) %copy-start.5) | copy-done | bytes 3538968
  95.3 1.3 copy-done.11
  96.5 8.3 %boxed.1.box_ref = bf16[384,288]{1,0:T(8,128)(2,1)S(1)} custom-call(s32[1]{0:T(128)} %bitcast.half_ref, bf16[384,1536]{1,0:T(8,128)(2,1)S(1)} %copy-done.11, bf16[1152,1536]{1,0:T(8,128)(2,1)S(1)} %copy-done.5, f32[2,144]{1,0:T(2,128)S(1)} %broadcast_select_fusion.gate_ref, bf16[384,896]{1,0:T(8,128)(2,1)S(1)} %constant_dynamic-update-slice_fusion.refs_0_, ...), custom_call_target="tpu_custom_call" | custom-call | flops 7699999744 | bytes 25200000 | tf_op jit(solution)/shard_map/boxed/pallas_call | solution.py:351
  106.7 11.0 %cross.1.cross_ref = bf16[384,576]{1,0:T(8,128)(2,1)S(1)} custom-call(s32[1]{0:T(128)} %bitcast.half_ref, f32[1,1]{1,0:T(1,128)S(6)} %convert_element_type.3.count_ref, bf16[384,1152]{1,0:T(8,128)(2,1)S(1)} %copy-done.13, bf16[384,1152]{1,0:T(8,128)(2,1)S(1)} %copy-done.15, bf16[288,896]{1,0:T(8,128)(2,1)S(1)} %pad_maximum_fusion.refs_1_, ...), custom_call_target="tpu_custom_call" | custom-call | flops 9900000256 | bytes 32400000 | tf_op jit(solution)/shard_map/cross/pallas_call | solution.py:351
  118.5 1.0 copy-done.7
  119.5 2.2 %collect.1.attn_ref = bf16[384,1152]{1,0:T(8,128)(2,1)S(1)} custom-call(s32[1]{0:T(128)} %bitcast.half_ref, s32[1,1152]{1,0:T(1,128)S(1)} %add.38.refs_1_.source_ref, bf16[384,576]{1,0:T(8,128)(2,1)S(1)} %copy-done.7, bf16[384,288]{1,0:T(8,128)(2,1)S(1)} %bitcast.9, bf16[384,288]{1,0:T(8,128)(2,1)S(1)} %copy-done.9), custom_call_target="tpu_custom_call" | custom-call | flops 2200000000 | bytes 7200000 | tf_op jit(solution)/shard_map/collect/pallas_call | solution.py:351
  121.8 5.7 %final.1 = bf16[384,1152]{1,0:T(8,128)(2,1)} custom-call(s32[1]{0:T(128)} %bitcast.half_ref, bf16[384,1152]{1,0:T(8,128)(2,1)} %bitcast.1.tokens_ref, bf16[384,1152]{1,0:T(8,128)(2,1)S(1)} %collect.1.attn_ref, bf16[288,640]{1,0:T(8,128)(2,1)S(1)} %constant_dynamic-update-slice_fusion.4.refs_0_, bf16[288,640]{1,0:T(8,128)(2,1)} %collective-permute-done.24.refs_1_, ...), custom_call_target="tpu_custom_call" | custom-call | flops 4400000000 | bytes 14400000 | tf_op jit(solution)/shard_map/final/pallas_call | solution.py:351
  (98 shorter events, 12.9 us)
Async XLA Ops:
  4.2 10.2 %collective-permute-start = (bf16[96,896]{1,0:T(8,128)(2,1)S(1)}, bf16[96,896]{1,0:T(8,128)(2,1)S(1)}, u32[]{:S(2)}, u32[]{:S(2)}) collective-permute-start(bf16[96,896]{1,0:T(8,128)(2,1)S(1)} %get-tuple-element.32), channel_id=1, source_target_pairs={{0,4},{1,5},{2,6},{3,7},{4,0},{5,1},{6,2},{7,3},{8,12},{9,13},{10,... | collective-permute-start | bytes 516104 | tf_op jit(solution)/shard_map/ppermute | solution.py:25
  7.3 15.6 %collective-permute-start.1 = (bf16[96,896]{1,0:T(8,128)(2,1)S(1)}, bf16[96,896]{1,0:T(8,128)(2,1)S(1)}, u32[]{:S(2)}, u32[]{:S(2)}) collective-permute-start(bf16[96,896]{1,0:T(8,128)(2,1)S(1)} %get-tuple-element.32), channel_id=1, source_target_pairs={{0,8},{1,9},{2,10},{3,11},{4,12},{5,13},{6,14},{7,15},{8,0},{9,1},... | collective-permute-start | bytes 516104 | tf_op jit(solution)/shard_map/ppermute | solution.py:25
  9.9 13.0 %collective-permute-start.2 = (bf16[96,896]{1,0:T(8,128)(2,1)S(1)}, bf16[96,896]{1,0:T(8,128)(2,1)S(1)}, u32[]{:S(2)}, u32[]{:S(2)}) collective-permute-start(bf16[96,896]{1,0:T(8,128)(2,1)S(1)} %get-tuple-element.32), channel_id=1, source_target_pairs={{0,12},{1,13},{2,14},{3,15},{4,8},{5,9},{6,10},{7,11},{8,4},{9,5},... | collective-permute-start | bytes 516104 | tf_op jit(solution)/shard_map/ppermute | solution.py:25
  9.9 23.0 %collective-permute-start.3 = (bf16[384,1152]{1,0:T(8,128)(2,1)}, bf16[384,1152]{1,0:T(8,128)(2,1)S(1)}, u32[]{:S(2)}, u32[]{:S(2)}) collective-permute-start(bf16[384,1152]{1,0:T(8,128)(2,1)} %bitcast.1.tokens_ref), channel_id=1, source_target_pairs={{0,16},{16,0},{1,17},{17,1},{2,18},{18,2},{3,19},{19,3},{4,20},{20... | collective-permute-start | bytes 2654216 | tf_op jit(solution)/shard_map/ppermute | solution.py:25
  22.9 20.4 %collective-permute-start.4 = (bf16[384,896]{1,0:T(8,128)(2,1)S(1)}, bf16[384,896]{1,0:T(8,128)(2,1)}, u32[]{:S(2)}, u32[]{:S(2)}) collective-permute-start(bf16[384,896]{1,0:T(8,128)(2,1)S(1)} %constant_dynamic-update-slice_fusion.refs_0_), channel_id=1, source_target_pairs={{0,1},{1,0},{2,3},{3,2},{4,5},{5,4},{6,7},{7,6},{8,9},{9,8},{10,11... | collective-permute-start | bytes 2064392 | tf_op jit(solution)/shard_map/ppermute | solution.py:48
  24.5 37.0 %all-to-all-start = ((bf16[16,24,1152]{2,1,0:T(8,128)(2,1)}), bf16[16,24,1152]{2,1,0:T(8,128)(2,1)S(1)}, u32[]{:S(2)}, u32[]{:S(2)}) async-start(bf16[16,24,1152]{2,1,0:T(8,128)(2,1)} %bitcast.3), calls=%async_computation | async-start | bytes 1769472 | tf_op jit(solution)/shard_map/all_to_all | solution.py:434
  30.9 29.9 %collective-permute-start.5 = (bf16[384,896]{1,0:T(8,128)(2,1)S(1)}, bf16[384,896]{1,0:T(8,128)(2,1)}, u32[]{:S(2)}, u32[]{:S(2)}) collective-permute-start(bf16[384,896]{1,0:T(8,128)(2,1)S(1)} %constant_dynamic-update-slice_fusion.refs_0_), channel_id=1, source_target_pairs={{0,2},{1,3},{2,0},{3,1},{4,6},{5,7},{6,4},{7,5},{8,10},{9,11},{10,... | collective-permute-start | bytes 2064392 | tf_op jit(solution)/shard_map/ppermute | solution.py:48
  43.3 18.0 %collective-permute-start.6 = (bf16[384,896]{1,0:T(8,128)(2,1)}, bf16[384,896]{1,0:T(8,128)(2,1)S(1)}, u32[]{:S(2)}, u32[]{:S(2)}) collective-permute-start(bf16[384,896]{1,0:T(8,128)(2,1)} %collective-permute-done.4.refs_1_), channel_id=1, source_target_pairs={{0,2},{1,3},{2,0},{3,1},{4,6},{5,7},{6,4},{7,5},{8,10},{9,11},{10,... | collective-permute-start | bytes 2064392 | tf_op jit(solution)/shard_map/ppermute | solution.py:48
  43.4 6.0 %collective-permute-start.11 = (bf16[72,896]{1,0:T(8,128)(2,1)S(1)}, bf16[72,896]{1,0:T(8,128)(2,1)S(1)}, u32[]{:S(2)}, u32[]{:S(2)}) collective-permute-start(bf16[72,896]{1,0:T(8,128)(2,1)S(1)} %get-tuple-element.40), channel_id=1, source_target_pairs={{0,4},{1,5},{2,6},{3,7},{4,0},{5,1},{6,2},{7,3},{8,12},{9,13},{10,... | collective-permute-start | bytes 387080 | tf_op jit(solution)/shard_map/ppermute | solution.py:25
  45.4 15.3 %collective-permute-start.12 = (bf16[72,896]{1,0:T(8,128)(2,1)S(1)}, bf16[72,896]{1,0:T(8,128)(2,1)S(1)}, u32[]{:S(2)}, u32[]{:S(2)}) collective-permute-start(bf16[72,896]{1,0:T(8,128)(2,1)S(1)} %get-tuple-element.40), channel_id=1, source_target_pairs={{0,8},{1,9},{2,10},{3,11},{4,12},{5,13},{6,14},{7,15},{8,0},{9,1},... | collective-permute-start | bytes 387080 | tf_op jit(solution)/shard_map/ppermute | solution.py:25
  47.7 13.7 %collective-permute-start.13 = (bf16[72,896]{1,0:T(8,128)(2,1)S(1)}, bf16[72,896]{1,0:T(8,128)(2,1)S(1)}, u32[]{:S(2)}, u32[]{:S(2)}) collective-permute-start(bf16[72,896]{1,0:T(8,128)(2,1)S(1)} %get-tuple-element.40), channel_id=1, source_target_pairs={{0,12},{1,13},{2,14},{3,15},{4,8},{5,9},{6,10},{7,11},{8,4},{9,5},... | collective-permute-start | bytes 387080 | tf_op jit(solution)/shard_map/ppermute | solution.py:25
  49.4 19.5 %collective-permute-start.7 = (bf16[384,896]{1,0:T(8,128)(2,1)S(1)}, bf16[384,896]{1,0:T(8,128)(2,1)}, u32[]{:S(2)}, u32[]{:S(2)}) collective-permute-start(bf16[384,896]{1,0:T(8,128)(2,1)S(1)} %constant_dynamic-update-slice_fusion.refs_0_), channel_id=1, source_target_pairs={{0,16},{16,0},{1,17},{17,1},{2,18},{18,2},{3,19},{19,3},{4,20},{20... | collective-permute-start | bytes 2064392 | tf_op jit(solution)/shard_map/ppermute | solution.py:25
  60.8 9.7 %collective-permute-start.8 = (bf16[384,896]{1,0:T(8,128)(2,1)}, bf16[384,896]{1,0:T(8,128)(2,1)}, u32[]{:S(2)}, u32[]{:S(2)}) collective-permute-start(bf16[384,896]{1,0:T(8,128)(2,1)} %collective-permute-done.4.refs_1_), channel_id=1, source_target_pairs={{0,16},{16,0},{1,17},{17,1},{2,18},{18,2},{3,19},{19,3},{4,20},{20... | collective-permute-start | bytes 2064392 | tf_op jit(solution)/shard_map/ppermute | solution.py:25
  60.8 9.7 %collective-permute-start.9 = (bf16[384,896]{1,0:T(8,128)(2,1)}, bf16[384,896]{1,0:T(8,128)(2,1)}, u32[]{:S(2)}, u32[]{:S(2)}) collective-permute-start(bf16[384,896]{1,0:T(8,128)(2,1)} %collective-permute-done.5.refs_2_), channel_id=1, source_target_pairs={{0,16},{16,0},{1,17},{17,1},{2,18},{18,2},{3,19},{19,3},{4,20},{20... | collective-permute-start | bytes 2064392 | tf_op jit(solution)/shard_map/ppermute | solution.py:25
  61.3 9.5 %collective-permute-start.10 = (bf16[384,896]{1,0:T(8,128)(2,1)S(1)}, bf16[384,896]{1,0:T(8,128)(2,1)}, u32[]{:S(2)}, u32[]{:S(2)}) collective-permute-start(bf16[384,896]{1,0:T(8,128)(2,1)S(1)} %collective-permute-done.6.refs_3_), channel_id=1, source_target_pairs={{0,16},{16,0},{1,17},{17,1},{2,18},{18,2},{3,19},{19,3},{4,20},{20... | collective-permute-start | bytes 2064392 | tf_op jit(solution)/shard_map/ppermute | solution.py:25
  67.4 13.8 %collective-permute-start.14 = (bf16[288,896]{1,0:T(8,128)(2,1)S(1)}, bf16[288,896]{1,0:T(8,128)(2,1)S(1)}, u32[]{:S(2)}, u32[]{:S(2)}) collective-permute-start(bf16[288,896]{1,0:T(8,128)(2,1)S(1)} %pad_maximum_fusion.refs_1_), channel_id=1, source_target_pairs={{0,1},{1,0},{2,3},{3,2},{4,5},{5,4},{6,7},{7,6},{8,9},{9,8},{10,11... | collective-permute-start | bytes 1548296 | tf_op jit(solution)/shard_map/ppermute | solution.py:48
  69.0 16.8 %collective-permute-start.15 = (bf16[288,896]{1,0:T(8,128)(2,1)S(1)}, bf16[288,896]{1,0:T(8,128)(2,1)}, u32[]{:S(2)}, u32[]{:S(2)}) collective-permute-start(bf16[288,896]{1,0:T(8,128)(2,1)S(1)} %pad_maximum_fusion.refs_1_), channel_id=1, source_target_pairs={{0,2},{1,3},{2,0},{3,1},{4,6},{5,7},{6,4},{7,5},{8,10},{9,11},{10,... | collective-permute-start | bytes 1548296 | tf_op jit(solution)/shard_map/ppermute | solution.py:48
  70.5 22.1 %collective-permute-start.17 = (bf16[288,896]{1,0:T(8,128)(2,1)S(1)}, bf16[288,896]{1,0:T(8,128)(2,1)}, u32[]{:S(2)}, u32[]{:S(2)}) collective-permute-start(bf16[288,896]{1,0:T(8,128)(2,1)S(1)} %pad_maximum_fusion.refs_1_), channel_id=1, source_target_pairs={{0,16},{16,0},{1,17},{17,1},{2,18},{18,2},{3,19},{19,3},{4,20},{20... | collective-permute-start | bytes 1548296 | tf_op jit(solution)/shard_map/ppermute | solution.py:25
  70.5 11.2 %collective-permute-start.22 = (bf16[72,640]{1,0:T(8,128)(2,1)S(1)}, bf16[72,640]{1,0:T(8,128)(2,1)S(1)}, u32[]{:S(2)}, u32[]{:S(2)}) collective-permute-start(bf16[72,640]{1,0:T(8,128)(2,1)S(1)} %get-tuple-element.45), channel_id=1, source_target_pairs={{0,8},{1,9},{2,10},{3,11},{4,12},{5,13},{6,14},{7,15},{8,0},{9,1},... | collective-permute-start | bytes 276488 | tf_op jit(solution)/shard_map/ppermute | solution.py:25
  70.9 10.9 %collective-permute-start.23 = (bf16[72,640]{1,0:T(8,128)(2,1)S(1)}, bf16[72,640]{1,0:T(8,128)(2,1)S(1)}, u32[]{:S(2)}, u32[]{:S(2)}) collective-permute-start(bf16[72,640]{1,0:T(8,128)(2,1)S(1)} %get-tuple-element.45), channel_id=1, source_target_pairs={{0,12},{1,13},{2,14},{3,15},{4,8},{5,9},{6,10},{7,11},{8,4},{9,5},... | collective-permute-start | bytes 276488 | tf_op jit(solution)/shard_map/ppermute | solution.py:25
  81.2 12.1 %collective-permute-start.16 = (bf16[288,896]{1,0:T(8,128)(2,1)S(1)}, bf16[288,896]{1,0:T(8,128)(2,1)}, u32[]{:S(2)}, u32[]{:S(2)}) collective-permute-start(bf16[288,896]{1,0:T(8,128)(2,1)S(1)} %collective-permute-done.14.refs_2_), channel_id=1, source_target_pairs={{0,2},{1,3},{2,0},{3,1},{4,6},{5,7},{6,4},{7,5},{8,10},{9,11},{10,... | collective-permute-start | bytes 1548296 | tf_op jit(solution)/shard_map/ppermute | solution.py:48
  81.8 9.4 %collective-permute-start.24 = (bf16[288,640]{1,0:T(8,128)(2,1)S(1)}, bf16[288,640]{1,0:T(8,128)(2,1)}, u32[]{:S(2)}, u32[]{:S(2)}) collective-permute-start(bf16[288,640]{1,0:T(8,128)(2,1)S(1)} %constant_dynamic-update-slice_fusion.4.refs_0_), channel_id=1, source_target_pairs={{0,1},{1,0},{2,3},{3,2},{4,5},{5,4},{6,7},{7,6},{8,9},{9,8},{10,11... | collective-permute-start | bytes 1105928 | tf_op jit(solution)/shard_map/ppermute | solution.py:48
  85.7 19.9 %collective-permute-start.18 = (bf16[288,896]{1,0:T(8,128)(2,1)S(1)}, bf16[288,896]{1,0:T(8,128)(2,1)}, u32[]{:S(2)}, u32[]{:S(2)}) collective-permute-start(bf16[288,896]{1,0:T(8,128)(2,1)S(1)} %collective-permute-done.14.refs_2_), channel_id=1, source_target_pairs={{0,16},{16,0},{1,17},{17,1},{2,18},{18,2},{3,19},{19,3},{4,20},{20... | collective-permute-start | bytes 1548296 | tf_op jit(solution)/shard_map/ppermute | solution.py:25
  85.8 20.3 %collective-permute-start.19 = (bf16[288,896]{1,0:T(8,128)(2,1)}, bf16[288,896]{1,0:T(8,128)(2,1)}, u32[]{:S(2)}, u32[]{:S(2)}) collective-permute-start(bf16[288,896]{1,0:T(8,128)(2,1)} %collective-permute-done.15.refs_3_), channel_id=1, source_target_pairs={{0,16},{16,0},{1,17},{17,1},{2,18},{18,2},{3,19},{19,3},{4,20},{20... | collective-permute-start | bytes 1548296 | tf_op jit(solution)/shard_map/ppermute | solution.py:25
  86.2 32.2 %all-to-all-start.1 = ((bf16[16,24,288]{2,1,0:T(8,128)(2,1)}), bf16[16,24,288]{2,1,0:T(8,128)(2,1)S(1)}, u32[]{:S(2)}, u32[]{:S(2)}) async-start(bf16[16,24,288]{2,1,0:T(8,128)(2,1)} %bitcast.5), calls=%async_computation.1 | async-start | bytes 589824 | tf_op jit(solution)/shard_map/all_to_all | solution.py:459
  91.2 14.9 %collective-permute-start.25 = (bf16[288,640]{1,0:T(8,128)(2,1)S(1)}, bf16[288,640]{1,0:T(8,128)(2,1)}, u32[]{:S(2)}, u32[]{:S(2)}) collective-permute-start(bf16[288,640]{1,0:T(8,128)(2,1)S(1)} %constant_dynamic-update-slice_fusion.4.refs_0_), channel_id=1, source_target_pairs={{0,2},{1,3},{2,0},{3,1},{4,6},{5,7},{6,4},{7,5},{8,10},{9,11},{10,... | collective-permute-start | bytes 1105928 | tf_op jit(solution)/shard_map/ppermute | solution.py:48
  92.5 14.0 %collective-permute-start.26 = (bf16[288,640]{1,0:T(8,128)(2,1)}, bf16[288,640]{1,0:T(8,128)(2,1)}, u32[]{:S(2)}, u32[]{:S(2)}) collective-permute-start(bf16[288,640]{1,0:T(8,128)(2,1)} %collective-permute-done.24.refs_1_), channel_id=1, source_target_pairs={{0,2},{1,3},{2,0},{3,1},{4,6},{5,7},{6,4},{7,5},{8,10},{9,11},{10,... | collective-permute-start | bytes 1105928 | tf_op jit(solution)/shard_map/ppermute | solution.py:48
  93.3 13.4 %collective-permute-start.20 = (bf16[288,896]{1,0:T(8,128)(2,1)}, bf16[288,896]{1,0:T(8,128)(2,1)S(1)}, u32[]{:S(2)}, u32[]{:S(2)}) collective-permute-start(bf16[288,896]{1,0:T(8,128)(2,1)} %collective-permute-done.16.refs_4_), channel_id=1, source_target_pairs={{0,16},{16,0},{1,17},{17,1},{2,18},{18,2},{3,19},{19,3},{4,20},{20... | collective-permute-start | bytes 1548296 | tf_op jit(solution)/shard_map/ppermute | solution.py:25
  105.6 16.2 %collective-permute-start.27 = (bf16[288,640]{1,0:T(8,128)(2,1)S(1)}, bf16[288,640]{1,0:T(8,128)(2,1)S(1)}, u32[]{:S(2)}, u32[]{:S(2)}) collective-permute-start(bf16[288,640]{1,0:T(8,128)(2,1)S(1)} %constant_dynamic-update-slice_fusion.4.refs_0_), channel_id=1, source_target_pairs={{0,16},{16,0},{1,17},{17,1},{2,18},{18,2},{3,19},{19,3},{4,20},{20... | collective-permute-start | bytes 1105928 | tf_op jit(solution)/shard_map/ppermute | solution.py:25
  106.1 15.7 %collective-permute-start.28 = (bf16[288,640]{1,0:T(8,128)(2,1)}, bf16[288,640]{1,0:T(8,128)(2,1)S(1)}, u32[]{:S(2)}, u32[]{:S(2)}) collective-permute-start(bf16[288,640]{1,0:T(8,128)(2,1)} %collective-permute-done.24.refs_1_), channel_id=1, source_target_pairs={{0,16},{16,0},{1,17},{17,1},{2,18},{18,2},{3,19},{19,3},{4,20},{20... | collective-permute-start | bytes 1105928 | tf_op jit(solution)/shard_map/ppermute | solution.py:25
  106.1 15.6 %collective-permute-start.29 = (bf16[288,640]{1,0:T(8,128)(2,1)}, bf16[288,640]{1,0:T(8,128)(2,1)S(1)}, u32[]{:S(2)}, u32[]{:S(2)}) collective-permute-start(bf16[288,640]{1,0:T(8,128)(2,1)} %collective-permute-done.25.refs_2_), channel_id=1, source_target_pairs={{0,16},{16,0},{1,17},{17,1},{2,18},{18,2},{3,19},{19,3},{4,20},{20... | collective-permute-start | bytes 1105928 | tf_op jit(solution)/shard_map/ppermute | solution.py:25
  106.6 15.2 %collective-permute-start.30 = (bf16[288,640]{1,0:T(8,128)(2,1)}, bf16[288,640]{1,0:T(8,128)(2,1)}, u32[]{:S(2)}, u32[]{:S(2)}) collective-permute-start(bf16[288,640]{1,0:T(8,128)(2,1)} %collective-permute-done.26.refs_3_), channel_id=1, source_target_pairs={{0,16},{16,0},{1,17},{17,1},{2,18},{18,2},{3,19},{19,3},{4,20},{20... | collective-permute-start | bytes 1105928 | tf_op jit(solution)/shard_map/ppermute | solution.py:25
  (20 other events, 88.8 us)

commit v2 on v1

--- a/solution.py
+++ b/solution.py
@@ -29,13 +29,10 @@
     return lax.optimization_barrier((value, *before))[0]
 
 
-def tie_all(values, *before):
-    return lax.optimization_barrier((*values, *before))[: len(values)]
-
-
 def far_blocks(shard):
     size = lax.axis_size("tm")
-    return jnp.concatenate([shard] + [swap(shard, "tm", d) for d in range(4, size, 4)], axis=0)
+    parts = [swap(shard, "tm", d) for d in range(4, size, 4)]
+    return jnp.concatenate([shard] + parts, axis=0)
 
 
 def near_step(value, step):
@@ -92,20 +89,33 @@
         low, high = head * HD, (head + 1) * HD
         left = low // 128 * 128
         right = min(width, -(-high // 128) * 128)
+        spare = right - 1 - left if high < right else 0
         lane = lax.broadcasted_iota(jnp.int32, (1, right - left), 1) + left
         mine = (lane >= low) & (lane < high)
+        counts = lane == spare + left
         q = jnp.where(mine, query[:, left:right].astype(F32), 0.0).astype(BF16)
-        scores = [dot_t(q, k[:, left:right]) for k in keys]
+        scores = dot_t(q, jnp.concatenate([k[:, left:right] for k in keys], axis=0))
+        ends = [0]
+        for k in keys:
+            ends.append(ends[-1] + k.shape[0])
+        scores = [scores[:, a:b] for a, b in zip(ends[:-1], ends[1:])]
         scores = [s if m is None else jnp.where(m, s, DEAD) for s, m in zip(scores, masks)]
-        tops = [jnp.max(s, axis=-1, keepdims=True) for s in scores]
+        tops = [
+            functools.reduce(
+                jnp.maximum, [s[:, at : at + 128] for at in range(0, s.shape[1], 128)]
+            )
+            for s in scores
+        ]
         tops = [t if o is None else jnp.where(o < DEFINITE, t, DEAD) for t, o in zip(tops, offsets)]
-        top = functools.reduce(jnp.maximum, tops)
+        top = jnp.max(functools.reduce(jnp.maximum, tops), axis=-1, keepdims=True)
         expos = [
-            jnp.exp2((s - (top if o is None else top + o)) * scale) for s, o in zip(scores, offsets)
+            jnp.exp2((s - (top if o is None else top + o)) * scale).astype(BF16)
+            for s, o in zip(scores, offsets)
         ]
-        total = sum(jnp.sum(e, axis=-1, keepdims=True) for e in expos)
-        out = sum(dot(e.astype(BF16), v[:, left:right]) for e, v in zip(expos, values))
-        store(left, right, mine, out / total)
+        value = jnp.concatenate([v[:, left:right] for v in values], axis=0)
+        value = jnp.where(counts, 1.0, value.astype(F32)).astype(BF16)
+        out = dot(jnp.concatenate(expos, axis=1), value)
+        store(left, right, mine, out / out[:, spare : spare + 1])
 
 
 def keep_rows(half, ref, at, end, left, right, mine, result):
@@ -120,9 +130,19 @@
 
 
 def send_kernel(
-    half_ref, count_ref, valid_ref, qkv_ref, w_out_ref, box_ref, early_ref, cross_ref, closing_ref,
-    *, parts,
+    half_ref, count_ref, valid_ref, qkv_hbm, w_out_hbm, box_hbm, early_ref, cross_ref, closing_ref,
+    qkv_ref, w_out_ref, box_ref, sems, *, parts,
 ):
+    copies = [
+        pltpu.make_async_copy(a, b, sems.at[j])
+        for j, (a, b) in enumerate(
+            ((qkv_hbm, qkv_ref), (box_hbm, box_ref), (w_out_hbm, w_out_ref))
+        )
+    ]
+    for copy in copies:
+        copy.start()
+    for copy in copies:
+        copy.wait()
     cw, tw, bw = parts
     block, width = early_ref.shape
     rows, depth = w_out_ref.shape
@@ -159,15 +179,14 @@
 
 def order_kernel(tokens_ref, *refs, others):
     other_refs = refs[:others]
-    source_ref, wide_source_ref, out_ref, wide_ref, pick_ref = refs[others : others + 5]
-    out_refs = refs[others + 5 :]
+    source_ref, wide_source_ref, out_ref, wide_ref = refs[others : others + 4]
+    out_refs = refs[others + 4 :]
     depth = tokens_ref.shape[1]
     pick = chooser(depth, source_ref[...])
     out_ref[...] = dot(tokens_ref[...], pick).astype(BF16)
     for a, b in zip(other_refs, out_refs):
         b[...] = dot(a[...], pick).astype(BF16)
-    pick_ref[...] = chooser(depth, wide_source_ref[...])
-    wide_ref[...] = dot(tokens_ref[...], pick_ref[...]).astype(BF16)
+    wide_ref[...] = dot(tokens_ref[...], chooser(depth, wide_source_ref[...])).astype(BF16)
 
 
 def regroup(rows, positions):
@@ -177,10 +196,10 @@
     return (lax.broadcasted_iota(jnp.int32, (1, rows), 1) == source).astype(F32).astype(BF16)
 
 
-def widen_kernel(tokens_ref, pick_ref, wide_ref, *, positions):
+def widen_kernel(tokens_ref, source_ref, wide_ref, *, positions):
     tokens = tokens_ref[...]
     tokens = dot(regroup(tokens.shape[0], positions), tokens).astype(BF16)
-    wide_ref[...] = dot(tokens, pick_ref[...]).astype(BF16)
+    wide_ref[...] = dot(tokens, chooser(tokens.shape[1], source_ref[...])).astype(BF16)
 
 
 def load_halves(half_ref, piece_refs, scratch, sems, columns):
@@ -225,7 +244,7 @@
 
 
 def box_kernel(
-    half_ref, wide_ref, pick_ref, gate_ref, *refs, slots, blocks, skip
+    half_ref, wide_ref, source_ref, gate_ref, *refs, slots, blocks, skip
 ):
     piece_refs = refs[:8]
     out_ref, acc_ref, box_ref, flag_ref, weight_ref, carried_ref, sems, carried_sems = refs[8:]
@@ -265,7 +284,7 @@
     flags = dot(flag_ref[...].astype(BF16), spread_slots.astype(BF16))
     mine = lax.broadcasted_iota(jnp.int32, (blocks, blocks * slots), 0) == of_block
     live = jnp.sum(jnp.where(mine, flags, 0.0), axis=0, keepdims=True)
-    box = dot(box_ref[...].astype(BF16), pick_ref[...]).astype(BF16)
+    box = dot(box_ref[...].astype(BF16), chooser(depth, source_ref[...])).astype(BF16)
     for half in range(2):
         waits[half]()
         weights = weight_ref[half]
@@ -314,9 +333,12 @@
         out_ref[:, half * part : (half + 1) * part] = acc_ref[...].astype(BF16)
 
 
-def collect_kernel(half_ref, source_ref, cross_ref, time_ref, box_ref, out_ref):
+def final_kernel(half_ref, tokens_ref, source_ref, cross_ref, time_ref, box_ref, *refs):
+    piece_refs, (out_ref, weight_ref, sems) = refs[:8], refs[8:]
+    width = weight_ref.shape[2]
+    waits = load_halves(half_ref, piece_refs, weight_ref, sems, pl.ds(0, width))
     which = half_ref[0]
-    total = None
+    attn = None
     base = 0
     for ref in (cross_ref, time_ref, box_ref):
         part = ref.shape[1] // 2
@@ -324,34 +346,28 @@
             side = which if half == 0 else 1 - which
             pick = chooser(part, source_ref[...], base + side * part)
             term = dot(ref[:, half * part : (half + 1) * part], pick)
-            total = term if total is None else total + term
+            attn = term if attn is None else attn + term
         base += 2 * part
-    out_ref[...] = total.astype(BF16)
-
-
-def final_kernel(half_ref, tokens_ref, attn_ref, *refs):
-    piece_refs, (out_ref, weight_ref, sems) = refs[:8], refs[8:]
-    width = weight_ref.shape[2]
-    waits = load_halves(half_ref, piece_refs, weight_ref, sems, pl.ds(0, width))
+    attn = attn.astype(BF16)
     step = out_ref.shape[1] - width
     for half in range(2):
         waits[half]()
-        side = half_ref[0] if half == 0 else 1 - half_ref[0]
+        side = which if half == 0 else 1 - which
         at = pl.ds(pl.multiple_of(side * step, 128), width)
-        out_ref[:, at] = (tokens_ref[:, at].astype(F32) + dot(attn_ref[...], weight_ref[half])).astype(
-            BF16
-        )
-
-
-def call(kernel, outs, *args, scalars=0, scratch=(), pieces=(), name=None, vmem_mib=24, us=4):
+        out_ref[:, at] = (tokens_ref[:, at].astype(F32) + dot(attn, weight_ref[half])).astype(BF16)
+
+
+def call(
+    kernel, outs, *args, scalars=0, scratch=(), pieces=(), name=None, vmem_mib=24, us=4
+):
     vmem = pl.BlockSpec(memory_space=pltpu.VMEM)
     smem = pl.BlockSpec(memory_space=pltpu.SMEM)
-    anywhere = pl.BlockSpec(memory_space=pl.ANY)
+    hbm = pl.BlockSpec(memory_space=pltpu.HBM)
     single = not isinstance(outs, list)
     return pl.pallas_call(
         kernel,
         out_shape=outs if single else tuple(outs),
-        in_specs=[smem] * scalars + [vmem] * (len(args) - scalars) + [anywhere] * len(pieces),
+        in_specs=[smem] * scalars + [vmem] * (len(args) - scalars) + [hbm] * len(pieces),
         out_specs=vmem if single else tuple(vmem for _ in outs),
         scratch_shapes=list(scratch),
         compiler_params=pltpu.CompilerParams(vmem_limit_bytes=vmem_mib * 2**20),
@@ -391,8 +407,12 @@
     early, crossing, closing = call(
         functools.partial(send_kernel, parts=(cw, tw, bw)),
         [shaped(block, width), shaped(rows, cross_width), shaped(rows, out_width)],
-        which, box_count, frame_valid, w_qkv, w_out, boxes,
-        scalars=3, name="send", us=2,
+        which, box_count, frame_valid,
+        scalars=3,
+        pieces=(w_qkv, w_out, boxes),
+        scratch=[pltpu.VMEM(x.shape, BF16) for x in (w_qkv, w_out, boxes)]
+        + [pltpu.SemaphoreType.DMA((3,))],
+        name="send", us=2,
     )
 
     if cameras == 2:
@@ -409,41 +429,41 @@
     wide_source = jnp.full((size, block), -1, jnp.int32)
     wide_source = wide_source.at[:, 24:used].set(source.reshape(size, rows)).reshape(1, -1)
 
-    ordered, wide, pick, *ordered_others = call(
+    def near_blocks(far, *before):
+        one = near_step(far, 0)
+        two = near_step(far, 1)
+        return far, one, two, near_step(tie(one, *before), 1)
+
+    def with_other_core(blocks):
+        return (*blocks, *(swap(b, "view", 1) for b in blocks))
+
+    def weight_scratch(far_rows, columns):
+        return [pltpu.VMEM((2, 4 * far_rows, columns), BF16), pltpu.SemaphoreType.DMA((2, 4))]
+
+    early_far = far_blocks(early)
+    early_one, early_two = near_step(early_far, 0), near_step(early_far, 1)
+    crossing_far = far_blocks(tie(crossing, early_far))
+    positions = count // size
+    token_slices = lax.all_to_all(
+        tie(tokens, early_far).reshape(size, positions, depth),
+        "tm", split_axis=0, concat_axis=0, tiled=True,
+    ).reshape(count, depth)
+    ordered, wide, *ordered_others = call(
         functools.partial(order_kernel, others=len(others)),
-        [shaped(count, depth), shaped(count, size * block), shaped(depth, size * block)]
+        [shaped(count, depth), shaped(count, size * block)]
         + [shaped(count, depth) for _ in others],
         tokens, *others, source, wide_source,
         name="order", us=6,
     )
 
-    def near_blocks(far, *before):
-        one = near_step(far, 0)
-        two = near_step(far, 1)
-        return far, one, two, near_step(tie(one, *before) if before else one, 1)
-
-    def with_other_core(blocks):
-        return (*blocks, *(swap(b, "view", 1) for b in blocks))
-
-    def weight_scratch(far_rows, columns):
-        return [pltpu.VMEM((2, 4 * far_rows, columns), BF16), pltpu.SemaphoreType.DMA((2, 4))]
-
-    early = far_blocks(early)
-    crossing = far_blocks(tie(crossing, early))
-    positions = count // size
-    token_slices = lax.all_to_all(
-        tie(tokens, early).reshape(size, positions, depth),
-        "tm", split_axis=0, concat_axis=0, tiled=True,
-    ).reshape(count, depth)
-    early = near_blocks(early, ordered)
+    early_near = early_far, early_one, early_two, near_step(tie(early_one, ordered), 1)
     wide_slices = call(
         functools.partial(widen_kernel, positions=positions),
-        shaped(count, size * block), token_slices, pick, name="widen", us=2,
-    )
-    closing = far_blocks(tie(closing, token_slices))
-    early_rows = early[0].shape[0]
-    early_near = early
-    early = with_other_core(early)
+        shaped(count, size * block), token_slices, wide_source, name="widen", us=2,
+    )
+    closing_far = far_blocks(tie(closing, token_slices))
+    early_rows = early_far.shape[0]
+    early = with_other_core(early_near)
     timed = call(
         functools.partial(time_kernel, positions=positions),
         shaped(count, 2 * tw),
@@ -455,18 +475,16 @@
         name="timed", us=5,
     )
     timed_here = timed
-    crossing = near_blocks(tie(crossing, early_near[1], early_near[2]), timed_here)
+    crossing = near_blocks(tie(crossing_far, early_one, early_two), timed_here)
     timed = lax.all_to_all(
         timed.reshape(size, positions, 2 * tw), "tm", split_axis=0, concat_axis=0, tiled=True
     ).reshape(count, 2 * tw)
-    closing = near_blocks(closing, timed_here)
-    link_counts = tie(link_counts, timed_here)
     gates = box_gate.reshape(2, bw)
     gates = jnp.where(half == 0, gates, gates[::-1])
     boxed = call(
         functools.partial(box_kernel, slots=slots, blocks=size, skip=3 * tw),
         shaped(count, 2 * bw),
-        which, wide, pick, gates,
+        which, wide, wide_source, gates,
         scalars=1,
         pieces=early,
         scratch=[
@@ -478,28 +496,25 @@
             *weight_scratch(early_rows, width)[1:],
             pltpu.SemaphoreType.DMA((4,)),
         ],
-        name="boxed", us=7,
-    )
+        name="boxed", us=7, vmem_mib=16 + size // 2,
+    )
+    closing = near_blocks(closing_far, timed_here)
     cross_rows = crossing[0].shape[0]
     cross = call(
         functools.partial(cross_kernel, others=len(others)),
         shaped(count, 2 * cw),
-        which, link_counts, ordered, *ordered_others,
+        which, tie(link_counts, timed_here), ordered, *ordered_others,
         scalars=2,
         pieces=with_other_core(crossing),
         scratch=[pltpu.VMEM((count, cw), F32)] + weight_scratch(cross_rows, cross_width),
         name="cross", us=9,
     )
-    attn = call(
-        collect_kernel, shaped(count, depth), which, source, cross, timed, boxed,
-        scalars=1, name="collect", us=2,
-    )
     result = call(
-        final_kernel, shaped(count, depth), which, tokens, attn,
+        final_kernel, shaped(count, depth), which, tokens, source, cross, timed, boxed,
         scalars=1,
         pieces=with_other_core(closing),
         scratch=weight_scratch(closing[0].shape[0], out_width),
-        name="final", us=4,
+        name="final", us=5,
     )
     return result.reshape(frames_x.shape)
 

time: 128 us -> 127 us (level)
  local copies, waits for them, and re-layouts: 16.3 us -> 11.8 us
  starting transfers between devices: 39.3 us -> 42.2 us
    unnamed x44 -> x42, local copies, waits for them, and re-layouts: 15.3 us -> 10.8 us
    ppermute x22, starting transfers between devices: 17.7 us -> 21.6 us  [swap(): return lax.ppermute(value, axis, [(i, i ^ by) for i in range(size)])]
    pallas_call x8 -> x7, Pallas kernels: 41.1 us -> 40.4 us  [call(): pl.pallas_call(kernel, out_shape=outs if single else tuple(outs), in_spec...]
  transfers between devices with their start and end apart: 33 -> 33, of which waited for: 6 -> 7; matrix products, arithmetic and copies ran while one was open for 1% -> 1% of each run, Pallas kernels for 28% -> 25%
where the time goes in v2:
time: 127 us; the launch traced here: 126 us
  starting transfers between devices  42.2 us (33%)
  Pallas kernels  40.4 us (32%)
  waiting for transfers between devices  28.9 us (23%)
  local copies, waits for them, and re-layouts  11.8 us (9%)
  between operations  3.05 us (2%)
    pallas_call x7, Pallas kernels, call(): pl.pallas_call(kernel, out_shape=outs if single else tuple(outs), in_spec...  40.4 us
    ppermute x22, waiting for transfers between devices, swap(): return lax.ppermute(value, axis, [(i, i ^ by) for i in range(size)])  25 us
    ppermute x22, starting transfers between devices, swap(): return lax.ppermute(value, axis, [(i, i ^ by) for i in range(size)])  21.6 us
    unnamed x42, local copies, waits for them, and re-layouts  10.8 us
    ppermute x9, starting transfers between devices, near_step(): return lax.ppermute(value, ('view', 'tm'), pairs)  10.7 us
    all_to_all x1, starting transfers between devices, per_device(): lax.all_to_all(tie(tokens, early_far).reshape(size, positions, depth), 't...  6.14 us
    ppermute x9, waiting for transfers between devices, near_step(): return lax.ppermute(value, ('view', 'tm'), pairs)  3.91 us
    all_to_all x1, starting transfers between devices, per_device(): lax.all_to_all(timed.reshape(size, positions, 2 * tw), 'tm', split_axis=0...  3.72 us
  transfers between devices with their start and end apart: 33, of which 7 were waited for; matrix products, arithmetic and copies ran while one was open for 1% of the time, Pallas kernels for 25%

profile of v2, /device:TPU:0, one launch (start us, length us, event | category | flops | bytes accessed | tf_op | source)
XLA Modules:
  0.0 126.5 jit_solution(12881569056614214198)
XLA Ops:
  1.3 1.0 copy-done
  4.8 3.1 %collective-permute-start = (bf16[96,896]{1,0:T(8,128)(2,1)S(1)}, bf16[96,896]{1,0:T(8,128)(2,1)S(1)}, u32[]{:S(2)}, u32[]{:S(2)}) collective-permute-start(bf16[96,896]{1,0:T(8,128)(2,1)S(1)} %get-tuple-element.31), channel_id=1, source_target_pairs={{0,4},{1,5},{2,6},{3,7},{4,0},{5,1},{6,2},{7,3},{8,12},{9,13},{10,... | collective-permute-start | bytes 516104 | tf_op jit(solution)/shard_map/ppermute | solution.py:25
  7.9 2.6 %collective-permute-start.1 = (bf16[96,896]{1,0:T(8,128)(2,1)S(1)}, bf16[96,896]{1,0:T(8,128)(2,1)S(1)}, u32[]{:S(2)}, u32[]{:S(2)}) collective-permute-start(bf16[96,896]{1,0:T(8,128)(2,1)S(1)} %get-tuple-element.31), channel_id=1, source_target_pairs={{0,8},{1,9},{2,10},{3,11},{4,12},{5,13},{6,14},{7,15},{8,0},{9,1},... | collective-permute-start | bytes 516104 | tf_op jit(solution)/shard_map/ppermute | solution.py:25
  10.5 4.5 %collective-permute-done = bf16[96,896]{1,0:T(8,128)(2,1)S(1)} collective-permute-done((bf16[96,896]{1,0:T(8,128)(2,1)S(1)}, bf16[96,896]{1,0:T(8,128)(2,1)S(1)}, u32[]{:S(2)}, u32[]{:S(2)}) %collective-permute-start) | collective-permute-done | bytes 172064 | tf_op jit(solution)/shard_map/ppermute | solution.py:25
  15.0 8.5 %collective-permute-done.1 = bf16[96,896]{1,0:T(8,128)(2,1)S(1)} collective-permute-done((bf16[96,896]{1,0:T(8,128)(2,1)S(1)}, bf16[96,896]{1,0:T(8,128)(2,1)S(1)}, u32[]{:S(2)}, u32[]{:S(2)}) %collective-permute-start.1) | collective-permute-done | bytes 172064 | tf_op jit(solution)/shard_map/ppermute | solution.py:25
  23.5 1.6 %collective-permute-start.3 = (bf16[384,896]{1,0:T(8,128)(2,1)S(1)}, bf16[384,896]{1,0:T(8,128)(2,1)}, u32[]{:S(2)}, u32[]{:S(2)}) collective-permute-start(bf16[384,896]{1,0:T(8,128)(2,1)S(1)} %constant_dynamic-update-slice_fusion.refs_0_), channel_id=1, source_target_pairs={{0,1},{1,0},{2,3},{3,2},{4,5},{5,4},{6,7},{7,6},{8,9},{9,8},{10,11... | collective-permute-start | bytes 2064392 | tf_op jit(solution)/shard_map/ppermute | solution.py:45
  25.1 6.1 %all-to-all-start = ((bf16[16,24,1152]{2,1,0:T(8,128)(2,1)}), bf16[16,24,1152]{2,1,0:T(8,128)(2,1)S(1)}, u32[]{:S(2)}, u32[]{:S(2)}) async-start(bf16[16,24,1152]{2,1,0:T(8,128)(2,1)} %bitcast.3), calls=%async_computation | async-start | bytes 1769472 | tf_op jit(solution)/shard_map/all_to_all | solution.py:447
  31.6 2.0 %collective-permute-start.4 = (bf16[384,896]{1,0:T(8,128)(2,1)S(1)}, bf16[384,896]{1,0:T(8,128)(2,1)}, u32[]{:S(2)}, u32[]{:S(2)}) collective-permute-start(bf16[384,896]{1,0:T(8,128)(2,1)S(1)} %constant_dynamic-update-slice_fusion.refs_0_), channel_id=1, source_target_pairs={{0,2},{1,3},{2,0},{3,1},{4,6},{5,7},{6,4},{7,5},{8,10},{9,11},{10,... | collective-permute-start | bytes 2064392 | tf_op jit(solution)/shard_map/ppermute | solution.py:45
  33.5 5.6 %order.1 = (bf16[384,1152]{1,0:T(8,128)(2,1)S(1)}, bf16[384,1536]{1,0:T(8,128)(2,1)S(1)}, bf16[384,1152]{1,0:T(8,128)(2,1)S(1)}) custom-call(bf16[384,1152]{1,0:T(8,128)(2,1)} %bitcast.1.tokens_ref, bf16[384,1152]{1,0:T(8,128)(2,1)S(1)} %collective-permute-done.5.refs_0_, s32[1,1152]{1,0:T(1,128)S(1)} %add.38.refs_1_.source_ref, ...), custom_call_target="tpu_custom_call" | custom-call | flops 6600000000 | bytes 21600000 | tf_op jit(solution)/shard_map/order/pallas_call | solution.py:367
  39.2 1.1 copy-done.5
  42.2 3.9 %collective-permute-start.11 = (bf16[72,896]{1,0:T(8,128)(2,1)S(1)}, bf16[72,896]{1,0:T(8,128)(2,1)S(1)}, u32[]{:S(2)}, u32[]{:S(2)}) collective-permute-start(bf16[72,896]{1,0:T(8,128)(2,1)S(1)} %get-tuple-element.38), channel_id=1, source_target_pairs={{0,4},{1,5},{2,6},{3,7},{4,0},{5,1},{6,2},{7,3},{8,12},{9,13},{10,... | collective-permute-start | bytes 387080 | tf_op jit(solution)/shard_map/ppermute | solution.py:25
  46.1 2.9 %collective-permute-start.12 = (bf16[72,896]{1,0:T(8,128)(2,1)S(1)}, bf16[72,896]{1,0:T(8,128)(2,1)S(1)}, u32[]{:S(2)}, u32[]{:S(2)}) collective-permute-start(bf16[72,896]{1,0:T(8,128)(2,1)S(1)} %get-tuple-element.38), channel_id=1, source_target_pairs={{0,8},{1,9},{2,10},{3,11},{4,12},{5,13},{6,14},{7,15},{8,0},{9,1},... | collective-permute-start | bytes 387080 | tf_op jit(solution)/shard_map/ppermute | solution.py:25
  49.0 1.5 %collective-permute-start.13 = (bf16[72,896]{1,0:T(8,128)(2,1)S(1)}, bf16[72,896]{1,0:T(8,128)(2,1)S(1)}, u32[]{:S(2)}, u32[]{:S(2)}) collective-permute-start(bf16[72,896]{1,0:T(8,128)(2,1)S(1)} %get-tuple-element.38), channel_id=1, source_target_pairs={{0,12},{1,13},{2,14},{3,15},{4,8},{5,9},{6,10},{7,11},{8,4},{9,5},... | collective-permute-start | bytes 387080 | tf_op jit(solution)/shard_map/ppermute | solution.py:25
  50.5 10.9 %collective-permute-done.12 = bf16[72,896]{1,0:T(8,128)(2,1)S(1)} collective-permute-done((bf16[72,896]{1,0:T(8,128)(2,1)S(1)}, bf16[72,896]{1,0:T(8,128)(2,1)S(1)}, u32[]{:S(2)}, u32[]{:S(2)}) %collective-permute-start.12) | collective-permute-done | bytes 129056 | tf_op jit(solution)/shard_map/ppermute | solution.py:25
  62.1 1.7 %collective-permute-start.21 = (bf16[72,640]{1,0:T(8,128)(2,1)S(1)}, bf16[72,640]{1,0:T(8,128)(2,1)S(1)}, u32[]{:S(2)}, u32[]{:S(2)}) collective-permute-start(bf16[72,640]{1,0:T(8,128)(2,1)S(1)} %get-tuple-element.43), channel_id=1, source_target_pairs={{0,4},{1,5},{2,6},{3,7},{4,0},{5,1},{6,2},{7,3},{8,12},{9,13},{10,... | collective-permute-start | bytes 276488 | tf_op jit(solution)/shard_map/ppermute | solution.py:25
  63.8 2.2 %widen.1.wide_ref = bf16[384,1536]{1,0:T(8,128)(2,1)S(1)} custom-call(bf16[384,1152]{1,0:T(8,128)(2,1)S(1)} %bitcast.8, s32[1,1536]{1,0:T(1,128)S(1)} %reshape.86.source_ref.refs_2_), custom_call_target="tpu_custom_call" | custom-call | flops 2200000000 | bytes 7200000 | tf_op jit(solution)/shard_map/widen/pallas_call | solution.py:367
  66.1 1.1 collective-permute-done.21
  67.1 1.5 %collective-permute-start.14 = (bf16[288,896]{1,0:T(8,128)(2,1)S(1)}, bf16[288,896]{1,0:T(8,128)(2,1)S(1)}, u32[]{:S(2)}, u32[]{:S(2)}) collective-permute-start(bf16[288,896]{1,0:T(8,128)(2,1)S(1)} %pad_maximum_fusion.refs_1_), channel_id=1, source_target_pairs={{0,1},{1,0},{2,3},{3,2},{4,5},{5,4},{6,7},{7,6},{8,9},{9,8},{10,11... | collective-permute-start | bytes 1548296 | tf_op jit(solution)/shard_map/ppermute | solution.py:45
  68.6 1.5 %collective-permute-start.15 = (bf16[288,896]{1,0:T(8,128)(2,1)S(1)}, bf16[288,896]{1,0:T(8,128)(2,1)}, u32[]{:S(2)}, u32[]{:S(2)}) collective-permute-start(bf16[288,896]{1,0:T(8,128)(2,1)S(1)} %pad_maximum_fusion.refs_1_), channel_id=1, source_target_pairs={{0,2},{1,3},{2,0},{3,1},{4,6},{5,7},{6,4},{7,5},{8,10},{9,11},{10,... | collective-permute-start | bytes 1548296 | tf_op jit(solution)/shard_map/ppermute | solution.py:45
  70.2 1.3 %collective-permute-start.22 = (bf16[72,640]{1,0:T(8,128)(2,1)S(1)}, bf16[72,640]{1,0:T(8,128)(2,1)S(1)}, u32[]{:S(2)}, u32[]{:S(2)}) collective-permute-start(bf16[72,640]{1,0:T(8,128)(2,1)S(1)} %get-tuple-element.43), channel_id=1, source_target_pairs={{0,8},{1,9},{2,10},{3,11},{4,12},{5,13},{6,14},{7,15},{8,0},{9,1},... | collective-permute-start | bytes 276488 | tf_op jit(solution)/shard_map/ppermute | solution.py:25
  71.5 2.4 %collective-permute-start.23 = (bf16[72,640]{1,0:T(8,128)(2,1)S(1)}, bf16[72,640]{1,0:T(8,128)(2,1)S(1)}, u32[]{:S(2)}, u32[]{:S(2)}) collective-permute-start(bf16[72,640]{1,0:T(8,128)(2,1)S(1)} %get-tuple-element.43), channel_id=1, source_target_pairs={{0,12},{1,13},{2,14},{3,15},{4,8},{5,9},{6,10},{7,11},{8,4},{9,5},... | collective-permute-start | bytes 276488 | tf_op jit(solution)/shard_map/ppermute | solution.py:25
  73.8 6.0 %timed.1 = bf16[384,288]{1,0:T(8,128)(2,1)} custom-call(s32[1]{0:T(128)} %bitcast.half_ref, bf16[384,1536]{1,0:T(8,128)(2,1)S(1)} %widen.1.wide_ref, bf16[384,896]{1,0:T(8,128)(2,1)S(1)} %constant_dynamic-update-slice_fusion.refs_0_, bf16[384,896]{1,0:T(8,128)(2,1)} %collective-permute-done.3.refs_1_, bf16[384,896]{1,0:T(8,128)(2,1)} %collective-permute-done.4.refs_2_, ...), custom_call_target="tpu_custom_call" | custom-call | flops 5500000256 | bytes 18000000 | tf_op jit(solution)/shard_map/timed/pallas_call | solution.py:367
  79.9 1.9 %collective-permute-done.14.refs_2_ = bf16[288,896]{1,0:T(8,128)(2,1)S(1)} collective-permute-done((bf16[288,896]{1,0:T(8,128)(2,1)S(1)}, bf16[288,896]{1,0:T(8,128)(2,1)S(1)}, u32[]{:S(2)}, u32[]{:S(2)}) %collective-permute-start.14) | collective-permute-done | bytes 516128 | tf_op jit(solution)/shard_map/ppermute | solution.py:45
  82.4 1.5 %collective-permute-start.24 = (bf16[288,640]{1,0:T(8,128)(2,1)S(1)}, bf16[288,640]{1,0:T(8,128)(2,1)}, u32[]{:S(2)}, u32[]{:S(2)}) collective-permute-start(bf16[288,640]{1,0:T(8,128)(2,1)S(1)} %constant_dynamic-update-slice_fusion.4.refs_0_), channel_id=1, source_target_pairs={{0,1},{1,0},{2,3},{3,2},{4,5},{5,4},{6,7},{7,6},{8,9},{9,8},{10,11... | collective-permute-start | bytes 1105928 | tf_op jit(solution)/shard_map/ppermute | solution.py:45
  86.5 3.7 %all-to-all-start.1 = ((bf16[16,24,288]{2,1,0:T(8,128)(2,1)}), bf16[16,24,288]{2,1,0:T(8,128)(2,1)S(1)}, u32[]{:S(2)}, u32[]{:S(2)}) async-start(bf16[16,24,288]{2,1,0:T(8,128)(2,1)} %bitcast.5), calls=%async_computation.1 | async-start | bytes 589824 | tf_op jit(solution)/shard_map/all_to_all | solution.py:479
  90.2 1.8 %collective-permute-done.24.refs_1_ = bf16[288,640]{1,0:T(8,128)(2,1)} collective-permute-done((bf16[288,640]{1,0:T(8,128)(2,1)S(1)}, bf16[288,640]{1,0:T(8,128)(2,1)}, u32[]{:S(2)}, u32[]{:S(2)}) %collective-permute-start.24) | collective-permute-done | bytes 368672 | tf_op jit(solution)/shard_map/ppermute | solution.py:45
  92.6 1.5 %collective-permute-start.26 = (bf16[288,640]{1,0:T(8,128)(2,1)}, bf16[288,640]{1,0:T(8,128)(2,1)}, u32[]{:S(2)}, u32[]{:S(2)}) collective-permute-start(bf16[288,640]{1,0:T(8,128)(2,1)} %collective-permute-done.24.refs_1_), channel_id=1, source_target_pairs={{0,2},{1,3},{2,0},{3,1},{4,6},{5,7},{6,4},{7,5},{8,10},{9,11},{10,... | collective-permute-start | bytes 1105928 | tf_op jit(solution)/shard_map/ppermute | solution.py:45
  94.0 1.3 %copy-done.6 = bf16[384,1536]{1,0:T(8,128)(2,1)S(1)} copy-done((bf16[384,1536]{1,0:T(8,128)(2,1)S(1)}, bf16[384,1536]{1,0:T(8,128)(2,1)}, u32[]{:S(2)}) %copy-start.6) | copy-done | bytes 1179672
  95.3 8.4 %boxed.1.box_ref = bf16[384,288]{1,0:T(8,128)(2,1)S(1)} custom-call(s32[1]{0:T(128)} %bitcast.half_ref, bf16[384,1536]{1,0:T(8,128)(2,1)S(1)} %copy-done.6, s32[1,1536]{1,0:T(1,128)S(1)} %reshape.86.source_ref.refs_2_, f32[2,144]{1,0:T(2,128)S(1)} %broadcast_select_fusion.gate_ref, bf16[384,896]{1,0:T(8,128)(2,1)S(1)} %constant_dynamic-update-slice_fusion.refs_0_, ...), custom_call_target="tpu_custom_call" | custom-call | flops 7699999744 | bytes 25200000 | tf_op jit(solution)/shard_map/boxed/pallas_call | solution.py:367
  105.1 9.7 %cross.1.cross_ref = bf16[384,576]{1,0:T(8,128)(2,1)S(1)} custom-call(s32[1]{0:T(128)} %bitcast.half_ref, f32[1,1]{1,0:T(1,128)S(6)} %convert_element_type.3.count_ref, bf16[384,1152]{1,0:T(8,128)(2,1)S(1)} %copy-done.10, bf16[384,1152]{1,0:T(8,128)(2,1)S(1)} %copy-done.12, bf16[288,896]{1,0:T(8,128)(2,1)S(1)} %pad_maximum_fusion.refs_1_, ...), custom_call_target="tpu_custom_call" | custom-call | flops 9900000256 | bytes 32400000 | tf_op jit(solution)/shard_map/cross/pallas_call | solution.py:367
  116.6 1.0 copy-done.8
  118.6 7.7 %final.1 = bf16[384,1152]{1,0:T(8,128)(2,1)} custom-call(s32[1]{0:T(128)} %bitcast.half_ref, bf16[384,1152]{1,0:T(8,128)(2,1)} %bitcast.1.tokens_ref, s32[1,1152]{1,0:T(1,128)S(1)} %add.38.refs_1_.source_ref, bf16[384,576]{1,0:T(8,128)(2,1)S(1)} %copy-done.8, bf16[384,288]{1,0:T(8,128)(2,1)S(1)} %bitcast.9, bf16[384,288]{1,0:T(8,128)(2,1)S(1)} %copy-done.14, ...), custom_call_target="tpu_custom_call" | custom-call | flops 5500000256 | bytes 18000000 | tf_op jit(solution)/shard_map/final/pallas_call | solution.py:367
  (95 shorter events, 12.0 us)
Async XLA Ops:
  4.8 10.2 %collective-permute-start = (bf16[96,896]{1,0:T(8,128)(2,1)S(1)}, bf16[96,896]{1,0:T(8,128)(2,1)S(1)}, u32[]{:S(2)}, u32[]{:S(2)}) collective-permute-start(bf16[96,896]{1,0:T(8,128)(2,1)S(1)} %get-tuple-element.31), channel_id=1, source_target_pairs={{0,4},{1,5},{2,6},{3,7},{4,0},{5,1},{6,2},{7,3},{8,12},{9,13},{10,... | collective-permute-start | bytes 516104 | tf_op jit(solution)/shard_map/ppermute | solution.py:25
  7.9 15.6 %collective-permute-start.1 = (bf16[96,896]{1,0:T(8,128)(2,1)S(1)}, bf16[96,896]{1,0:T(8,128)(2,1)S(1)}, u32[]{:S(2)}, u32[]{:S(2)}) collective-permute-start(bf16[96,896]{1,0:T(8,128)(2,1)S(1)} %get-tuple-element.31), channel_id=1, source_target_pairs={{0,8},{1,9},{2,10},{3,11},{4,12},{5,13},{6,14},{7,15},{8,0},{9,1},... | collective-permute-start | bytes 516104 | tf_op jit(solution)/shard_map/ppermute | solution.py:25
  10.5 13.0 %collective-permute-start.2 = (bf16[96,896]{1,0:T(8,128)(2,1)S(1)}, bf16[96,896]{1,0:T(8,128)(2,1)S(1)}, u32[]{:S(2)}, u32[]{:S(2)}) collective-permute-start(bf16[96,896]{1,0:T(8,128)(2,1)S(1)} %get-tuple-element.31), channel_id=1, source_target_pairs={{0,12},{1,13},{2,14},{3,15},{4,8},{5,9},{6,10},{7,11},{8,4},{9,5},... | collective-permute-start | bytes 516104 | tf_op jit(solution)/shard_map/ppermute | solution.py:25
  10.5 23.0 %collective-permute-start.5 = (bf16[384,1152]{1,0:T(8,128)(2,1)}, bf16[384,1152]{1,0:T(8,128)(2,1)S(1)}, u32[]{:S(2)}, u32[]{:S(2)}) collective-permute-start(bf16[384,1152]{1,0:T(8,128)(2,1)} %bitcast.1.tokens_ref), channel_id=1, source_target_pairs={{0,16},{16,0},{1,17},{17,1},{2,18},{18,2},{3,19},{19,3},{4,20},{20... | collective-permute-start | bytes 2654216 | tf_op jit(solution)/shard_map/ppermute | solution.py:25
  23.5 18.6 %collective-permute-start.3 = (bf16[384,896]{1,0:T(8,128)(2,1)S(1)}, bf16[384,896]{1,0:T(8,128)(2,1)}, u32[]{:S(2)}, u32[]{:S(2)}) collective-permute-start(bf16[384,896]{1,0:T(8,128)(2,1)S(1)} %constant_dynamic-update-slice_fusion.refs_0_), channel_id=1, source_target_pairs={{0,1},{1,0},{2,3},{3,2},{4,5},{5,4},{6,7},{7,6},{8,9},{9,8},{10,11... | collective-permute-start | bytes 2064392 | tf_op jit(solution)/shard_map/ppermute | solution.py:45
  25.1 37.0 %all-to-all-start = ((bf16[16,24,1152]{2,1,0:T(8,128)(2,1)}), bf16[16,24,1152]{2,1,0:T(8,128)(2,1)S(1)}, u32[]{:S(2)}, u32[]{:S(2)}) async-start(bf16[16,24,1152]{2,1,0:T(8,128)(2,1)} %bitcast.3), calls=%async_computation | async-start | bytes 1769472 | tf_op jit(solution)/shard_map/all_to_all | solution.py:447
  31.6 29.9 %collective-permute-start.4 = (bf16[384,896]{1,0:T(8,128)(2,1)S(1)}, bf16[384,896]{1,0:T(8,128)(2,1)}, u32[]{:S(2)}, u32[]{:S(2)}) collective-permute-start(bf16[384,896]{1,0:T(8,128)(2,1)S(1)} %constant_dynamic-update-slice_fusion.refs_0_), channel_id=1, source_target_pairs={{0,2},{1,3},{2,0},{3,1},{4,6},{5,7},{6,4},{7,5},{8,10},{9,11},{10,... | collective-permute-start | bytes 2064392 | tf_op jit(solution)/shard_map/ppermute | solution.py:45
  42.1 19.9 %collective-permute-start.6 = (bf16[384,896]{1,0:T(8,128)(2,1)}, bf16[384,896]{1,0:T(8,128)(2,1)S(1)}, u32[]{:S(2)}, u32[]{:S(2)}) collective-permute-start(bf16[384,896]{1,0:T(8,128)(2,1)} %collective-permute-done.3.refs_1_), channel_id=1, source_target_pairs={{0,2},{1,3},{2,0},{3,1},{4,6},{5,7},{6,4},{7,5},{8,10},{9,11},{10,... | collective-permute-start | bytes 2064392 | tf_op jit(solution)/shard_map/ppermute | solution.py:45
  42.2 8.3 %collective-permute-start.11 = (bf16[72,896]{1,0:T(8,128)(2,1)S(1)}, bf16[72,896]{1,0:T(8,128)(2,1)S(1)}, u32[]{:S(2)}, u32[]{:S(2)}) collective-permute-start(bf16[72,896]{1,0:T(8,128)(2,1)S(1)} %get-tuple-element.38), channel_id=1, source_target_pairs={{0,4},{1,5},{2,6},{3,7},{4,0},{5,1},{6,2},{7,3},{8,12},{9,13},{10,... | collective-permute-start | bytes 387080 | tf_op jit(solution)/shard_map/ppermute | solution.py:25
  46.1 15.3 %collective-permute-start.12 = (bf16[72,896]{1,0:T(8,128)(2,1)S(1)}, bf16[72,896]{1,0:T(8,128)(2,1)S(1)}, u32[]{:S(2)}, u32[]{:S(2)}) collective-permute-start(bf16[72,896]{1,0:T(8,128)(2,1)S(1)} %get-tuple-element.38), channel_id=1, source_target_pairs={{0,8},{1,9},{2,10},{3,11},{4,12},{5,13},{6,14},{7,15},{8,0},{9,1},... | collective-permute-start | bytes 387080 | tf_op jit(solution)/shard_map/ppermute | solution.py:25
  49.0 13.0 %collective-permute-start.13 = (bf16[72,896]{1,0:T(8,128)(2,1)S(1)}, bf16[72,896]{1,0:T(8,128)(2,1)S(1)}, u32[]{:S(2)}, u32[]{:S(2)}) collective-permute-start(bf16[72,896]{1,0:T(8,128)(2,1)S(1)} %get-tuple-element.38), channel_id=1, source_target_pairs={{0,12},{1,13},{2,14},{3,15},{4,8},{5,9},{6,10},{7,11},{8,4},{9,5},... | collective-permute-start | bytes 387080 | tf_op jit(solution)/shard_map/ppermute | solution.py:25
  50.5 18.2 %collective-permute-start.7 = (bf16[384,896]{1,0:T(8,128)(2,1)S(1)}, bf16[384,896]{1,0:T(8,128)(2,1)}, u32[]{:S(2)}, u32[]{:S(2)}) collective-permute-start(bf16[384,896]{1,0:T(8,128)(2,1)S(1)} %constant_dynamic-update-slice_fusion.refs_0_), channel_id=1, source_target_pairs={{0,16},{16,0},{1,17},{17,1},{2,18},{18,2},{3,19},{19,3},{4,20},{20... | collective-permute-start | bytes 2064392 | tf_op jit(solution)/shard_map/ppermute | solution.py:25
  61.4 8.8 %collective-permute-start.8 = (bf16[384,896]{1,0:T(8,128)(2,1)}, bf16[384,896]{1,0:T(8,128)(2,1)}, u32[]{:S(2)}, u32[]{:S(2)}) collective-permute-start(bf16[384,896]{1,0:T(8,128)(2,1)} %collective-permute-done.3.refs_1_), channel_id=1, source_target_pairs={{0,16},{16,0},{1,17},{17,1},{2,18},{18,2},{3,19},{19,3},{4,20},{20... | collective-permute-start | bytes 2064392 | tf_op jit(solution)/shard_map/ppermute | solution.py:25
  61.4 8.8 %collective-permute-start.9 = (bf16[384,896]{1,0:T(8,128)(2,1)}, bf16[384,896]{1,0:T(8,128)(2,1)}, u32[]{:S(2)}, u32[]{:S(2)}) collective-permute-start(bf16[384,896]{1,0:T(8,128)(2,1)} %collective-permute-done.4.refs_2_), channel_id=1, source_target_pairs={{0,16},{16,0},{1,17},{17,1},{2,18},{18,2},{3,19},{19,3},{4,20},{20... | collective-permute-start | bytes 2064392 | tf_op jit(solution)/shard_map/ppermute | solution.py:25
  61.9 9.5 %collective-permute-start.10 = (bf16[384,896]{1,0:T(8,128)(2,1)S(1)}, bf16[384,896]{1,0:T(8,128)(2,1)}, u32[]{:S(2)}, u32[]{:S(2)}) collective-permute-start(bf16[384,896]{1,0:T(8,128)(2,1)S(1)} %collective-permute-done.6.refs_3_), channel_id=1, source_target_pairs={{0,16},{16,0},{1,17},{17,1},{2,18},{18,2},{3,19},{19,3},{4,20},{20... | collective-permute-start | bytes 2064392 | tf_op jit(solution)/shard_map/ppermute | solution.py:25
  67.1 14.6 %collective-permute-start.14 = (bf16[288,896]{1,0:T(8,128)(2,1)S(1)}, bf16[288,896]{1,0:T(8,128)(2,1)S(1)}, u32[]{:S(2)}, u32[]{:S(2)}) collective-permute-start(bf16[288,896]{1,0:T(8,128)(2,1)S(1)} %pad_maximum_fusion.refs_1_), channel_id=1, source_target_pairs={{0,1},{1,0},{2,3},{3,2},{4,5},{5,4},{6,7},{7,6},{8,9},{9,8},{10,11... | collective-permute-start | bytes 1548296 | tf_op jit(solution)/shard_map/ppermute | solution.py:45
  68.6 17.3 %collective-permute-start.15 = (bf16[288,896]{1,0:T(8,128)(2,1)S(1)}, bf16[288,896]{1,0:T(8,128)(2,1)}, u32[]{:S(2)}, u32[]{:S(2)}) collective-permute-start(bf16[288,896]{1,0:T(8,128)(2,1)S(1)} %pad_maximum_fusion.refs_1_), channel_id=1, source_target_pairs={{0,2},{1,3},{2,0},{3,1},{4,6},{5,7},{6,4},{7,5},{8,10},{9,11},{10,... | collective-permute-start | bytes 1548296 | tf_op jit(solution)/shard_map/ppermute | solution.py:45
  70.2 22.4 %collective-permute-start.17 = (bf16[288,896]{1,0:T(8,128)(2,1)S(1)}, bf16[288,896]{1,0:T(8,128)(2,1)}, u32[]{:S(2)}, u32[]{:S(2)}) collective-permute-start(bf16[288,896]{1,0:T(8,128)(2,1)S(1)} %pad_maximum_fusion.refs_1_), channel_id=1, source_target_pairs={{0,16},{16,0},{1,17},{17,1},{2,18},{18,2},{3,19},{19,3},{4,20},{20... | collective-permute-start | bytes 1548296 | tf_op jit(solution)/shard_map/ppermute | solution.py:25
  70.2 12.1 %collective-permute-start.22 = (bf16[72,640]{1,0:T(8,128)(2,1)S(1)}, bf16[72,640]{1,0:T(8,128)(2,1)S(1)}, u32[]{:S(2)}, u32[]{:S(2)}) collective-permute-start(bf16[72,640]{1,0:T(8,128)(2,1)S(1)} %get-tuple-element.43), channel_id=1, source_target_pairs={{0,8},{1,9},{2,10},{3,11},{4,12},{5,13},{6,14},{7,15},{8,0},{9,1},... | collective-permute-start | bytes 276488 | tf_op jit(solution)/shard_map/ppermute | solution.py:25
  71.5 10.9 %collective-permute-start.23 = (bf16[72,640]{1,0:T(8,128)(2,1)S(1)}, bf16[72,640]{1,0:T(8,128)(2,1)S(1)}, u32[]{:S(2)}, u32[]{:S(2)}) collective-permute-start(bf16[72,640]{1,0:T(8,128)(2,1)S(1)} %get-tuple-element.43), channel_id=1, source_target_pairs={{0,12},{1,13},{2,14},{3,15},{4,8},{5,9},{6,10},{7,11},{8,4},{9,5},... | collective-permute-start | bytes 276488 | tf_op jit(solution)/shard_map/ppermute | solution.py:25
  81.7 12.3 %collective-permute-start.16 = (bf16[288,896]{1,0:T(8,128)(2,1)S(1)}, bf16[288,896]{1,0:T(8,128)(2,1)}, u32[]{:S(2)}, u32[]{:S(2)}) collective-permute-start(bf16[288,896]{1,0:T(8,128)(2,1)S(1)} %collective-permute-done.14.refs_2_), channel_id=1, source_target_pairs={{0,2},{1,3},{2,0},{3,1},{4,6},{5,7},{6,4},{7,5},{8,10},{9,11},{10,... | collective-permute-start | bytes 1548296 | tf_op jit(solution)/shard_map/ppermute | solution.py:45
  82.4 9.6 %collective-permute-start.24 = (bf16[288,640]{1,0:T(8,128)(2,1)S(1)}, bf16[288,640]{1,0:T(8,128)(2,1)}, u32[]{:S(2)}, u32[]{:S(2)}) collective-permute-start(bf16[288,640]{1,0:T(8,128)(2,1)S(1)} %constant_dynamic-update-slice_fusion.4.refs_0_), channel_id=1, source_target_pairs={{0,1},{1,0},{2,3},{3,2},{4,5},{5,4},{6,7},{7,6},{8,9},{9,8},{10,11... | collective-permute-start | bytes 1105928 | tf_op jit(solution)/shard_map/ppermute | solution.py:45
  85.9 17.9 %collective-permute-start.18 = (bf16[288,896]{1,0:T(8,128)(2,1)S(1)}, bf16[288,896]{1,0:T(8,128)(2,1)}, u32[]{:S(2)}, u32[]{:S(2)}) collective-permute-start(bf16[288,896]{1,0:T(8,128)(2,1)S(1)} %collective-permute-done.14.refs_2_), channel_id=1, source_target_pairs={{0,16},{16,0},{1,17},{17,1},{2,18},{18,2},{3,19},{19,3},{4,20},{20... | collective-permute-start | bytes 1548296 | tf_op jit(solution)/shard_map/ppermute | solution.py:25
  86.0 18.4 %collective-permute-start.19 = (bf16[288,896]{1,0:T(8,128)(2,1)}, bf16[288,896]{1,0:T(8,128)(2,1)}, u32[]{:S(2)}, u32[]{:S(2)}) collective-permute-start(bf16[288,896]{1,0:T(8,128)(2,1)} %collective-permute-done.15.refs_3_), channel_id=1, source_target_pairs={{0,16},{16,0},{1,17},{17,1},{2,18},{18,2},{3,19},{19,3},{4,20},{20... | collective-permute-start | bytes 1548296 | tf_op jit(solution)/shard_map/ppermute | solution.py:25
  86.5 29.2 %all-to-all-start.1 = ((bf16[16,24,288]{2,1,0:T(8,128)(2,1)}), bf16[16,24,288]{2,1,0:T(8,128)(2,1)S(1)}, u32[]{:S(2)}, u32[]{:S(2)}) async-start(bf16[16,24,288]{2,1,0:T(8,128)(2,1)} %bitcast.5), calls=%async_computation.1 | async-start | bytes 589824 | tf_op jit(solution)/shard_map/all_to_all | solution.py:479
  92.0 12.4 %collective-permute-start.25 = (bf16[288,640]{1,0:T(8,128)(2,1)S(1)}, bf16[288,640]{1,0:T(8,128)(2,1)S(1)}, u32[]{:S(2)}, u32[]{:S(2)}) collective-permute-start(bf16[288,640]{1,0:T(8,128)(2,1)S(1)} %constant_dynamic-update-slice_fusion.4.refs_0_), channel_id=1, source_target_pairs={{0,2},{1,3},{2,0},{3,1},{4,6},{5,7},{6,4},{7,5},{8,10},{9,11},{10,... | collective-permute-start | bytes 1105928 | tf_op jit(solution)/shard_map/ppermute | solution.py:45
  92.6 12.5 %collective-permute-start.26 = (bf16[288,640]{1,0:T(8,128)(2,1)}, bf16[288,640]{1,0:T(8,128)(2,1)}, u32[]{:S(2)}, u32[]{:S(2)}) collective-permute-start(bf16[288,640]{1,0:T(8,128)(2,1)} %collective-permute-done.24.refs_1_), channel_id=1, source_target_pairs={{0,2},{1,3},{2,0},{3,1},{4,6},{5,7},{6,4},{7,5},{8,10},{9,11},{10,... | collective-permute-start | bytes 1105928 | tf_op jit(solution)/shard_map/ppermute | solution.py:45
  94.0 11.1 %collective-permute-start.20 = (bf16[288,896]{1,0:T(8,128)(2,1)}, bf16[288,896]{1,0:T(8,128)(2,1)S(1)}, u32[]{:S(2)}, u32[]{:S(2)}) collective-permute-start(bf16[288,896]{1,0:T(8,128)(2,1)} %collective-permute-done.16.refs_4_), channel_id=1, source_target_pairs={{0,16},{16,0},{1,17},{17,1},{2,18},{18,2},{3,19},{19,3},{4,20},{20... | collective-permute-start | bytes 1548296 | tf_op jit(solution)/shard_map/ppermute | solution.py:25
  103.8 11.9 %collective-permute-start.27 = (bf16[288,640]{1,0:T(8,128)(2,1)S(1)}, bf16[288,640]{1,0:T(8,128)(2,1)S(1)}, u32[]{:S(2)}, u32[]{:S(2)}) collective-permute-start(bf16[288,640]{1,0:T(8,128)(2,1)S(1)} %constant_dynamic-update-slice_fusion.4.refs_0_), channel_id=1, source_target_pairs={{0,16},{16,0},{1,17},{17,1},{2,18},{18,2},{3,19},{19,3},{4,20},{20... | collective-permute-start | bytes 1105928 | tf_op jit(solution)/shard_map/ppermute | solution.py:25
  104.3 11.3 %collective-permute-start.28 = (bf16[288,640]{1,0:T(8,128)(2,1)}, bf16[288,640]{1,0:T(8,128)(2,1)S(1)}, u32[]{:S(2)}, u32[]{:S(2)}) collective-permute-start(bf16[288,640]{1,0:T(8,128)(2,1)} %collective-permute-done.24.refs_1_), channel_id=1, source_target_pairs={{0,16},{16,0},{1,17},{17,1},{2,18},{18,2},{3,19},{19,3},{4,20},{20... | collective-permute-start | bytes 1105928 | tf_op jit(solution)/shard_map/ppermute | solution.py:25
  104.4 11.2 %collective-permute-start.29 = (bf16[288,640]{1,0:T(8,128)(2,1)S(1)}, bf16[288,640]{1,0:T(8,128)(2,1)S(1)}, u32[]{:S(2)}, u32[]{:S(2)}) collective-permute-start(bf16[288,640]{1,0:T(8,128)(2,1)S(1)} %collective-permute-done.25.refs_2_), channel_id=1, source_target_pairs={{0,16},{16,0},{1,17},{17,1},{2,18},{18,2},{3,19},{19,3},{4,20},{20... | collective-permute-start | bytes 1105928 | tf_op jit(solution)/shard_map/ppermute | solution.py:25
  105.1 10.6 %collective-permute-start.30 = (bf16[288,640]{1,0:T(8,128)(2,1)}, bf16[288,640]{1,0:T(8,128)(2,1)}, u32[]{:S(2)}, u32[]{:S(2)}) collective-permute-start(bf16[288,640]{1,0:T(8,128)(2,1)} %collective-permute-done.26.refs_3_), channel_id=1, source_target_pairs={{0,16},{16,0},{1,17},{17,1},{2,18},{18,2},{3,19},{19,3},{4,20},{20... | collective-permute-start | bytes 1105928 | tf_op jit(solution)/shard_map/ppermute | solution.py:25
  (19 other events, 93.9 us)

commit v3 on v2

--- a/solution.py
+++ b/solution.py
@@ -342,11 +342,10 @@
     base = 0
     for ref in (cross_ref, time_ref, box_ref):
         part = ref.shape[1] // 2
-        for half in range(2):
-            side = which if half == 0 else 1 - which
-            pick = chooser(part, source_ref[...], base + side * part)
-            term = dot(ref[:, half * part : (half + 1) * part], pick)
-            attn = term if attn is None else attn + term
+        row = lax.broadcasted_iota(jnp.int32, (2 * part, 1), 0)
+        channel = base + row + jnp.where(row < part, which, -which) * part
+        term = dot(ref[...], (channel == source_ref[...]).astype(F32).astype(BF16))
+        attn = term if attn is None else attn + term
         base += 2 * part
     attn = attn.astype(BF16)
     step = out_ref.shape[1] - width

time: 127 us -> 127 us (level)
  no operation moved by 1% of the time
where the time goes in v3:
time: 127 us; the launch traced here: 126 us
  starting transfers between devices  42.2 us (33%)
  Pallas kernels  39.8 us (31%)
  waiting for transfers between devices  28.9 us (23%)
  local copies, waits for them, and re-layouts  11.8 us (9%)
  between operations  3.05 us (2%)
    pallas_call x7, Pallas kernels, call(): pl.pallas_call(kernel, out_shape=outs if single else tuple(outs), in_spec...  39.8 us
    ppermute x22, waiting for transfers between devices, swap(): return lax.ppermute(value, axis, [(i, i ^ by) for i in range(size)])  25 us
    ppermute x22, starting transfers between devices, swap(): return lax.ppermute(value, axis, [(i, i ^ by) for i in range(size)])  21.6 us
    unnamed x42, local copies, waits for them, and re-layouts  10.8 us
    ppermute x9, starting transfers between devices, near_step(): return lax.ppermute(value, ('view', 'tm'), pairs)  10.7 us
    all_to_all x1, starting transfers between devices, per_device(): lax.all_to_all(tie(tokens, early_far).reshape(size, positions, depth), 't...  6.14 us
    ppermute x9, waiting for transfers between devices, near_step(): return lax.ppermute(value, ('view', 'tm'), pairs)  3.91 us
    all_to_all x1, starting transfers between devices, per_device(): lax.all_to_all(timed.reshape(size, positions, 2 * tw), 'tm', split_axis=0...  3.72 us
  transfers between devices with their start and end apart: 33, of which 7 were waited for; matrix products, arithmetic and copies ran while one was open for 1% of the time, Pallas kernels for 25%

profile of v3, /device:TPU:0, one launch (start us, length us, event | category | flops | bytes accessed | tf_op | source)
XLA Modules:
  0.0 125.8 jit_solution(4297670669051304088)
XLA Ops:
  1.3 1.0 copy-done
  4.8 3.1 %collective-permute-start = (bf16[96,896]{1,0:T(8,128)(2,1)S(1)}, bf16[96,896]{1,0:T(8,128)(2,1)S(1)}, u32[]{:S(2)}, u32[]{:S(2)}) collective-permute-start(bf16[96,896]{1,0:T(8,128)(2,1)S(1)} %get-tuple-element.31), channel_id=1, source_target_pairs={{0,4},{1,5},{2,6},{3,7},{4,0},{5,1},{6,2},{7,3},{8,12},{9,13},{10,... | collective-permute-start | bytes 516104 | tf_op jit(solution)/shard_map/ppermute | solution.py:25
  7.9 2.6 %collective-permute-start.1 = (bf16[96,896]{1,0:T(8,128)(2,1)S(1)}, bf16[96,896]{1,0:T(8,128)(2,1)S(1)}, u32[]{:S(2)}, u32[]{:S(2)}) collective-permute-start(bf16[96,896]{1,0:T(8,128)(2,1)S(1)} %get-tuple-element.31), channel_id=1, source_target_pairs={{0,8},{1,9},{2,10},{3,11},{4,12},{5,13},{6,14},{7,15},{8,0},{9,1},... | collective-permute-start | bytes 516104 | tf_op jit(solution)/shard_map/ppermute | solution.py:25
  10.5 4.5 %collective-permute-done = bf16[96,896]{1,0:T(8,128)(2,1)S(1)} collective-permute-done((bf16[96,896]{1,0:T(8,128)(2,1)S(1)}, bf16[96,896]{1,0:T(8,128)(2,1)S(1)}, u32[]{:S(2)}, u32[]{:S(2)}) %collective-permute-start) | collective-permute-done | bytes 172064 | tf_op jit(solution)/shard_map/ppermute | solution.py:25
  15.0 8.5 %collective-permute-done.1 = bf16[96,896]{1,0:T(8,128)(2,1)S(1)} collective-permute-done((bf16[96,896]{1,0:T(8,128)(2,1)S(1)}, bf16[96,896]{1,0:T(8,128)(2,1)S(1)}, u32[]{:S(2)}, u32[]{:S(2)}) %collective-permute-start.1) | collective-permute-done | bytes 172064 | tf_op jit(solution)/shard_map/ppermute | solution.py:25
  23.5 1.6 %collective-permute-start.3 = (bf16[384,896]{1,0:T(8,128)(2,1)S(1)}, bf16[384,896]{1,0:T(8,128)(2,1)}, u32[]{:S(2)}, u32[]{:S(2)}) collective-permute-start(bf16[384,896]{1,0:T(8,128)(2,1)S(1)} %constant_dynamic-update-slice_fusion.refs_0_), channel_id=1, source_target_pairs={{0,1},{1,0},{2,3},{3,2},{4,5},{5,4},{6,7},{7,6},{8,9},{9,8},{10,11... | collective-permute-start | bytes 2064392 | tf_op jit(solution)/shard_map/ppermute | solution.py:45
  25.1 6.1 %all-to-all-start = ((bf16[16,24,1152]{2,1,0:T(8,128)(2,1)}), bf16[16,24,1152]{2,1,0:T(8,128)(2,1)S(1)}, u32[]{:S(2)}, u32[]{:S(2)}) async-start(bf16[16,24,1152]{2,1,0:T(8,128)(2,1)} %bitcast.3), calls=%async_computation | async-start | bytes 1769472 | tf_op jit(solution)/shard_map/all_to_all | solution.py:446
  31.6 2.0 %collective-permute-start.4 = (bf16[384,896]{1,0:T(8,128)(2,1)S(1)}, bf16[384,896]{1,0:T(8,128)(2,1)}, u32[]{:S(2)}, u32[]{:S(2)}) collective-permute-start(bf16[384,896]{1,0:T(8,128)(2,1)S(1)} %constant_dynamic-update-slice_fusion.refs_0_), channel_id=1, source_target_pairs={{0,2},{1,3},{2,0},{3,1},{4,6},{5,7},{6,4},{7,5},{8,10},{9,11},{10,... | collective-permute-start | bytes 2064392 | tf_op jit(solution)/shard_map/ppermute | solution.py:45
  33.5 5.6 %order.1 = (bf16[384,1152]{1,0:T(8,128)(2,1)S(1)}, bf16[384,1536]{1,0:T(8,128)(2,1)S(1)}, bf16[384,1152]{1,0:T(8,128)(2,1)S(1)}) custom-call(bf16[384,1152]{1,0:T(8,128)(2,1)} %bitcast.1.tokens_ref, bf16[384,1152]{1,0:T(8,128)(2,1)S(1)} %collective-permute-done.5.refs_0_, s32[1,1152]{1,0:T(1,128)S(1)} %add.38.refs_1_.source_ref, ...), custom_call_target="tpu_custom_call" | custom-call | flops 6600000000 | bytes 21600000 | tf_op jit(solution)/shard_map/order/pallas_call | solution.py:366
  39.2 1.1 copy-done.5
  42.2 3.9 %collective-permute-start.11 = (bf16[72,896]{1,0:T(8,128)(2,1)S(1)}, bf16[72,896]{1,0:T(8,128)(2,1)S(1)}, u32[]{:S(2)}, u32[]{:S(2)}) collective-permute-start(bf16[72,896]{1,0:T(8,128)(2,1)S(1)} %get-tuple-element.38), channel_id=1, source_target_pairs={{0,4},{1,5},{2,6},{3,7},{4,0},{5,1},{6,2},{7,3},{8,12},{9,13},{10,... | collective-permute-start | bytes 387080 | tf_op jit(solution)/shard_map/ppermute | solution.py:25
  46.1 2.9 %collective-permute-start.12 = (bf16[72,896]{1,0:T(8,128)(2,1)S(1)}, bf16[72,896]{1,0:T(8,128)(2,1)S(1)}, u32[]{:S(2)}, u32[]{:S(2)}) collective-permute-start(bf16[72,896]{1,0:T(8,128)(2,1)S(1)} %get-tuple-element.38), channel_id=1, source_target_pairs={{0,8},{1,9},{2,10},{3,11},{4,12},{5,13},{6,14},{7,15},{8,0},{9,1},... | collective-permute-start | bytes 387080 | tf_op jit(solution)/shard_map/ppermute | solution.py:25
  49.0 1.5 %collective-permute-start.13 = (bf16[72,896]{1,0:T(8,128)(2,1)S(1)}, bf16[72,896]{1,0:T(8,128)(2,1)S(1)}, u32[]{:S(2)}, u32[]{:S(2)}) collective-permute-start(bf16[72,896]{1,0:T(8,128)(2,1)S(1)} %get-tuple-element.38), channel_id=1, source_target_pairs={{0,12},{1,13},{2,14},{3,15},{4,8},{5,9},{6,10},{7,11},{8,4},{9,5},... | collective-permute-start | bytes 387080 | tf_op jit(solution)/shard_map/ppermute | solution.py:25
  50.5 10.9 %collective-permute-done.12 = bf16[72,896]{1,0:T(8,128)(2,1)S(1)} collective-permute-done((bf16[72,896]{1,0:T(8,128)(2,1)S(1)}, bf16[72,896]{1,0:T(8,128)(2,1)S(1)}, u32[]{:S(2)}, u32[]{:S(2)}) %collective-permute-start.12) | collective-permute-done | bytes 129056 | tf_op jit(solution)/shard_map/ppermute | solution.py:25
  62.1 1.7 %collective-permute-start.21 = (bf16[72,640]{1,0:T(8,128)(2,1)S(1)}, bf16[72,640]{1,0:T(8,128)(2,1)S(1)}, u32[]{:S(2)}, u32[]{:S(2)}) collective-permute-start(bf16[72,640]{1,0:T(8,128)(2,1)S(1)} %get-tuple-element.43), channel_id=1, source_target_pairs={{0,4},{1,5},{2,6},{3,7},{4,0},{5,1},{6,2},{7,3},{8,12},{9,13},{10,... | collective-permute-start | bytes 276488 | tf_op jit(solution)/shard_map/ppermute | solution.py:25
  63.8 2.2 %widen.1.wide_ref = bf16[384,1536]{1,0:T(8,128)(2,1)S(1)} custom-call(bf16[384,1152]{1,0:T(8,128)(2,1)S(1)} %bitcast.8, s32[1,1536]{1,0:T(1,128)S(1)} %reshape.86.source_ref.refs_2_), custom_call_target="tpu_custom_call" | custom-call | flops 2200000000 | bytes 7200000 | tf_op jit(solution)/shard_map/widen/pallas_call | solution.py:366
  66.1 1.1 collective-permute-done.21
  67.1 1.5 %collective-permute-start.14 = (bf16[288,896]{1,0:T(8,128)(2,1)S(1)}, bf16[288,896]{1,0:T(8,128)(2,1)S(1)}, u32[]{:S(2)}, u32[]{:S(2)}) collective-permute-start(bf16[288,896]{1,0:T(8,128)(2,1)S(1)} %pad_maximum_fusion.refs_1_), channel_id=1, source_target_pairs={{0,1},{1,0},{2,3},{3,2},{4,5},{5,4},{6,7},{7,6},{8,9},{9,8},{10,11... | collective-permute-start | bytes 1548296 | tf_op jit(solution)/shard_map/ppermute | solution.py:45
  68.6 1.5 %collective-permute-start.15 = (bf16[288,896]{1,0:T(8,128)(2,1)S(1)}, bf16[288,896]{1,0:T(8,128)(2,1)}, u32[]{:S(2)}, u32[]{:S(2)}) collective-permute-start(bf16[288,896]{1,0:T(8,128)(2,1)S(1)} %pad_maximum_fusion.refs_1_), channel_id=1, source_target_pairs={{0,2},{1,3},{2,0},{3,1},{4,6},{5,7},{6,4},{7,5},{8,10},{9,11},{10,... | collective-permute-start | bytes 1548296 | tf_op jit(solution)/shard_map/ppermute | solution.py:45
  70.2 1.3 %collective-permute-start.22 = (bf16[72,640]{1,0:T(8,128)(2,1)S(1)}, bf16[72,640]{1,0:T(8,128)(2,1)S(1)}, u32[]{:S(2)}, u32[]{:S(2)}) collective-permute-start(bf16[72,640]{1,0:T(8,128)(2,1)S(1)} %get-tuple-element.43), channel_id=1, source_target_pairs={{0,8},{1,9},{2,10},{3,11},{4,12},{5,13},{6,14},{7,15},{8,0},{9,1},... | collective-permute-start | bytes 276488 | tf_op jit(solution)/shard_map/ppermute | solution.py:25
  71.5 2.4 %collective-permute-start.23 = (bf16[72,640]{1,0:T(8,128)(2,1)S(1)}, bf16[72,640]{1,0:T(8,128)(2,1)S(1)}, u32[]{:S(2)}, u32[]{:S(2)}) collective-permute-start(bf16[72,640]{1,0:T(8,128)(2,1)S(1)} %get-tuple-element.43), channel_id=1, source_target_pairs={{0,12},{1,13},{2,14},{3,15},{4,8},{5,9},{6,10},{7,11},{8,4},{9,5},... | collective-permute-start | bytes 276488 | tf_op jit(solution)/shard_map/ppermute | solution.py:25
  73.8 6.0 %timed.1 = bf16[384,288]{1,0:T(8,128)(2,1)} custom-call(s32[1]{0:T(128)} %bitcast.half_ref, bf16[384,1536]{1,0:T(8,128)(2,1)S(1)} %widen.1.wide_ref, bf16[384,896]{1,0:T(8,128)(2,1)S(1)} %constant_dynamic-update-slice_fusion.refs_0_, bf16[384,896]{1,0:T(8,128)(2,1)} %collective-permute-done.3.refs_1_, bf16[384,896]{1,0:T(8,128)(2,1)} %collective-permute-done.4.refs_2_, ...), custom_call_target="tpu_custom_call" | custom-call | flops 5500000256 | bytes 18000000 | tf_op jit(solution)/shard_map/timed/pallas_call | solution.py:366
  79.9 1.9 %collective-permute-done.14.refs_2_ = bf16[288,896]{1,0:T(8,128)(2,1)S(1)} collective-permute-done((bf16[288,896]{1,0:T(8,128)(2,1)S(1)}, bf16[288,896]{1,0:T(8,128)(2,1)S(1)}, u32[]{:S(2)}, u32[]{:S(2)}) %collective-permute-start.14) | collective-permute-done | bytes 516128 | tf_op jit(solution)/shard_map/ppermute | solution.py:45
  82.4 1.5 %collective-permute-start.24 = (bf16[288,640]{1,0:T(8,128)(2,1)S(1)}, bf16[288,640]{1,0:T(8,128)(2,1)}, u32[]{:S(2)}, u32[]{:S(2)}) collective-permute-start(bf16[288,640]{1,0:T(8,128)(2,1)S(1)} %constant_dynamic-update-slice_fusion.4.refs_0_), channel_id=1, source_target_pairs={{0,1},{1,0},{2,3},{3,2},{4,5},{5,4},{6,7},{7,6},{8,9},{9,8},{10,11... | collective-permute-start | bytes 1105928 | tf_op jit(solution)/shard_map/ppermute | solution.py:45
  86.5 3.7 %all-to-all-start.1 = ((bf16[16,24,288]{2,1,0:T(8,128)(2,1)}), bf16[16,24,288]{2,1,0:T(8,128)(2,1)S(1)}, u32[]{:S(2)}, u32[]{:S(2)}) async-start(bf16[16,24,288]{2,1,0:T(8,128)(2,1)} %bitcast.5), calls=%async_computation.1 | async-start | bytes 589824 | tf_op jit(solution)/shard_map/all_to_all | solution.py:478
  90.2 1.8 %collective-permute-done.24.refs_1_ = bf16[288,640]{1,0:T(8,128)(2,1)} collective-permute-done((bf16[288,640]{1,0:T(8,128)(2,1)S(1)}, bf16[288,640]{1,0:T(8,128)(2,1)}, u32[]{:S(2)}, u32[]{:S(2)}) %collective-permute-start.24) | collective-permute-done | bytes 368672 | tf_op jit(solution)/shard_map/ppermute | solution.py:45
  92.6 1.5 %collective-permute-start.26 = (bf16[288,640]{1,0:T(8,128)(2,1)}, bf16[288,640]{1,0:T(8,128)(2,1)}, u32[]{:S(2)}, u32[]{:S(2)}) collective-permute-start(bf16[288,640]{1,0:T(8,128)(2,1)} %collective-permute-done.24.refs_1_), channel_id=1, source_target_pairs={{0,2},{1,3},{2,0},{3,1},{4,6},{5,7},{6,4},{7,5},{8,10},{9,11},{10,... | collective-permute-start | bytes 1105928 | tf_op jit(solution)/shard_map/ppermute | solution.py:45
  94.0 1.3 %copy-done.6 = bf16[384,1536]{1,0:T(8,128)(2,1)S(1)} copy-done((bf16[384,1536]{1,0:T(8,128)(2,1)S(1)}, bf16[384,1536]{1,0:T(8,128)(2,1)}, u32[]{:S(2)}) %copy-start.6) | copy-done | bytes 1179672
  95.3 8.4 %boxed.1.box_ref = bf16[384,288]{1,0:T(8,128)(2,1)S(1)} custom-call(s32[1]{0:T(128)} %bitcast.half_ref, bf16[384,1536]{1,0:T(8,128)(2,1)S(1)} %copy-done.6, s32[1,1536]{1,0:T(1,128)S(1)} %reshape.86.source_ref.refs_2_, f32[2,144]{1,0:T(2,128)S(1)} %broadcast_select_fusion.gate_ref, bf16[384,896]{1,0:T(8,128)(2,1)S(1)} %constant_dynamic-update-slice_fusion.refs_0_, ...), custom_call_target="tpu_custom_call" | custom-call | flops 7699999744 | bytes 25200000 | tf_op jit(solution)/shard_map/boxed/pallas_call | solution.py:366
  105.1 9.7 %cross.1.cross_ref = bf16[384,576]{1,0:T(8,128)(2,1)S(1)} custom-call(s32[1]{0:T(128)} %bitcast.half_ref, f32[1,1]{1,0:T(1,128)S(6)} %convert_element_type.3.count_ref, bf16[384,1152]{1,0:T(8,128)(2,1)S(1)} %copy-done.10, bf16[384,1152]{1,0:T(8,128)(2,1)S(1)} %copy-done.12, bf16[288,896]{1,0:T(8,128)(2,1)S(1)} %pad_maximum_fusion.refs_1_, ...), custom_call_target="tpu_custom_call" | custom-call | flops 9900000256 | bytes 32400000 | tf_op jit(solution)/shard_map/cross/pallas_call | solution.py:366
  116.6 1.0 copy-done.8
  118.6 7.0 %final.1 = bf16[384,1152]{1,0:T(8,128)(2,1)} custom-call(s32[1]{0:T(128)} %bitcast.half_ref, bf16[384,1152]{1,0:T(8,128)(2,1)} %bitcast.1.tokens_ref, s32[1,1152]{1,0:T(1,128)S(1)} %add.38.refs_1_.source_ref, bf16[384,576]{1,0:T(8,128)(2,1)S(1)} %copy-done.8, bf16[384,288]{1,0:T(8,128)(2,1)S(1)} %bitcast.9, bf16[384,288]{1,0:T(8,128)(2,1)S(1)} %copy-done.14, ...), custom_call_target="tpu_custom_call" | custom-call | flops 5500000256 | bytes 18000000 | tf_op jit(solution)/shard_map/final/pallas_call | solution.py:366
  (95 shorter events, 12.0 us)
Async XLA Ops:
  4.8 10.2 %collective-permute-start = (bf16[96,896]{1,0:T(8,128)(2,1)S(1)}, bf16[96,896]{1,0:T(8,128)(2,1)S(1)}, u32[]{:S(2)}, u32[]{:S(2)}) collective-permute-start(bf16[96,896]{1,0:T(8,128)(2,1)S(1)} %get-tuple-element.31), channel_id=1, source_target_pairs={{0,4},{1,5},{2,6},{3,7},{4,0},{5,1},{6,2},{7,3},{8,12},{9,13},{10,... | collective-permute-start | bytes 516104 | tf_op jit(solution)/shard_map/ppermute | solution.py:25
  7.9 15.6 %collective-permute-start.1 = (bf16[96,896]{1,0:T(8,128)(2,1)S(1)}, bf16[96,896]{1,0:T(8,128)(2,1)S(1)}, u32[]{:S(2)}, u32[]{:S(2)}) collective-permute-start(bf16[96,896]{1,0:T(8,128)(2,1)S(1)} %get-tuple-element.31), channel_id=1, source_target_pairs={{0,8},{1,9},{2,10},{3,11},{4,12},{5,13},{6,14},{7,15},{8,0},{9,1},... | collective-permute-start | bytes 516104 | tf_op jit(solution)/shard_map/ppermute | solution.py:25
  10.5 13.0 %collective-permute-start.2 = (bf16[96,896]{1,0:T(8,128)(2,1)S(1)}, bf16[96,896]{1,0:T(8,128)(2,1)S(1)}, u32[]{:S(2)}, u32[]{:S(2)}) collective-permute-start(bf16[96,896]{1,0:T(8,128)(2,1)S(1)} %get-tuple-element.31), channel_id=1, source_target_pairs={{0,12},{1,13},{2,14},{3,15},{4,8},{5,9},{6,10},{7,11},{8,4},{9,5},... | collective-permute-start | bytes 516104 | tf_op jit(solution)/shard_map/ppermute | solution.py:25
  10.5 23.0 %collective-permute-start.5 = (bf16[384,1152]{1,0:T(8,128)(2,1)}, bf16[384,1152]{1,0:T(8,128)(2,1)S(1)}, u32[]{:S(2)}, u32[]{:S(2)}) collective-permute-start(bf16[384,1152]{1,0:T(8,128)(2,1)} %bitcast.1.tokens_ref), channel_id=1, source_target_pairs={{0,16},{16,0},{1,17},{17,1},{2,18},{18,2},{3,19},{19,3},{4,20},{20... | collective-permute-start | bytes 2654216 | tf_op jit(solution)/shard_map/ppermute | solution.py:25
  23.5 18.6 %collective-permute-start.3 = (bf16[384,896]{1,0:T(8,128)(2,1)S(1)}, bf16[384,896]{1,0:T(8,128)(2,1)}, u32[]{:S(2)}, u32[]{:S(2)}) collective-permute-start(bf16[384,896]{1,0:T(8,128)(2,1)S(1)} %constant_dynamic-update-slice_fusion.refs_0_), channel_id=1, source_target_pairs={{0,1},{1,0},{2,3},{3,2},{4,5},{5,4},{6,7},{7,6},{8,9},{9,8},{10,11... | collective-permute-start | bytes 2064392 | tf_op jit(solution)/shard_map/ppermute | solution.py:45
  25.1 37.0 %all-to-all-start = ((bf16[16,24,1152]{2,1,0:T(8,128)(2,1)}), bf16[16,24,1152]{2,1,0:T(8,128)(2,1)S(1)}, u32[]{:S(2)}, u32[]{:S(2)}) async-start(bf16[16,24,1152]{2,1,0:T(8,128)(2,1)} %bitcast.3), calls=%async_computation | async-start | bytes 1769472 | tf_op jit(solution)/shard_map/all_to_all | solution.py:446
  31.6 29.9 %collective-permute-start.4 = (bf16[384,896]{1,0:T(8,128)(2,1)S(1)}, bf16[384,896]{1,0:T(8,128)(2,1)}, u32[]{:S(2)}, u32[]{:S(2)}) collective-permute-start(bf16[384,896]{1,0:T(8,128)(2,1)S(1)} %constant_dynamic-update-slice_fusion.refs_0_), channel_id=1, source_target_pairs={{0,2},{1,3},{2,0},{3,1},{4,6},{5,7},{6,4},{7,5},{8,10},{9,11},{10,... | collective-permute-start | bytes 2064392 | tf_op jit(solution)/shard_map/ppermute | solution.py:45
  42.1 19.9 %collective-permute-start.6 = (bf16[384,896]{1,0:T(8,128)(2,1)}, bf16[384,896]{1,0:T(8,128)(2,1)S(1)}, u32[]{:S(2)}, u32[]{:S(2)}) collective-permute-start(bf16[384,896]{1,0:T(8,128)(2,1)} %collective-permute-done.3.refs_1_), channel_id=1, source_target_pairs={{0,2},{1,3},{2,0},{3,1},{4,6},{5,7},{6,4},{7,5},{8,10},{9,11},{10,... | collective-permute-start | bytes 2064392 | tf_op jit(solution)/shard_map/ppermute | solution.py:45
  42.2 8.3 %collective-permute-start.11 = (bf16[72,896]{1,0:T(8,128)(2,1)S(1)}, bf16[72,896]{1,0:T(8,128)(2,1)S(1)}, u32[]{:S(2)}, u32[]{:S(2)}) collective-permute-start(bf16[72,896]{1,0:T(8,128)(2,1)S(1)} %get-tuple-element.38), channel_id=1, source_target_pairs={{0,4},{1,5},{2,6},{3,7},{4,0},{5,1},{6,2},{7,3},{8,12},{9,13},{10,... | collective-permute-start | bytes 387080 | tf_op jit(solution)/shard_map/ppermute | solution.py:25
  46.1 15.3 %collective-permute-start.12 = (bf16[72,896]{1,0:T(8,128)(2,1)S(1)}, bf16[72,896]{1,0:T(8,128)(2,1)S(1)}, u32[]{:S(2)}, u32[]{:S(2)}) collective-permute-start(bf16[72,896]{1,0:T(8,128)(2,1)S(1)} %get-tuple-element.38), channel_id=1, source_target_pairs={{0,8},{1,9},{2,10},{3,11},{4,12},{5,13},{6,14},{7,15},{8,0},{9,1},... | collective-permute-start | bytes 387080 | tf_op jit(solution)/shard_map/ppermute | solution.py:25
  49.0 13.0 %collective-permute-start.13 = (bf16[72,896]{1,0:T(8,128)(2,1)S(1)}, bf16[72,896]{1,0:T(8,128)(2,1)S(1)}, u32[]{:S(2)}, u32[]{:S(2)}) collective-permute-start(bf16[72,896]{1,0:T(8,128)(2,1)S(1)} %get-tuple-element.38), channel_id=1, source_target_pairs={{0,12},{1,13},{2,14},{3,15},{4,8},{5,9},{6,10},{7,11},{8,4},{9,5},... | collective-permute-start | bytes 387080 | tf_op jit(solution)/shard_map/ppermute | solution.py:25
  50.5 18.2 %collective-permute-start.7 = (bf16[384,896]{1,0:T(8,128)(2,1)S(1)}, bf16[384,896]{1,0:T(8,128)(2,1)}, u32[]{:S(2)}, u32[]{:S(2)}) collective-permute-start(bf16[384,896]{1,0:T(8,128)(2,1)S(1)} %constant_dynamic-update-slice_fusion.refs_0_), channel_id=1, source_target_pairs={{0,16},{16,0},{1,17},{17,1},{2,18},{18,2},{3,19},{19,3},{4,20},{20... | collective-permute-start | bytes 2064392 | tf_op jit(solution)/shard_map/ppermute | solution.py:25
  61.4 8.8 %collective-permute-start.8 = (bf16[384,896]{1,0:T(8,128)(2,1)}, bf16[384,896]{1,0:T(8,128)(2,1)}, u32[]{:S(2)}, u32[]{:S(2)}) collective-permute-start(bf16[384,896]{1,0:T(8,128)(2,1)} %collective-permute-done.3.refs_1_), channel_id=1, source_target_pairs={{0,16},{16,0},{1,17},{17,1},{2,18},{18,2},{3,19},{19,3},{4,20},{20... | collective-permute-start | bytes 2064392 | tf_op jit(solution)/shard_map/ppermute | solution.py:25
  61.4 8.8 %collective-permute-start.9 = (bf16[384,896]{1,0:T(8,128)(2,1)}, bf16[384,896]{1,0:T(8,128)(2,1)}, u32[]{:S(2)}, u32[]{:S(2)}) collective-permute-start(bf16[384,896]{1,0:T(8,128)(2,1)} %collective-permute-done.4.refs_2_), channel_id=1, source_target_pairs={{0,16},{16,0},{1,17},{17,1},{2,18},{18,2},{3,19},{19,3},{4,20},{20... | collective-permute-start | bytes 2064392 | tf_op jit(solution)/shard_map/ppermute | solution.py:25
  61.9 9.5 %collective-permute-start.10 = (bf16[384,896]{1,0:T(8,128)(2,1)S(1)}, bf16[384,896]{1,0:T(8,128)(2,1)}, u32[]{:S(2)}, u32[]{:S(2)}) collective-permute-start(bf16[384,896]{1,0:T(8,128)(2,1)S(1)} %collective-permute-done.6.refs_3_), channel_id=1, source_target_pairs={{0,16},{16,0},{1,17},{17,1},{2,18},{18,2},{3,19},{19,3},{4,20},{20... | collective-permute-start | bytes 2064392 | tf_op jit(solution)/shard_map/ppermute | solution.py:25
  67.1 14.6 %collective-permute-start.14 = (bf16[288,896]{1,0:T(8,128)(2,1)S(1)}, bf16[288,896]{1,0:T(8,128)(2,1)S(1)}, u32[]{:S(2)}, u32[]{:S(2)}) collective-permute-start(bf16[288,896]{1,0:T(8,128)(2,1)S(1)} %pad_maximum_fusion.refs_1_), channel_id=1, source_target_pairs={{0,1},{1,0},{2,3},{3,2},{4,5},{5,4},{6,7},{7,6},{8,9},{9,8},{10,11... | collective-permute-start | bytes 1548296 | tf_op jit(solution)/shard_map/ppermute | solution.py:45
  68.6 17.3 %collective-permute-start.15 = (bf16[288,896]{1,0:T(8,128)(2,1)S(1)}, bf16[288,896]{1,0:T(8,128)(2,1)}, u32[]{:S(2)}, u32[]{:S(2)}) collective-permute-start(bf16[288,896]{1,0:T(8,128)(2,1)S(1)} %pad_maximum_fusion.refs_1_), channel_id=1, source_target_pairs={{0,2},{1,3},{2,0},{3,1},{4,6},{5,7},{6,4},{7,5},{8,10},{9,11},{10,... | collective-permute-start | bytes 1548296 | tf_op jit(solution)/shard_map/ppermute | solution.py:45
  70.2 22.4 %collective-permute-start.17 = (bf16[288,896]{1,0:T(8,128)(2,1)S(1)}, bf16[288,896]{1,0:T(8,128)(2,1)}, u32[]{:S(2)}, u32[]{:S(2)}) collective-permute-start(bf16[288,896]{1,0:T(8,128)(2,1)S(1)} %pad_maximum_fusion.refs_1_), channel_id=1, source_target_pairs={{0,16},{16,0},{1,17},{17,1},{2,18},{18,2},{3,19},{19,3},{4,20},{20... | collective-permute-start | bytes 1548296 | tf_op jit(solution)/shard_map/ppermute | solution.py:25
  70.2 12.1 %collective-permute-start.22 = (bf16[72,640]{1,0:T(8,128)(2,1)S(1)}, bf16[72,640]{1,0:T(8,128)(2,1)S(1)}, u32[]{:S(2)}, u32[]{:S(2)}) collective-permute-start(bf16[72,640]{1,0:T(8,128)(2,1)S(1)} %get-tuple-element.43), channel_id=1, source_target_pairs={{0,8},{1,9},{2,10},{3,11},{4,12},{5,13},{6,14},{7,15},{8,0},{9,1},... | collective-permute-start | bytes 276488 | tf_op jit(solution)/shard_map/ppermute | solution.py:25
  71.5 10.9 %collective-permute-start.23 = (bf16[72,640]{1,0:T(8,128)(2,1)S(1)}, bf16[72,640]{1,0:T(8,128)(2,1)S(1)}, u32[]{:S(2)}, u32[]{:S(2)}) collective-permute-start(bf16[72,640]{1,0:T(8,128)(2,1)S(1)} %get-tuple-element.43), channel_id=1, source_target_pairs={{0,12},{1,13},{2,14},{3,15},{4,8},{5,9},{6,10},{7,11},{8,4},{9,5},... | collective-permute-start | bytes 276488 | tf_op jit(solution)/shard_map/ppermute | solution.py:25
  81.7 12.3 %collective-permute-start.16 = (bf16[288,896]{1,0:T(8,128)(2,1)S(1)}, bf16[288,896]{1,0:T(8,128)(2,1)}, u32[]{:S(2)}, u32[]{:S(2)}) collective-permute-start(bf16[288,896]{1,0:T(8,128)(2,1)S(1)} %collective-permute-done.14.refs_2_), channel_id=1, source_target_pairs={{0,2},{1,3},{2,0},{3,1},{4,6},{5,7},{6,4},{7,5},{8,10},{9,11},{10,... | collective-permute-start | bytes 1548296 | tf_op jit(solution)/shard_map/ppermute | solution.py:45
  82.4 9.6 %collective-permute-start.24 = (bf16[288,640]{1,0:T(8,128)(2,1)S(1)}, bf16[288,640]{1,0:T(8,128)(2,1)}, u32[]{:S(2)}, u32[]{:S(2)}) collective-permute-start(bf16[288,640]{1,0:T(8,128)(2,1)S(1)} %constant_dynamic-update-slice_fusion.4.refs_0_), channel_id=1, source_target_pairs={{0,1},{1,0},{2,3},{3,2},{4,5},{5,4},{6,7},{7,6},{8,9},{9,8},{10,11... | collective-permute-start | bytes 1105928 | tf_op jit(solution)/shard_map/ppermute | solution.py:45
  85.9 17.9 %collective-permute-start.18 = (bf16[288,896]{1,0:T(8,128)(2,1)S(1)}, bf16[288,896]{1,0:T(8,128)(2,1)}, u32[]{:S(2)}, u32[]{:S(2)}) collective-permute-start(bf16[288,896]{1,0:T(8,128)(2,1)S(1)} %collective-permute-done.14.refs_2_), channel_id=1, source_target_pairs={{0,16},{16,0},{1,17},{17,1},{2,18},{18,2},{3,19},{19,3},{4,20},{20... | collective-permute-start | bytes 1548296 | tf_op jit(solution)/shard_map/ppermute | solution.py:25
  86.0 18.4 %collective-permute-start.19 = (bf16[288,896]{1,0:T(8,128)(2,1)}, bf16[288,896]{1,0:T(8,128)(2,1)}, u32[]{:S(2)}, u32[]{:S(2)}) collective-permute-start(bf16[288,896]{1,0:T(8,128)(2,1)} %collective-permute-done.15.refs_3_), channel_id=1, source_target_pairs={{0,16},{16,0},{1,17},{17,1},{2,18},{18,2},{3,19},{19,3},{4,20},{20... | collective-permute-start | bytes 1548296 | tf_op jit(solution)/shard_map/ppermute | solution.py:25
  86.5 29.2 %all-to-all-start.1 = ((bf16[16,24,288]{2,1,0:T(8,128)(2,1)}), bf16[16,24,288]{2,1,0:T(8,128)(2,1)S(1)}, u32[]{:S(2)}, u32[]{:S(2)}) async-start(bf16[16,24,288]{2,1,0:T(8,128)(2,1)} %bitcast.5), calls=%async_computation.1 | async-start | bytes 589824 | tf_op jit(solution)/shard_map/all_to_all | solution.py:478
  92.0 12.4 %collective-permute-start.25 = (bf16[288,640]{1,0:T(8,128)(2,1)S(1)}, bf16[288,640]{1,0:T(8,128)(2,1)S(1)}, u32[]{:S(2)}, u32[]{:S(2)}) collective-permute-start(bf16[288,640]{1,0:T(8,128)(2,1)S(1)} %constant_dynamic-update-slice_fusion.4.refs_0_), channel_id=1, source_target_pairs={{0,2},{1,3},{2,0},{3,1},{4,6},{5,7},{6,4},{7,5},{8,10},{9,11},{10,... | collective-permute-start | bytes 1105928 | tf_op jit(solution)/shard_map/ppermute | solution.py:45
  92.6 12.5 %collective-permute-start.26 = (bf16[288,640]{1,0:T(8,128)(2,1)}, bf16[288,640]{1,0:T(8,128)(2,1)}, u32[]{:S(2)}, u32[]{:S(2)}) collective-permute-start(bf16[288,640]{1,0:T(8,128)(2,1)} %collective-permute-done.24.refs_1_), channel_id=1, source_target_pairs={{0,2},{1,3},{2,0},{3,1},{4,6},{5,7},{6,4},{7,5},{8,10},{9,11},{10,... | collective-permute-start | bytes 1105928 | tf_op jit(solution)/shard_map/ppermute | solution.py:45
  94.0 11.1 %collective-permute-start.20 = (bf16[288,896]{1,0:T(8,128)(2,1)}, bf16[288,896]{1,0:T(8,128)(2,1)S(1)}, u32[]{:S(2)}, u32[]{:S(2)}) collective-permute-start(bf16[288,896]{1,0:T(8,128)(2,1)} %collective-permute-done.16.refs_4_), channel_id=1, source_target_pairs={{0,16},{16,0},{1,17},{17,1},{2,18},{18,2},{3,19},{19,3},{4,20},{20... | collective-permute-start | bytes 1548296 | tf_op jit(solution)/shard_map/ppermute | solution.py:25
  103.8 11.9 %collective-permute-start.27 = (bf16[288,640]{1,0:T(8,128)(2,1)S(1)}, bf16[288,640]{1,0:T(8,128)(2,1)S(1)}, u32[]{:S(2)}, u32[]{:S(2)}) collective-permute-start(bf16[288,640]{1,0:T(8,128)(2,1)S(1)} %constant_dynamic-update-slice_fusion.4.refs_0_), channel_id=1, source_target_pairs={{0,16},{16,0},{1,17},{17,1},{2,18},{18,2},{3,19},{19,3},{4,20},{20... | collective-permute-start | bytes 1105928 | tf_op jit(solution)/shard_map/ppermute | solution.py:25
  104.3 11.3 %collective-permute-start.28 = (bf16[288,640]{1,0:T(8,128)(2,1)}, bf16[288,640]{1,0:T(8,128)(2,1)S(1)}, u32[]{:S(2)}, u32[]{:S(2)}) collective-permute-start(bf16[288,640]{1,0:T(8,128)(2,1)} %collective-permute-done.24.refs_1_), channel_id=1, source_target_pairs={{0,16},{16,0},{1,17},{17,1},{2,18},{18,2},{3,19},{19,3},{4,20},{20... | collective-permute-start | bytes 1105928 | tf_op jit(solution)/shard_map/ppermute | solution.py:25
  104.4 11.2 %collective-permute-start.29 = (bf16[288,640]{1,0:T(8,128)(2,1)S(1)}, bf16[288,640]{1,0:T(8,128)(2,1)S(1)}, u32[]{:S(2)}, u32[]{:S(2)}) collective-permute-start(bf16[288,640]{1,0:T(8,128)(2,1)S(1)} %collective-permute-done.25.refs_2_), channel_id=1, source_target_pairs={{0,16},{16,0},{1,17},{17,1},{2,18},{18,2},{3,19},{19,3},{4,20},{20... | collective-permute-start | bytes 1105928 | tf_op jit(solution)/shard_map/ppermute | solution.py:25
  105.1 10.6 %collective-permute-start.30 = (bf16[288,640]{1,0:T(8,128)(2,1)}, bf16[288,640]{1,0:T(8,128)(2,1)}, u32[]{:S(2)}, u32[]{:S(2)}) collective-permute-start(bf16[288,640]{1,0:T(8,128)(2,1)} %collective-permute-done.26.refs_3_), channel_id=1, source_target_pairs={{0,16},{16,0},{1,17},{17,1},{2,18},{18,2},{3,19},{19,3},{4,20},{20... | collective-permute-start | bytes 1105928 | tf_op jit(solution)/shard_map/ppermute | solution.py:25
  (19 other events, 93.9 us)
